TPU v7x, 32 devices: a whole 2x2x4 slice. The times are simulated.
32 devices in a mesh: seq: 16 (over z, y, x), kv: 2 (over core).
Axes of the slice: x: 2, y: 2, z: 4, core: 2. Of those that a mesh axis runs over, the one named last changes fastest.
Arguments:
- text_query: bfloat16 [2048, 2048], P('seq', 'kv'), may hold values from -20 to 20, as said below
- vision_key: bfloat16 [512, 256], P('seq', 'kv'), may hold values from -4 to 4, as said below
- vision_value: bfloat16 [512, 256], P('seq', 'kv'), may hold values from -6 to 6
- grad_output: bfloat16 [2048, 2048], P('seq', 'kv'), may hold values from -192 to 192
- key_weight: bfloat16 [8192, 256], P('seq', 'kv'), may hold values from -0.09375 to 0.09375
- value_weight: bfloat16 [8192, 256], P('seq', 'kv'), may hold values from -0.09375 to 0.09375
Outputs:
- grad_query: bfloat16 [2048, 2048], P('seq', 'kv')
- grad_vision: bfloat16 [512, 8192], P('seq', 'kv')
Inputs may be any that keep to these rules, and one draw needn't show every extreme that they name: `text_query`: entries of order one; some rows of single heads may be large multiples of a key row. `vision_key`: entries of order one.
All inputs are finite; a program needn't handle non-finite values.
Results may differ from a plain program's by a relative error of at most 0.02.
Values may be sent and summed in bfloat16 or wider, within the bound.
No kernel may reach another device: no remote copies, remote signals or barrier semaphores. Data moves between devices by JAX's collectives and lax.ppermute only.
A program may use at most 64 MiB of HBM per device.

v0:
```python
import math

import jax
import jax.numpy as jnp
from jax import lax
from jax.sharding import PartitionSpec as P

HEAD = 128


def sweep(block_step, running, shard_piece):
    key_part, value_part = shard_piece
    key_count = key_part.shape[0]
    block_rows = 512
    num_blocks = key_count // block_rows
    key_blocks = key_part.reshape(num_blocks, block_rows, key_part.shape[1])
    value_blocks = value_part.reshape(num_blocks, block_rows, value_part.shape[1])

    def inner(inner_state, inputs):
        key_block, value_block, block_index = inputs
        return (block_step(inner_state, key_block, value_block, block_index * block_rows), None)

    result, unused = lax.scan(
        inner, running, (key_blocks, value_blocks, jnp.arange(num_blocks, dtype=jnp.int32))
    )
    return result


def shards(text_query, vision_key, vision_value, grad_output, key_weight, value_weight):
    scaling = 1.0 / math.sqrt(HEAD)
    row_count = text_query.shape[0]
    head_count = text_query.shape[1] // HEAD
    queries = text_query.reshape(row_count, head_count, HEAD)
    upstream = grad_output.reshape(row_count, head_count, HEAD)
    shard_keys = vision_key.shape[0]
    total_keys = shard_keys * lax.axis_size("seq")

    def logit_pair(key_block, value_block):
        logits = (
            jnp.einsum("thd,kd->htk", queries, key_block, preferred_element_type=jnp.float32)
            * scaling
        )
        grad_probs = jnp.einsum(
            "thd,kd->htk", upstream, value_block, preferred_element_type=jnp.float32
        )
        return (logits, grad_probs)

    def stats_block(running, key_block, value_block, offset):
        row_max, row_sums, weighted = running
        logits, grad_probs = logit_pair(key_block, value_block)
        new_max = jnp.maximum(row_max, jnp.max(logits, axis=2))
        exponent = jnp.exp(logits - new_max[:, :, None])
        factor = jnp.exp(row_max - new_max)
        return (
            new_max,
            row_sums * factor + jnp.sum(exponent, axis=2),
            weighted * factor + jnp.sum(exponent * grad_probs, axis=2),
        )

    init_stats = (
        jnp.full((head_count, row_count), -jnp.inf, jnp.float32),
        jnp.zeros((head_count, row_count), jnp.float32),
        jnp.zeros((head_count, row_count), jnp.float32),
    )

    def make_grads(stats):
        row_max, row_sums, weighted = stats
        row_dots = weighted / row_sums

        def attend(key_block, value_block):
            logits, grad_probs = logit_pair(key_block, value_block)
            attention = jnp.exp(logits - row_max[:, :, None]) / row_sums[:, :, None]
            grad_logits = (attention * (grad_probs - row_dots[:, :, None]) * scaling).astype(
                jnp.bfloat16
            )
            return (attention, grad_logits)

        def block_terms(attention, grad_logits):
            value_term = jnp.einsum(
                "htk,thd->kd",
                attention.astype(jnp.bfloat16),
                upstream,
                preferred_element_type=jnp.float32,
            )
            key_term = jnp.einsum(
                "htk,thd->kd", grad_logits, queries, preferred_element_type=jnp.float32
            )
            return jnp.concatenate([key_term, value_term], axis=1)

        def grad_block(running, key_block, value_block, offset):
            query_grad, key_grads = running
            attention, grad_logits = attend(key_block, value_block)
            query_grad = query_grad + jnp.einsum(
                "htk,kd->thd", grad_logits, key_block, preferred_element_type=jnp.float32
            )
            key_grads = lax.dynamic_update_slice(
                key_grads, block_terms(attention, grad_logits), (offset, jnp.int32(0))
            )
            return (query_grad, key_grads)

        def query_block(query_grad, key_block, value_block, offset):
            attention, grad_logits = attend(key_block, value_block)
            return query_grad + jnp.einsum(
                "htk,kd->thd", grad_logits, key_block, preferred_element_type=jnp.float32
            )

        return (attend, block_terms, grad_block, query_block)

    init_query = jnp.zeros((row_count, head_count, HEAD), jnp.float32)
    init_grads = (init_query, jnp.zeros((total_keys, 2 * HEAD), jnp.float32))
    keys_all, values_all = (
        lax.all_gather(vision_key, "seq", axis=0, tiled=True),
        lax.all_gather(vision_value, "seq", axis=0, tiled=True),
    )
    stats = sweep(stats_block, init_stats, (keys_all, values_all))
    attend, block_terms, grad_block, query_block = make_grads(stats)
    query_grad, key_grads = sweep(grad_block, init_grads, (keys_all, values_all))
    owned_sums = lax.psum_scatter(key_grads, "seq", scatter_dimension=0, tiled=True)
    owned_grads = owned_sums.astype(jnp.bfloat16)
    merged_weights = jnp.concatenate([key_weight, value_weight], axis=1)
    vision_terms = jnp.einsum(
        "kc,rc->kr",
        owned_grads,
        lax.all_gather(merged_weights, "seq", axis=0, tiled=True),
        preferred_element_type=jnp.float32,
    )
    grad_vision = lax.psum_scatter(
        vision_terms.astype(jnp.bfloat16), "kv", scatter_dimension=1, tiled=True
    )
    grad_query = query_grad.reshape(row_count, head_count * HEAD).astype(jnp.bfloat16)
    return (grad_query, grad_vision)


def solution(mesh):
    return jax.shard_map(
        shards,
        mesh=mesh,
        in_specs=(
            P("seq", "kv"),
            P("seq", "kv"),
            P("seq", "kv"),
            P("seq", "kv"),
            P("seq", "kv"),
            P("seq", "kv"),
        ),
        out_specs=(P("seq", "kv"), P("seq", "kv")),
        check_vma=False,
    )
```

profile of v0, /device:TPU:1, one launch (start us, length us, event | category | flops | bytes accessed | tf_op | source)
XLA Modules:
  0.0 260.0 jit_solution(4501298037912788765)
XLA Ops:
  7.2 0.0 copy-start
  7.2 0.0 reduce-scatter.3.cloned.1.call-start
  7.2 35.6 %all_gather.9 = bf16[512,128]{1,0:T(8,128)(2,1)S(1)} all-gather(bf16[32,128]{1,0:T(8,128)(2,1)} %param.7), channel_id=1, replica_groups=mesh['seq'=16,'kv'=2] {'seq'}, dimensions={0}, use_global_device_ids=true | all-gather | bytes 139264 | tf_op jit(solution)/shard_map/all_gather | solution.py:112
  42.8 29.9 %all_gather.10 = bf16[512,128]{1,0:T(8,128)(2,1)S(1)} all-gather(bf16[32,128]{1,0:T(8,128)(2,1)} %param.8), channel_id=1, replica_groups=mesh['seq'=16,'kv'=2] {'seq'}, dimensions={0}, use_global_device_ids=true | all-gather | bytes 139264 | tf_op jit(solution)/shard_map/all_gather | solution.py:113
  72.7 1.4 bitcast_reduce_fusion
  74.2 0.6 fusion.6
  74.8 0.5 convolution_bitcast_fusion
  75.3 0.0 copy-start.1
  75.3 0.6 fusion.3
  76.0 0.3 copy-done.1
  76.3 0.4 convolution_bitcast_fusion.1
  76.7 0.8 pad_maximum_fusion
  77.6 0.0 reduce-scatter.3.cloned.1.call-update
  77.6 0.0 all-gather.2.cloned.1.call-start
  77.7 0.7 pad_maximum_fusion.1
  78.4 0.0 all-gather.2.cloned.1.call-update
  78.4 0.0 reduce-scatter.5.cloned.1.call-start
  78.5 76.0 %reduce-scatter.3.cloned.1.call-done = f32[32,256]{1,0:T(8,128)} async-done(((f32[512,256]{1,0:T(8,128)}), f32[32,256]{1,0:T(8,128)}) %reduce-scatter.3.cloned.1.call-update) | async-done | bytes 32784 | tf_op jit(solution)/shard_map/reduce_scatter | solution.py:118
  154.5 86.3 %all-gather.2.cloned.1.call-done = bf16[8192,256]{1,0:T(8,128)(2,1)} async-done(((bf16[512,256]{1,0:T(8,128)(2,1)}), bf16[8192,256]{1,0:T(8,128)(2,1)}) %all-gather.2.cloned.1.call-update) | async-done | bytes 4194320 | tf_op jit(solution)/shard_map/all_gather | solution.py:124
  240.8 4.3 %convolution_convert_fusion = bf16[32,8192]{1,0:T(8,128)(2,1)} fusion(bf16[8192,256]{1,0:T(8,128)(2,1)} %all-gather.2.cloned.1.call-done, f32[32,256]{1,0:T(8,128)} %reduce-scatter.3.cloned.1.call-done), kind=kOutput, calls=%fused_computation | convolution fusion | flops 134488064 | bytes 4751360 | tf_op jit(solution)/shard_map/kc,rc->kr/dot_general | solution.py:121
  245.1 0.0 reduce-scatter.5.cloned.1.call-update
  245.2 0.4 convolution_convert_fusion.1
  245.5 0.9 copy.11
  246.4 7.1 %reduce-scatter.5.cloned.1.call-done = bf16[32,4096]{1,0:T(8,128)(2,1)} async-done(((bf16[32,8192]{1,0:T(8,128)(2,1)}), bf16[32,4096]{1,0:T(8,128)(2,1)}) %reduce-scatter.5.cloned.1.call-update) | async-done | bytes 262160 | tf_op jit(solution)/shard_map/reduce_scatter | solution.py:127
  (6 shorter events, 0.0 us)
Async XLA Ops:
  7.2 67.0 %copy-start = (bf16[128,1024]{1,0:T(8,128)(2,1)S(1)}, bf16[128,1024]{1,0:T(8,128)(2,1)}, u32[]{:S(2)}) copy-start(bf16[128,1024]{1,0:T(8,128)(2,1)} %param.9) | copy-start | bytes 786436
  7.2 147.3 %reduce-scatter.3.cloned.1.call-start = ((), (), s32[]{:S(2)}) async-start(), calls=%async_computation.2 | async-start | bytes 557056 | tf_op jit(solution)/shard_map/reduce_scatter | solution.py:118
  75.3 1.0 copy-start.1
  76.3 1.4 copy-start.2
  76.3 1.4 copy-start.3
  77.6 163.2 %all-gather.2.cloned.1.call-start = ((), (), s32[]{:S(2)}) async-start(), calls=%async_computation.3 | async-start | bytes 4456448 | tf_op jit(solution)/shard_map/all_gather | solution.py:124
  78.4 175.0 %reduce-scatter.5.cloned.1.call-start = ((), (), s32[]{:S(2)}) async-start(), calls=%async_computation.4 | async-start | bytes 786432 | tf_op jit(solution)/shard_map/reduce_scatter | solution.py:127
Sparse Core Ops, SparseCore 0:
  77.7 76.7 reduce-scatter.2
  158.2 82.5 all-gather.1
  245.3 8.0 reduce-scatter.4
where the time goes:
time: 260 us
  waiting for transfers between devices  169 us (65%)
  blocking collectives  65.5 us (25%)
  between operations  13.8 us (5%)
  matrix products  7.65 us (3%)
    all_gather x1, waiting for transfers between devices, shards(): lax.all_gather(merged_weights, 'seq', axis=0, tiled=True)  86.3 us
    reduce_scatter x1, waiting for transfers between devices, shards(): lax.psum_scatter(key_grads, 'seq', scatter_dimension=0, tiled=True)  76 us
    all_gather x1, blocking collectives, shards(): lax.all_gather(vision_key, 'seq', axis=0, tiled=True)  35.6 us
    all_gather x1, blocking collectives, shards(): lax.all_gather(vision_value, 'seq', axis=0, tiled=True)  29.9 us
    reduce_scatter x1, waiting for transfers between devices, shards(): lax.psum_scatter(vision_terms.astype(jnp.bfloat16), 'kv', scatter_dimensi...  7.05 us
  transfers between devices with their start and end apart: 3, of which 3 were waited for; matrix products, arithmetic and copies ran while one was open for 1% of the time, Pallas kernels for 0%

commit v1 on v0

v1 whole, which is shorter than its diff:
```python
import math

import jax
import jax.numpy as jnp
from jax import lax
from jax.sharding import PartitionSpec as P

HEAD = 128


def exchange(block, axis, size, distance):
    return lax.ppermute(block, axis, [(i, i ^ distance) for i in range(size)])


def gather_cube(block, cube):
    blocks = [block]
    if cube >= 4:
        blocks += [exchange(block, "seq", 2 * cube, d) for d in (1, 2, 3)]
    while len(blocks) < cube:
        distance = len(blocks)
        moved = exchange(jnp.stack(blocks), "seq", 2 * cube, distance)
        blocks += [moved[i] for i in range(distance)]
    return jnp.stack(blocks)


def attention_terms(queries, upstream, keys, values):
    scaling = 1.0 / math.sqrt(HEAD)
    rows = queries.shape[0]
    heads = queries.shape[1] // HEAD
    queries = queries.reshape(rows, heads, HEAD)
    upstream = upstream.reshape(rows, heads, HEAD)
    f32 = jnp.float32
    logits = jnp.einsum("thd,kd->htk", queries, keys, preferred_element_type=f32) * scaling
    grad_probs = jnp.einsum("thd,kd->htk", upstream, values, preferred_element_type=f32)
    exponent = jnp.exp(logits - jnp.max(logits, axis=2, keepdims=True))
    attention = exponent / jnp.sum(exponent, axis=2, keepdims=True)
    row_dots = jnp.sum(attention * grad_probs, axis=2, keepdims=True)
    grad_logits = (attention * (grad_probs - row_dots) * scaling).astype(jnp.bfloat16)
    attention_low = attention.astype(jnp.bfloat16)
    grad_query = jnp.einsum("htk,kd->thd", grad_logits, keys, preferred_element_type=f32)
    key_term = jnp.einsum("htk,thd->kd", grad_logits, queries, preferred_element_type=f32)
    value_term = jnp.einsum("htk,thd->kd", attention_low, upstream, preferred_element_type=f32)
    terms = jnp.concatenate([key_term, value_term], axis=1).astype(jnp.bfloat16)
    return grad_query.reshape(rows, heads * HEAD).astype(jnp.bfloat16), terms


def shards(text_query, vision_key, vision_value, grad_output, key_weight, value_weight):
    chips = lax.axis_size("seq")
    cores = lax.axis_size("kv")
    cube = chips // 2
    half = cores // 2
    me = lax.axis_index("seq")
    core = lax.axis_index("kv")
    groups = [list(range(cube)), list(range(cube, chips))]
    own = vision_key.shape[0]
    weights = gather_cube(jnp.concatenate([key_weight, value_weight], axis=1), cube)

    pair = jnp.concatenate([vision_key, vision_value], axis=1)
    everyone = lax.all_to_all(
        jnp.broadcast_to(pair, (chips,) + pair.shape), "seq", 0, 0
    ).reshape(chips * own, 2 * HEAD)
    grad_query, terms = attention_terms(
        text_query, grad_output, everyone[:, :HEAD], everyone[:, HEAD:]
    )

    blocks = terms.reshape(2, cube, own, 2 * HEAD).transpose(1, 0, 2, 3)
    arrived = lax.all_to_all(blocks, "seq", 0, 0, axis_index_groups=groups)
    partial = jnp.sum(arrived.astype(jnp.float32), axis=0)
    grads = (partial + exchange(partial, "seq", chips, cube)).astype(jnp.bfloat16)

    product = jnp.einsum("qtc,drc->qdtr", grads, weights, preferred_element_type=jnp.float32)
    place = (me % cube) ^ jnp.arange(cube)
    product = jnp.take(product, place, axis=1)
    columns = product.transpose(0, 2, 1, 3).reshape(2, own, half, -1).transpose(0, 2, 1, 3)
    columns = columns.reshape(cores, own, -1)
    total = lax.dynamic_index_in_dim(columns, core, 0, keepdims=False)
    for d in range(1, cores):
        other = lax.dynamic_index_in_dim(columns, core ^ d, 0, keepdims=False)
        total = total + exchange(other.astype(jnp.bfloat16), "kv", cores, d).astype(jnp.float32)
    total = total.astype(jnp.bfloat16)
    routes = [
        (u * cores + j, (u ^ cube) * cores + (j + half) % cores)
        for u in range(chips)
        for j in range(cores)
        if j // half != u // cube
    ]
    received = lax.ppermute(total, ("seq", "kv"), routes)
    grad_vision = jnp.where(core // half == me // cube, total, received)
    return (grad_query, grad_vision)


def solution(mesh):
    spec = P("seq", "kv")
    return jax.shard_map(
        shards,
        mesh=mesh,
        in_specs=(spec,) * 6,
        out_specs=(spec, spec),
        check_vma=False,
    )
```

time: 260 us -> 75.6 us (0.29)
  waiting for transfers between devices: 169 us -> 22.7 us
  blocking collectives: 65.5 us -> 0 us
  starting transfers between devices: 0.12 us -> 22.6 us
  local copies, waits for them, and re-layouts: 1.18 us -> 15.1 us
  between operations: 13.8 us -> 0.87 us
  other arithmetic: 2.21 us -> 5.96 us
    all_gather x1 -> x0, waiting for transfers between devices: 86.3 us -> none  [shards(): lax.all_gather(merged_weights, 'seq', axis=0, tiled=True)]
    reduce_scatter x2 -> x0, waiting for transfers between devices: 83.1 us -> none  [the longest x1 76 us: shards(): lax.psum_scatter(key_grads, 'seq', scatter_dimension=0, tiled=True)]
    all_gather x2 -> x0, blocking collectives: 65.5 us -> none  [the longest x1 35.6 us: shards(): lax.all_gather(vision_key, 'seq', axis=0, tiled=True)]
    all_to_all x0 -> x2, waiting for transfers between devices: none -> 13.2 us  [the longest x1 12.4 us: shards(): arrived = lax.all_to_all(blocks, 'seq', 0, 0, axis_index_groups=groups)]
    ppermute x0 -> x7, starting transfers between devices: none -> 12.5 us  [the longest x6 9.15 us: exchange(): return lax.ppermute(block, axis, [(i, i ^ distance) for i in range(size)])]
    all_to_all x0 -> x2, starting transfers between devices: none -> 10.1 us  [the longest x1 6.7 us: shards(): lax.all_to_all(jnp.broadcast_to(pair, (chips,) + pair.shape), 'seq', 0, 0)]
    ppermute x0 -> x7, waiting for transfers between devices: none -> 9.5 us  [the longest x6 4.82 us: exchange(): return lax.ppermute(block, axis, [(i, i ^ distance) for i in range(size)])]
    unnamed x9 -> x28, local copies, waits for them, and re-layouts: 1.18 us -> 9.36 us
  transfers between devices with their start and end apart: 3 -> 9, of which waited for: 3 -> 6; matrix products, arithmetic and copies ran while one was open for 1% -> 25% of each run, Pallas kernels for 0% -> 0%
where the time goes in v1:
time: 75.6 us; the launch traced here: 75 us
  waiting for transfers between devices  22.7 us (30%)
  starting transfers between devices  22.6 us (30%)
  local copies, waits for them, and re-layouts  15.1 us (20%)
  matrix products  7.71 us (10%)
  other arithmetic  5.96 us (8%)
  between operations  0.87 us (1%)
    all_to_all x1, waiting for transfers between devices, shards(): arrived = lax.all_to_all(blocks, 'seq', 0, 0, axis_index_groups=groups)  12.4 us
    unnamed x28, local copies, waits for them, and re-layouts  9.36 us
    ppermute x6, starting transfers between devices, exchange(): return lax.ppermute(block, axis, [(i, i ^ distance) for i in range(size)])  9.15 us
    all_to_all x1, starting transfers between devices, shards(): lax.all_to_all(jnp.broadcast_to(pair, (chips,) + pair.shape), 'seq', 0, 0)  6.7 us
    ppermute x6, waiting for transfers between devices, exchange(): return lax.ppermute(block, axis, [(i, i ^ distance) for i in range(size)])  4.82 us
    ppermute x1, waiting for transfers between devices, shards(): received = lax.ppermute(total, ('seq', 'kv'), routes)  4.68 us
    all_to_all x1, starting transfers between devices, shards(): arrived = lax.all_to_all(blocks, 'seq', 0, 0, axis_index_groups=groups)  3.41 us
    ppermute x1, starting transfers between devices, shards(): received = lax.ppermute(total, ('seq', 'kv'), routes)  3.38 us
  transfers between devices with their start and end apart: 9, of which 6 were waited for; matrix products, arithmetic and copies ran while one was open for 25% of the time, Pallas kernels for 0%

profile of v1, /device:TPU:1, one launch (start us, length us, event | category | flops | bytes accessed | tf_op | source)
XLA Modules:
  0.0 75.0 jit_solution(1995533231156684763)
XLA Ops:
  0.7 1.0 %constant_dynamic-update-slice_fusion.1 = bf16[512,256]{1,0:T(8,128)(2,1)S(1)} fusion(bf16[512,128]{1,0:T(8,128)(2,1)} %param.10), kind=kLoop, calls=%fused_computation.53 | loop fusion | bytes 262144
  1.6 0.9 %constant_dynamic-update-slice_fusion = bf16[512,256]{1,0:T(8,128)(2,1)S(1)} fusion(bf16[512,256]{1,0:T(8,128)(2,1)S(1)} %constant_dynamic-update-slice_fusion.1, bf16[512,128]{1,0:T(8,128)(2,1)} %param.11), kind=kLoop, calls=%fused_computation.52 | loop fusion | bytes 262144 | tf_op jit(solution)/shard_map/concatenate | solution.py:56
  2.6 3.1 %collective-permute-start.2 = (bf16[512,256]{1,0:T(8,128)(2,1)S(1)}, bf16[512,256]{1,0:T(8,128)(2,1)S(1)}, u32[]{:S(2)}, u32[]{:S(2)}) collective-permute-start(bf16[512,256]{1,0:T(8,128)(2,1)S(1)} %constant_dynamic-update-slice_fusion), channel_id=1, source_target_pairs={{0,6},{2,4},{4,2},{6,0},{8,14},{10,12},{12,10},{14,8},{16,22},{18,... | collective-permute-start | bytes 786440 | tf_op jit(solution)/shard_map/ppermute | solution.py:12
  7.5 6.7 %all-to-all-start = ((bf16[16,32,256]{2,1,0:T(8,128)(2,1)}), bf16[16,32,256]{2,1,0:T(8,128)(2,1)S(1)}, u32[]{:S(2)}, u32[]{:S(2)}) async-start(bf16[16,32,256]{2,1,0:T(8,128)(2,1)} %broadcast_in_dim.16), calls=%async_computation | async-start | bytes 524288 | tf_op jit(solution)/shard_map/all_to_all | solution.py:59
  16.5 1.9 %collective-permute-done.1 = bf16[512,256]{1,0:T(8,128)(2,1)S(1)} collective-permute-done((bf16[512,256]{1,0:T(8,128)(2,1)S(1)}, bf16[512,256]{1,0:T(8,128)(2,1)S(1)}, u32[]{:S(2)}, u32[]{:S(2)}) %collective-permute-start.1) | collective-permute-done | bytes 262176 | tf_op jit(solution)/shard_map/ppermute | solution.py:12
  18.5 1.6 %collective-permute-start.3 = (bf16[4,512,256]{2,1,0:T(8,128)(2,1)S(1)}, bf16[4,512,256]{2,1,0:T(8,128)(2,1)}, u32[]{:S(2)}, u32[]{:S(2)}) collective-permute-start(bf16[4,512,256]{2,1,0:T(8,128)(2,1)S(1)} %pad_maximum_fusion), channel_id=1, source_target_pairs={{0,8},{2,10},{4,12},{6,14},{8,0},{10,2},{12,4},{14,6},{16,24},{18,... | collective-permute-start | bytes 3145736 | tf_op jit(solution)/shard_map/ppermute | solution.py:12
  20.8 0.9 %all-to-all-done = bf16[16,32,256]{2,1,0:T(8,128)(2,1)S(1)} async-done(((bf16[16,32,256]{2,1,0:T(8,128)(2,1)}), bf16[16,32,256]{2,1,0:T(8,128)(2,1)S(1)}, u32[]{:S(2)}, u32[]{:S(2)}) %all-to-all-start) | async-done | bytes 262176 | tf_op jit(solution)/shard_map/all_to_all | solution.py:59
  22.4 1.4 %bitcast_reduce_fusion = (f32[8,128]{1,0:T(8,128)S(1)}, f32[512,128,8]{1,0,2:T(8,128)S(1)}) fusion(bf16[512,256]{1,0:T(8,128)(2,1)} %bitcast.137, bf16[128,1024]{1,0:T(8,128)(2,1)S(1)} %copy-done.1), kind=kOutput, calls=%fused_computation.17 | convolution fusion | flops 135265280 | bytes 2494464 | tf_op jit(solution)/shard_map/thd,kd->htk/dot_general | solution.py:33
  27.8 3.4 %all-to-all-start.1 = ((bf16[8,2,32,256]{3,2,1,0:T(8,128)(2,1)}), bf16[8,2,32,256]{3,2,1,0:T(8,128)(2,1)S(1)}, u32[]{:S(2)}, u32[]{:S(2)}) async-start(bf16[8,2,32,256]{3,2,1,0:T(8,128)(2,1)} %maximum_bitcast_fusion), calls=%async_computation.1 | async-start | bytes 524288 | tf_op jit(solution)/shard_map/all_to_all | solution.py:67
  31.2 1.7 %constant_dynamic-update-slice_fusion.4 = bf16[8,512,256]{2,1,0:T(8,128)(2,1)} fusion(bf16[8,512,256]{2,1,0:T(8,128)(2,1)} %constant_dynamic-update-slice_fusion.5, bf16[512,256]{1,0:T(8,128)(2,1)} %copy-done.3), kind=kLoop, calls=%fused_computation.56 | loop fusion | bytes 524288
  32.9 1.7 %constant_dynamic-update-slice_fusion.3 = bf16[8,512,256]{2,1,0:T(8,128)(2,1)} fusion(bf16[8,512,256]{2,1,0:T(8,128)(2,1)} %constant_dynamic-update-slice_fusion.4, bf16[512,256]{1,0:T(8,128)(2,1)} %copy-done.2), kind=kLoop, calls=%fused_computation.55 | loop fusion | bytes 524288
  34.6 12.4 %all-to-all-done.1 = bf16[8,2,32,256]{3,2,1,0:T(8,128)(2,1)S(1)} async-done(((bf16[8,2,32,256]{3,2,1,0:T(8,128)(2,1)}), bf16[8,2,32,256]{3,2,1,0:T(8,128)(2,1)S(1)}, u32[]{:S(2)}, u32[]{:S(2)}) %all-to-all-start.1) | async-done | bytes 262176 | tf_op jit(solution)/shard_map/all_to_all | solution.py:67
  47.0 0.9 %collective-permute-start.4 = (f32[2,32,256]{2,1,0:T(8,128)S(1)}, f32[2,32,256]{2,1,0:T(8,128)S(1)}, u32[]{:S(2)}, u32[]{:S(2)}) collective-permute-start(f32[2,32,256]{2,1,0:T(8,128)S(1)} %convert_reduce_fusion), channel_id=1, source_target_pairs={{0,16},{2,18},{4,20},{6,22},{8,24},{10,26},{12,28},{14,30},{16,0},... | collective-permute-start | bytes 196616 | tf_op jit(solution)/shard_map/ppermute | solution.py:12
  47.9 2.3 %constant_dynamic-update-slice_fusion.2 = bf16[8,512,256]{2,1,0:T(8,128)(2,1)} fusion(bf16[8,512,256]{2,1,0:T(8,128)(2,1)} %constant_dynamic-update-slice_fusion.3, bf16[4,512,256]{2,1,0:T(8,128)(2,1)} %collective-permute-done.3), kind=kLoop, calls=%fused_computation.54 | loop fusion | bytes 2097152 | tf_op jit(solution)/shard_map/stack | solution.py:23
  50.2 1.6 %collective-permute-done.4 = f32[2,32,256]{2,1,0:T(8,128)S(1)} collective-permute-done((f32[2,32,256]{2,1,0:T(8,128)S(1)}, f32[2,32,256]{2,1,0:T(8,128)S(1)}, u32[]{:S(2)}, u32[]{:S(2)}) %collective-permute-start.4) | collective-permute-done | bytes 65568 | tf_op jit(solution)/shard_map/ppermute | solution.py:12
  51.8 2.3 %fusion.14 = f32[2,8,32,512]{3,2,0,1:T(8,128)S(1)} fusion(bf16[8,512,256]{2,1,0:T(8,128)(2,1)} %constant_dynamic-update-slice_fusion.2, f32[2,32,256]{2,1,0:T(8,128)S(1)} %convert_reduce_fusion, f32[2,32,256]{2,1,0:T(8,128)S(1)} %collective-permute-done.4), kind=kOutput, calls=%fused_computation.21 | convolution fusion | flops 134250496 | bytes 3276800 | tf_op jit(solution)/shard_map/qtc,drc->qdtr/dot_general | solution.py:71
  54.1 1.6 %gather_fusion = f32[8,2,32,512]{3,2,1,0:T(8,128)} fusion(f32[2,8,32,512]{3,2,0,1:T(8,128)S(1)} %fusion.14, s32[1024]{0:T(1024)S(1)} %pad_clamp_fusion), kind=kCustom, calls=%fused_computation | custom fusion | bytes 2097184 | tf_op jit(solution)/shard_map/jit(_take)/gather | solution.py:73
  55.7 1.4 %select_bitcast_fusion = f32[8,2,4,8,512]{4,3,2,1,0:T(8,128)S(1)} fusion(f32[8,2,32,512]{3,2,1,0:T(8,128)} %gather_fusion, pred[8]{0:T(512)(128)(4,1)S(1)} %compare_and_fusion), kind=kLoop, calls=%fused_computation.24 | loop fusion | flops 262144 | bytes 2097160
  57.3 3.3 %collective-permute-start.5 = (bf16[32,4096]{1,0:T(8,128)(2,1)S(1)}, bf16[32,4096]{1,0:T(8,128)(2,1)}, u32[]{:S(2)}, u32[]{:S(2)}) collective-permute-start(bf16[32,4096]{1,0:T(8,128)(2,1)S(1)} %fusion.23), channel_id=1, source_target_pairs={{0,1},{1,0},{2,3},{3,2},{4,5},{5,4},{6,7},{7,6},{8,9},{9,8},{10,11... | collective-permute-start | bytes 786440 | tf_op jit(solution)/shard_map/ppermute | solution.py:12
  60.6 1.3 %collective-permute-done.5 = bf16[32,4096]{1,0:T(8,128)(2,1)} collective-permute-done((bf16[32,4096]{1,0:T(8,128)(2,1)S(1)}, bf16[32,4096]{1,0:T(8,128)(2,1)}, u32[]{:S(2)}, u32[]{:S(2)}) %collective-permute-start.5) | collective-permute-done | bytes 262176 | tf_op jit(solution)/shard_map/ppermute | solution.py:12
  61.9 1.0 %fusion.20 = bf16[32,4096]{1,0:T(8,128)(2,1)S(1)} fusion(bf16[32,4096]{1,0:T(8,128)(2,1)} %collective-permute-done.5, f32[2,32,4096]{2,1,0:T(8,128)S(1)} %bitcast.129, s32[]{:T(128)S(6)} %select_n.58), kind=kLoop, calls=%fused_computation.28 | loop fusion | flops 393216 | bytes 1048580 | tf_op jit(solution)/shard_map/convert_element_type | solution.py:80
  62.9 3.4 %collective-permute-start.6 = (bf16[32,4096]{1,0:T(8,128)(2,1)S(1)}, bf16[32,4096]{1,0:T(8,128)(2,1)S(1)}, u32[]{:S(2)}, u32[]{:S(2)}) collective-permute-start(bf16[32,4096]{1,0:T(8,128)(2,1)S(1)} %fusion.20), channel_id=1, source_target_pairs={{1,16},{3,18},{5,20},{7,22},{9,24},{11,26},{13,28},{15,30},{16,1},... | collective-permute-start | bytes 786440 | tf_op jit(solution)/shard_map/ppermute | solution.py:87
  66.2 2.5 %convolution_convert_fusion = bf16[128,8,128]{2,0,1:T(8,128)(2,1)S(1)} fusion(f32[512,128,8]{1,0,2:T(8,128)} %copy-done, f32[8,128]{1,0:T(8,128)S(1)} %get-tuple-element.12, f32[512,128,8]{1,0,2:T(8,128)S(1)} %get-tuple-element.11, f32[8,128]{1,0:T(8,128)S(1)} %fusion.13, f32[8,128]{1,0:T(8,128)S(1)} %get-tuple-element.10, bf16[512,256]{1,0:T(8,128)(2,1)} %bitcast.138), kind=kOutput, calls=%fused_computation.22 | convolution fusion | flops 138018816 | bytes 4599808 | tf_op jit(solution)/shard_map/htk,kd->thd/dot_general | solution.py:40
  69.6 4.7 %collective-permute-done.6 = bf16[32,4096]{1,0:T(8,128)(2,1)S(1)} collective-permute-done((bf16[32,4096]{1,0:T(8,128)(2,1)S(1)}, bf16[32,4096]{1,0:T(8,128)(2,1)S(1)}, u32[]{:S(2)}, u32[]{:S(2)}) %collective-permute-start.6) | collective-permute-done | bytes 262176 | tf_op jit(solution)/shard_map/ppermute | solution.py:87
  (47 shorter events, 11.3 us)
Async XLA Ops:
  0.6 14.3 %copy-start.6 = (bf16[128,1024]{1,0:T(8,128)(2,1)S(1)}, bf16[128,1024]{1,0:T(8,128)(2,1)}, u32[]{:S(2)}) copy-start(bf16[128,1024]{1,0:T(8,128)(2,1)} %param.9) | copy-start | bytes 786436
  0.6 15.0 %copy-start.1 = (bf16[128,1024]{1,0:T(8,128)(2,1)S(1)}, bf16[128,1024]{1,0:T(8,128)(2,1)}, u32[]{:S(2)}) copy-start(bf16[128,1024]{1,0:T(8,128)(2,1)} %param.6) | copy-start | bytes 786436
  2.6 13.9 %collective-permute-start.2 = (bf16[512,256]{1,0:T(8,128)(2,1)S(1)}, bf16[512,256]{1,0:T(8,128)(2,1)S(1)}, u32[]{:S(2)}, u32[]{:S(2)}) collective-permute-start(bf16[512,256]{1,0:T(8,128)(2,1)S(1)} %constant_dynamic-update-slice_fusion), channel_id=1, source_target_pairs={{0,6},{2,4},{4,2},{6,0},{8,14},{10,12},{12,10},{14,8},{16,22},{18,... | collective-permute-start | bytes 786440 | tf_op jit(solution)/shard_map/ppermute | solution.py:12
  5.6 12.7 %collective-permute-start.1 = (bf16[512,256]{1,0:T(8,128)(2,1)S(1)}, bf16[512,256]{1,0:T(8,128)(2,1)S(1)}, u32[]{:S(2)}, u32[]{:S(2)}) collective-permute-start(bf16[512,256]{1,0:T(8,128)(2,1)S(1)} %constant_dynamic-update-slice_fusion), channel_id=1, source_target_pairs={{0,4},{2,6},{4,0},{6,2},{8,12},{10,14},{12,8},{14,10},{16,20},{18,... | collective-permute-start | bytes 786440 | tf_op jit(solution)/shard_map/ppermute | solution.py:12
  5.9 12.5 %collective-permute-start = (bf16[512,256]{1,0:T(8,128)(2,1)S(1)}, bf16[512,256]{1,0:T(8,128)(2,1)S(1)}, u32[]{:S(2)}, u32[]{:S(2)}) collective-permute-start(bf16[512,256]{1,0:T(8,128)(2,1)S(1)} %constant_dynamic-update-slice_fusion), channel_id=1, source_target_pairs={{0,2},{2,0},{4,6},{6,4},{8,10},{10,8},{12,14},{14,12},{16,18},{18,... | collective-permute-start | bytes 786440 | tf_op jit(solution)/shard_map/ppermute | solution.py:12
  7.5 14.2 %all-to-all-start = ((bf16[16,32,256]{2,1,0:T(8,128)(2,1)}), bf16[16,32,256]{2,1,0:T(8,128)(2,1)S(1)}, u32[]{:S(2)}, u32[]{:S(2)}) async-start(bf16[16,32,256]{2,1,0:T(8,128)(2,1)} %broadcast_in_dim.16), calls=%async_computation | async-start | bytes 524288 | tf_op jit(solution)/shard_map/all_to_all | solution.py:59
  16.5 5.2 %copy-start.2 = (bf16[512,256]{1,0:T(8,128)(2,1)}, bf16[512,256]{1,0:T(8,128)(2,1)S(1)}, u32[]{:S(2)}) copy-start(bf16[512,256]{1,0:T(8,128)(2,1)S(1)} %collective-permute-done.2) | copy-start | bytes 786436
  18.4 3.3 %copy-start.3 = (bf16[512,256]{1,0:T(8,128)(2,1)}, bf16[512,256]{1,0:T(8,128)(2,1)S(1)}, u32[]{:S(2)}) copy-start(bf16[512,256]{1,0:T(8,128)(2,1)S(1)} %collective-permute-done.1) | copy-start | bytes 786436
  18.5 29.4 %collective-permute-start.3 = (bf16[4,512,256]{2,1,0:T(8,128)(2,1)S(1)}, bf16[4,512,256]{2,1,0:T(8,128)(2,1)}, u32[]{:S(2)}, u32[]{:S(2)}) collective-permute-start(bf16[4,512,256]{2,1,0:T(8,128)(2,1)S(1)} %pad_maximum_fusion), channel_id=1, source_target_pairs={{0,8},{2,10},{4,12},{6,14},{8,0},{10,2},{12,4},{14,6},{16,24},{18,... | collective-permute-start | bytes 3145736 | tf_op jit(solution)/shard_map/ppermute | solution.py:12
  21.6 0.7 copy-start.4
  22.3 1.8 %copy-start.5 = (bf16[16,32,256]{2,1,0:T(8,128)(2,1)S(1)}, bf16[16,32,256]{2,1,0:T(8,128)(2,1)}, u32[]{:S(2)}) copy-start(bf16[16,32,256]{2,1,0:T(8,128)(2,1)} %copy-done.4) | copy-start | bytes 786436
  22.4 1.8 %copy-start.7 = (bf16[128,1024]{1,0:T(8,128)(2,1)S(1)}, bf16[128,1024]{1,0:T(8,128)(2,1)}, u32[]{:S(2)}) copy-start(bf16[128,1024]{1,0:T(8,128)(2,1)} %param.9) | copy-start | bytes 786436
  24.8 1.3 %copy-start = (f32[512,128,8]{1,0,2:T(8,128)}, f32[512,128,8]{1,0,2:T(8,128)S(1)}, u32[]{:S(2)}) copy-start(f32[512,128,8]{1,0,2:T(8,128)S(1)} %get-tuple-element.13) | copy-start | bytes 6291460
  24.8 1.3 %copy-start.9 = (bf16[16,8,8,128]{3,2,1,0:T(8,128)(2,1)S(1)}, bf16[16,8,8,128]{3,2,1,0:T(8,128)(2,1)}, u32[]{:S(2)}) copy-start(bf16[16,8,8,128]{3,2,1,0:T(8,128)(2,1)} %copy.54) | copy-start | bytes 786436
  24.8 1.8 %copy-start.8 = (bf16[16,8,8,128]{3,2,1,0:T(8,128)(2,1)S(1)}, bf16[16,8,8,128]{3,2,1,0:T(8,128)(2,1)}, u32[]{:S(2)}) copy-start(bf16[16,8,8,128]{3,2,1,0:T(8,128)(2,1)} %copy.55) | copy-start | bytes 786436
  27.8 19.2 %all-to-all-start.1 = ((bf16[8,2,32,256]{3,2,1,0:T(8,128)(2,1)}), bf16[8,2,32,256]{3,2,1,0:T(8,128)(2,1)S(1)}, u32[]{:S(2)}, u32[]{:S(2)}) async-start(bf16[8,2,32,256]{3,2,1,0:T(8,128)(2,1)} %maximum_bitcast_fusion), calls=%async_computation.1 | async-start | bytes 524288 | tf_op jit(solution)/shard_map/all_to_all | solution.py:67
  47.0 4.8 %collective-permute-start.4 = (f32[2,32,256]{2,1,0:T(8,128)S(1)}, f32[2,32,256]{2,1,0:T(8,128)S(1)}, u32[]{:S(2)}, u32[]{:S(2)}) collective-permute-start(f32[2,32,256]{2,1,0:T(8,128)S(1)} %convert_reduce_fusion), channel_id=1, source_target_pairs={{0,16},{2,18},{4,20},{6,22},{8,24},{10,26},{12,28},{14,30},{16,0},... | collective-permute-start | bytes 196616 | tf_op jit(solution)/shard_map/ppermute | solution.py:12
  57.3 4.6 %collective-permute-start.5 = (bf16[32,4096]{1,0:T(8,128)(2,1)S(1)}, bf16[32,4096]{1,0:T(8,128)(2,1)}, u32[]{:S(2)}, u32[]{:S(2)}) collective-permute-start(bf16[32,4096]{1,0:T(8,128)(2,1)S(1)} %fusion.23), channel_id=1, source_target_pairs={{0,1},{1,0},{2,3},{3,2},{4,5},{5,4},{6,7},{7,6},{8,9},{9,8},{10,11... | collective-permute-start | bytes 786440 | tf_op jit(solution)/shard_map/ppermute | solution.py:12
  62.9 11.4 %collective-permute-start.6 = (bf16[32,4096]{1,0:T(8,128)(2,1)S(1)}, bf16[32,4096]{1,0:T(8,128)(2,1)S(1)}, u32[]{:S(2)}, u32[]{:S(2)}) collective-permute-start(bf16[32,4096]{1,0:T(8,128)(2,1)S(1)} %fusion.20), channel_id=1, source_target_pairs={{1,16},{3,18},{5,20},{7,22},{9,24},{11,26},{13,28},{15,30},{16,1},... | collective-permute-start | bytes 786440 | tf_op jit(solution)/shard_map/ppermute | solution.py:87

commit v2 on v1

v2 whole, which is shorter than its diff:
```python
import functools
import math

import jax
import jax.numpy as jnp
from jax import lax
from jax.experimental import pallas as pl
from jax.experimental.pallas import tpu as pltpu
from jax.sharding import PartitionSpec as P

HEAD = 128
F32 = jnp.float32
BF16 = jnp.bfloat16
IN_VMEM = pl.BlockSpec(memory_space=pltpu.VMEM)
SIDE_BY_SIDE = (((1,), (1,)), ((), ()))
ON_TOP = (((0,), (0,)), ((), ()))


def exchange(block, axis, size, distance):
    return lax.ppermute(block, axis, [(i, i ^ distance) for i in range(size)])


def attention_kernel(queries_ref, upstream_ref, vision_ref, query_ref, terms_ref, rows, low):
    row_count, width = queries_ref.shape
    heads = width // HEAD
    scaling = 1.0 / math.sqrt(HEAD)
    keys = vision_ref[:, :HEAD]
    values = vision_ref[:, HEAD:]
    for h in range(heads):
        lanes = slice(h * HEAD, (h + 1) * HEAD)
        at = slice(h * row_count, (h + 1) * row_count)
        rows[0, at, :] = queries_ref[:, lanes]
        rows[1, at, :] = upstream_ref[:, lanes]
    step = 2 if heads % 2 == 0 else 1
    for h in range(0, heads, step):
        at = slice(h * row_count, (h + step) * row_count)
        logits = lax.dot_general(keys, rows[0, at, :], SIDE_BY_SIDE, preferred_element_type=F32)
        grad_probs = lax.dot_general(values, rows[1, at, :], SIDE_BY_SIDE, preferred_element_type=F32)
        top = jnp.max(logits, axis=0, keepdims=True)
        exponent = jnp.exp2((logits - top) * (scaling * math.log2(math.e)))
        inverse = 1.0 / jnp.sum(exponent, axis=0, keepdims=True)
        row_dots = jnp.sum(exponent * grad_probs, axis=0, keepdims=True) * inverse
        low[1, :, at] = (exponent * inverse).astype(BF16)
        grad_logits = (exponent * (grad_probs - row_dots) * (inverse * scaling)).astype(BF16)
        low[0, :, at] = grad_logits
        grad_query = lax.dot_general(grad_logits, keys, ON_TOP, preferred_element_type=F32)
        for i in range(step):
            lanes = slice((h + i) * HEAD, (h + i + 1) * HEAD)
            query_ref[:, lanes] = grad_query[i * row_count : (i + 1) * row_count].astype(BF16)
    plane, line, own, _ = terms_ref.shape
    for i in range(2):
        term = jnp.dot(low[i], rows[i], preferred_element_type=F32).astype(BF16)
        term = term.reshape(line, plane, own, HEAD)
        for p in range(plane):
            terms_ref[p, :, :, i * HEAD : (i + 1) * HEAD] = term[:, p]


def attention_terms(queries, upstream, vision, plane, line):
    rows, width = queries.shape
    tokens = vision.shape[0]
    pairs = rows * width // HEAD
    return pl.pallas_call(
        attention_kernel,
        out_shape=(
            jax.ShapeDtypeStruct((rows, width), BF16),
            jax.ShapeDtypeStruct((plane, line, tokens // (plane * line), 2 * HEAD), BF16),
        ),
        in_specs=[IN_VMEM] * 3,
        out_specs=(IN_VMEM, IN_VMEM),
        scratch_shapes=[
            pltpu.VMEM((2, pairs, HEAD), BF16),
            pltpu.VMEM((2, tokens, pairs), BF16),
        ],
        compiler_params=pltpu.CompilerParams(vmem_limit_bytes=48 * 1024 * 1024),
        cost_estimate=pl.CostEstimate(
            flops=10 * pairs * tokens * HEAD,
            bytes_accessed=8 * rows * width + 4 * tokens * HEAD,
            transcendentals=pairs * tokens,
        ),
        name="attention_terms",
    )(queries, upstream, vision)


def project_kernel(mine_ref, near_ref, far_ref, cross_ref, *refs):
    plane = (len(refs) - 3) // 2
    weights, (stay_ref, go_ref, grads) = refs[:-3], refs[-3:]
    me = lax.axis_index("seq")
    home = lax.axis_index("kv") == me // (2 * plane)
    odd = lax.rem(me // plane, 2)
    spot = lax.rem(me, plane)
    total = mine_ref[...] + near_ref[...].astype(F32) + far_ref[...].astype(F32)
    grads[...] = (total + cross_ref[...].astype(F32)).astype(BF16)
    stay = jnp.where(home, odd, 1 - odd)
    width = grads.shape[2] // 2
    rows = grads.shape[1]
    ordered = jnp.concatenate([grads[stay], grads[1 - stay]], axis=0)
    for d in range(plane):
        product = lax.dot_general(
            ordered[:, :width], weights[d][...], SIDE_BY_SIDE, preferred_element_type=F32
        )
        product += lax.dot_general(
            ordered[:, width:], weights[plane + d][...], SIDE_BY_SIDE, preferred_element_type=F32
        )
        columns = weights[d].shape[0]
        at = pl.ds(pl.multiple_of(jnp.bitwise_xor(spot, d) * columns, columns), columns)
        stay_ref[:, at] = product[:rows].astype(BF16)
        go_ref[:, at] = product[rows:].astype(BF16)


def project(mine, arrived, weights):
    rows = mine.shape[1]
    plane = len(weights) // 2
    columns = plane * weights[0].shape[0]
    shape = jax.ShapeDtypeStruct((rows, columns), BF16)
    return pl.pallas_call(
        project_kernel,
        out_shape=(shape, shape),
        in_specs=[IN_VMEM] * (4 + len(weights)),
        out_specs=(IN_VMEM, IN_VMEM),
        scratch_shapes=[pltpu.VMEM(mine.shape, BF16)],
        compiler_params=pltpu.CompilerParams(vmem_limit_bytes=32 * 1024 * 1024),
        cost_estimate=pl.CostEstimate(
            flops=8 * rows * columns * 2 * HEAD, bytes_accessed=8 * columns * HEAD, transcendentals=0
        ),
        name="project",
    )(mine, *arrived, *weights)


def gather_cube(block, cube):
    blocks = [block]
    while len(blocks) < cube:
        distance = len(blocks)
        moved = exchange(jnp.stack(blocks), "seq", 2 * cube, distance)
        blocks += [moved[i] for i in range(distance)]
    return jnp.stack(blocks)


def many_cores(text_query, vision_key, vision_value, grad_output, key_weight, value_weight):
    chips = lax.axis_size("seq")
    cores = lax.axis_size("kv")
    cube = chips // 2
    half = cores // 2
    me = lax.axis_index("seq")
    core = lax.axis_index("kv")
    groups = [list(range(cube)), list(range(cube, chips))]
    own = vision_key.shape[0]
    weights = gather_cube(jnp.concatenate([key_weight, value_weight], axis=1), cube)
    pair = jnp.concatenate([vision_key, vision_value], axis=1)
    vision = lax.all_to_all(jnp.broadcast_to(pair, (chips,) + pair.shape), "seq", 0, 0)
    grad_query, terms = attention_terms(
        text_query, grad_output, vision.reshape(chips * own, 2 * HEAD), cube, 2
    )
    arrived = lax.all_to_all(terms, "seq", 0, 0, axis_index_groups=groups)
    partial = jnp.sum(arrived.astype(F32), axis=0)
    grads = (partial + exchange(partial, "seq", chips, cube)).astype(BF16)
    product = jnp.einsum("qtc,drc->qdtr", grads, weights, preferred_element_type=F32)
    place = (me % cube) ^ jnp.arange(cube)
    product = jnp.take(product, place, axis=1)
    columns = product.transpose(0, 2, 1, 3).reshape(2, own, half, -1).transpose(0, 2, 1, 3)
    columns = columns.reshape(cores, own, -1)
    total = lax.dynamic_index_in_dim(columns, core, 0, keepdims=False)
    for d in range(1, cores):
        other = lax.dynamic_index_in_dim(columns, core ^ d, 0, keepdims=False)
        total = total + exchange(other.astype(BF16), "kv", cores, d).astype(F32)
    total = total.astype(BF16)
    routes = [
        (u * cores + j, (u ^ cube) * cores + (j + half) % cores)
        for u in range(chips)
        for j in range(cores)
        if j // half != u // cube
    ]
    received = lax.ppermute(total, ("seq", "kv"), routes)
    grad_vision = jnp.where(core // half == me // cube, total, received)
    return (grad_query, grad_vision)


def two_cores(text_query, vision_key, vision_value, grad_output, key_weight, value_weight):
    chips = lax.axis_size("seq")
    me = lax.axis_index("seq")
    core = lax.axis_index("kv")
    line = 4
    plane = chips // line
    own = vision_key.shape[0]

    pair = jnp.concatenate([vision_key, vision_value], axis=1)
    vision = lax.all_to_all(jnp.broadcast_to(pair, (chips,) + pair.shape), "seq", 0, 0)
    weight = jnp.concatenate([key_weight, value_weight], axis=1)
    weights = [weight] + [exchange(weight, "seq", chips, d) for d in range(1, plane)]
    grad_query, terms = attention_terms(
        text_query, grad_output, vision.reshape(chips * own, 2 * HEAD), plane, line
    )
    terms, weights[1:3] = lax.optimization_barrier((terms, weights[1:3]))
    weights += [exchange(w, "kv", 2, 1) for w in weights]

    groups = [list(range(z * plane, (z + 1) * plane)) for z in range(line)]
    arrived = lax.all_to_all(terms, "seq", 0, 0, axis_index_groups=groups)
    sums = jnp.sum(arrived.astype(F32), axis=0)
    mine = lax.dynamic_slice_in_dim(sums, 2 * core, 2, 0)
    yours = lax.dynamic_slice_in_dim(sums, 2 - 2 * core, 2, 0)
    mine = jnp.concatenate([mine, exchange(yours, "kv", 2, 1)], axis=2)
    near, far, cross = plane, 2 * plane, 3 * plane
    arrived = [exchange(mine.astype(BF16), "seq", chips, d) for d in (near, far, cross)]
    stay, go = project(mine, arrived, weights)

    routes_a, routes_b = [], []
    for u in range(chips):
        home = u // far
        routes_a.append((2 * u + home, 2 * (u ^ near) + home))
        routes_a.append((2 * u + 1 - home, 2 * (u ^ far) + home))
        routes_b.append((2 * u + 1 - home, 2 * (u ^ cross) + home))
    at_home = core == me // far
    first = lax.ppermute(go, ("seq", "kv"), routes_a)
    second = lax.ppermute(stay, ("seq", "kv"), routes_b)
    same = jnp.where(at_home, stay, first)
    other = jnp.where(at_home, first, second)
    upper = (me // near) % 2 == 1
    grad_vision = jnp.concatenate(
        [jnp.where(upper, other, same), jnp.where(upper, same, other)], axis=1
    )
    return (grad_query, grad_vision)


def solution(mesh):
    spec = P("seq", "kv")
    return jax.shard_map(
        two_cores if mesh.shape["kv"] == 2 and mesh.shape["seq"] % 4 == 0 else many_cores,
        mesh=mesh,
        in_specs=(spec,) * 6,
        out_specs=(spec, spec),
        check_vma=False,
    )
```

time: 75.6 us -> 53.6 us (0.71)
  local copies, waits for them, and re-layouts: 15.1 us -> 0.83 us
  matrix products: 7.71 us -> 0 us
  starting transfers between devices: 22.6 us -> 28.8 us
  waiting for transfers between devices: 22.7 us -> 16.8 us
  Pallas kernels: 0 us -> 4.49 us
  other arithmetic: 5.96 us -> 1.52 us
    unnamed x28 -> x9, local copies, waits for them, and re-layouts: 9.36 us -> 0.04 us
    dot_general x6 -> x0, matrix products: 7.71 us -> none  [the longest x1 2.47 us: attention_terms(): jnp.einsum('htk,kd->thd', grad_logits, keys, preferred_element_type=f32)]
    all_to_all x2, waiting for transfers between devices: 13.2 us -> 6.29 us  [the longest x1 5.14 us: two_cores(): lax.all_to_all(jnp.broadcast_to(pair, (chips,) + pair.shape), 'seq', 0, 0)]
    ppermute x6 -> x11, starting transfers between devices: 9.15 us -> 14 us  [exchange(): return lax.ppermute(block, axis, [(i, i ^ distance) for i in range(size)])]
    pallas_call x0 -> x2, Pallas kernels: none -> 4.49 us  [the longest x1 3.74 us: attention_terms(): pl.pallas_call(attention_kernel, out_shape=(jax.ShapeDtypeStruct((rows, w...]
    another operation x3 -> x0, local copies, waits for them, and re-layouts: 2.39 us -> none  [the longest x1 2.29 us: gather_cube(): return jnp.stack(blocks)]
    convert_element_type x2 -> x1, other arithmetic: 1.81 us -> 0.01 us  [two_cores(): mine.astype(BF16)]
    gather x1 -> x0, local copies, waits for them, and re-layouts: 1.59 us -> none  [shards(): product = jnp.take(product, place, axis=1)]
  transfers between devices with their start and end apart: 9 -> 15, of which waited for: 6 -> 7; matrix products, arithmetic and copies ran while one was open for 25% -> 0% of each run, Pallas kernels for 0% -> 7%
where the time goes in v2:
time: 53.6 us; the launch traced here: 53.2 us
  starting transfers between devices  28.8 us (54%)
  waiting for transfers between devices  16.8 us (31%)
  Pallas kernels  4.49 us (8%)
  other arithmetic  1.52 us (3%)
  local copies, waits for them, and re-layouts  0.83 us (2%)
  between operations  0.79 us (1%)
    ppermute x11, starting transfers between devices, exchange(): return lax.ppermute(block, axis, [(i, i ^ distance) for i in range(size)])  14 us
    all_to_all x1, starting transfers between devices, two_cores(): lax.all_to_all(jnp.broadcast_to(pair, (chips,) + pair.shape), 'seq', 0, 0)  7.55 us
    ppermute x11, waiting for transfers between devices, exchange(): return lax.ppermute(block, axis, [(i, i ^ distance) for i in range(size)])  5.67 us
    all_to_all x1, waiting for transfers between devices, two_cores(): lax.all_to_all(jnp.broadcast_to(pair, (chips,) + pair.shape), 'seq', 0, 0)  5.14 us
    pallas_call x1, Pallas kernels, attention_terms(): pl.pallas_call(attention_kernel, out_shape=(jax.ShapeDtypeStruct((rows, w...  3.74 us
    all_to_all x1, starting transfers between devices, two_cores(): arrived = lax.all_to_all(terms, 'seq', 0, 0, axis_index_groups=groups)  3.41 us
    ppermute x1, starting transfers between devices, two_cores(): second = lax.ppermute(stay, ('seq', 'kv'), routes_b)  3.34 us
    ppermute x1, waiting for transfers between devices, two_cores(): first = lax.ppermute(go, ('seq', 'kv'), routes_a)  2.43 us
  transfers between devices with their start and end apart: 15, of which 7 were waited for; matrix products, arithmetic and copies ran while one was open for 0% of the time, Pallas kernels for 7%

profile of v2, /device:TPU:1, one launch (start us, length us, event | category | flops | bytes accessed | tf_op | source)
XLA Modules:
  0.0 53.2 jit_solution(15541227092237815745)
XLA Ops:
  0.6 0.7 %pad_maximum_fusion.2 = bf16[32,256]{1,0:T(8,128)(2,1)S(1)} fusion(bf16[32,128]{1,0:T(8,128)(2,1)} %param.8, bf16[32,128]{1,0:T(8,128)(2,1)} %param.7), kind=kLoop, calls=%fused_computation.7 | loop fusion | flops 32768 | bytes 32768 | tf_op jit(solution)/shard_map/concatenate | solution.py:185
  1.3 0.7 %broadcast_in_dim.3 = bf16[16,32,256]{2,1,0:T(8,128)(2,1)} broadcast(bf16[32,256]{1,0:T(8,128)(2,1)S(1)} %pad_maximum_fusion.2), dimensions={1,2} | broadcast | bytes 278528 | tf_op jit(solution)/shard_map/broadcast_in_dim | solution.py:186
  2.1 7.5 %all-to-all-start = ((bf16[16,32,256]{2,1,0:T(8,128)(2,1)}), bf16[16,32,256]{2,1,0:T(8,128)(2,1)S(1)}, u32[]{:S(2)}, u32[]{:S(2)}) async-start(bf16[16,32,256]{2,1,0:T(8,128)(2,1)} %broadcast_in_dim.3), calls=%async_computation | async-start | bytes 524288 | tf_op jit(solution)/shard_map/all_to_all | solution.py:186
  9.8 1.4 %collective-permute-start.1 = (bf16[512,256]{1,0:T(8,128)(2,1)S(1)}, bf16[512,256]{1,0:T(8,128)(2,1)S(1)}, u32[]{:S(2)}, u32[]{:S(2)}) collective-permute-start(bf16[512,256]{1,0:T(8,128)(2,1)S(1)} %constant_dynamic-update-slice_fusion.refs_0_), channel_id=1, source_target_pairs={{0,4},{2,6},{4,0},{6,2},{8,12},{10,14},{12,8},{14,10},{16,20},{18,... | collective-permute-start | bytes 786440 | tf_op jit(solution)/shard_map/ppermute | solution.py:20
  11.2 1.2 %collective-permute-start = (bf16[512,256]{1,0:T(8,128)(2,1)S(1)}, bf16[512,256]{1,0:T(8,128)(2,1)S(1)}, u32[]{:S(2)}, u32[]{:S(2)}) collective-permute-start(bf16[512,256]{1,0:T(8,128)(2,1)S(1)} %constant_dynamic-update-slice_fusion.refs_0_), channel_id=1, source_target_pairs={{0,2},{2,0},{4,6},{6,4},{8,10},{10,8},{12,14},{14,12},{16,18},{18,... | collective-permute-start | bytes 786440 | tf_op jit(solution)/shard_map/ppermute | solution.py:20
  12.5 5.1 %all-to-all-done = bf16[16,32,256]{2,1,0:T(8,128)(2,1)S(1)} async-done(((bf16[16,32,256]{2,1,0:T(8,128)(2,1)}), bf16[16,32,256]{2,1,0:T(8,128)(2,1)S(1)}, u32[]{:S(2)}, u32[]{:S(2)}) %all-to-all-start) | async-done | bytes 262176 | tf_op jit(solution)/shard_map/all_to_all | solution.py:186
  17.6 3.7 %attention_terms.1 = (bf16[128,1024]{1,0:T(8,128)(2,1)}, bf16[4,4,32,256]{3,2,1,0:T(8,128)(2,1)}) custom-call(bf16[128,1024]{1,0:T(8,128)(2,1)S(1)} %copy-done, bf16[128,1024]{1,0:T(8,128)(2,1)S(1)} %copy-done.1, bf16[512,256]{1,0:T(8,128)(2,1)S(1)} %bitcast.1), custom_call_target="tpu_custom_call" | custom-call | flops 671088640 | bytes 1310720 | tf_op jit(solution)/shard_map/attention_terms/pallas_call | solution.py:62
  21.4 3.4 %all-to-all-start.1 = ((bf16[4,4,32,256]{3,2,1,0:T(8,128)(2,1)}), bf16[4,4,32,256]{3,2,1,0:T(8,128)(2,1)S(1)}, u32[]{:S(2)}, u32[]{:S(2)}) async-start(bf16[4,4,32,256]{3,2,1,0:T(8,128)(2,1)} %get-tuple-element.11), calls=%async_computation.1 | async-start | bytes 524288 | tf_op jit(solution)/shard_map/all_to_all | solution.py:196
  24.8 2.9 %collective-permute-start.7 = (bf16[512,256]{1,0:T(8,128)(2,1)S(1)}, bf16[512,256]{1,0:T(8,128)(2,1)S(1)}, u32[]{:S(2)}, u32[]{:S(2)}) collective-permute-start(bf16[512,256]{1,0:T(8,128)(2,1)S(1)} %constant_dynamic-update-slice_fusion.refs_0_), channel_id=1, source_target_pairs={{0,1},{1,0},{2,3},{3,2},{4,5},{5,4},{6,7},{7,6},{8,9},{9,8},{10,11... | collective-permute-start | bytes 786440 | tf_op jit(solution)/shard_map/ppermute | solution.py:20
  27.8 1.2 %all-to-all-done.1 = bf16[4,4,32,256]{3,2,1,0:T(8,128)(2,1)S(1)} async-done(((bf16[4,4,32,256]{3,2,1,0:T(8,128)(2,1)}), bf16[4,4,32,256]{3,2,1,0:T(8,128)(2,1)S(1)}, u32[]{:S(2)}, u32[]{:S(2)}) %all-to-all-start.1) | async-done | bytes 262176 | tf_op jit(solution)/shard_map/all_to_all | solution.py:196
  29.0 4.1 %collective-permute-start.2 = (f32[2,32,256]{2,1,0:T(8,128)S(1)}, f32[2,32,256]{2,1,0:T(8,128)S(1)}, u32[]{:S(2)}, u32[]{:S(2)}) collective-permute-start(f32[2,32,256]{2,1,0:T(8,128)S(1)} %get-tuple-element.19), channel_id=1, source_target_pairs={{0,1},{1,0},{2,3},{3,2},{4,5},{5,4},{6,7},{7,6},{8,9},{9,8},{10,11... | collective-permute-start | bytes 196616 | tf_op jit(solution)/shard_map/ppermute | solution.py:20
  33.2 0.4 collective-permute-start.9
  33.6 0.4 collective-permute-done.2
  34.0 1.8 %collective-permute-start.5 = (bf16[2,32,512]{2,1,0:T(8,128)(2,1)S(1)}, bf16[2,32,512]{2,1,0:T(8,128)(2,1)S(1)}, u32[]{:S(2)}, u32[]{:S(2)}) collective-permute-start(bf16[2,32,512]{2,1,0:T(8,128)(2,1)S(1)} %fusion), channel_id=1, source_target_pairs={{0,24},{2,26},{4,28},{6,30},{8,16},{10,18},{12,20},{14,22},{16,8},... | collective-permute-start | bytes 196616 | tf_op jit(solution)/shard_map/ppermute | solution.py:20
  35.9 0.3 collective-permute-start.4
  36.2 1.5 %collective-permute-start.3 = (bf16[2,32,512]{2,1,0:T(8,128)(2,1)S(1)}, bf16[2,32,512]{2,1,0:T(8,128)(2,1)S(1)}, u32[]{:S(2)}, u32[]{:S(2)}) collective-permute-start(bf16[2,32,512]{2,1,0:T(8,128)(2,1)S(1)} %fusion), channel_id=1, source_target_pairs={{0,8},{2,10},{4,12},{6,14},{8,0},{10,2},{12,4},{14,6},{16,24},{18,... | collective-permute-start | bytes 196616 | tf_op jit(solution)/shard_map/ppermute | solution.py:20
  37.7 1.5 %collective-permute-done.5.cross_ref = bf16[2,32,512]{2,1,0:T(8,128)(2,1)S(1)} collective-permute-done((bf16[2,32,512]{2,1,0:T(8,128)(2,1)S(1)}, bf16[2,32,512]{2,1,0:T(8,128)(2,1)S(1)}, u32[]{:S(2)}, u32[]{:S(2)}) %collective-permute-start.5) | collective-permute-done | bytes 65568 | tf_op jit(solution)/shard_map/ppermute | solution.py:20
  39.2 3.8 %collective-permute-done.4.far_ref = bf16[2,32,512]{2,1,0:T(8,128)(2,1)S(1)} collective-permute-done((bf16[2,32,512]{2,1,0:T(8,128)(2,1)S(1)}, bf16[2,32,512]{2,1,0:T(8,128)(2,1)S(1)}, u32[]{:S(2)}, u32[]{:S(2)}) %collective-permute-start.4) | collective-permute-done | bytes 65568 | tf_op jit(solution)/shard_map/ppermute | solution.py:20
  42.9 0.8 %project.1 = (bf16[32,2048]{1,0:T(8,128)(2,1)S(1)}, bf16[32,2048]{1,0:T(8,128)(2,1)S(1)}) custom-call(f32[2,32,512]{2,1,0:T(8,128)S(1)} %pad_maximum_fusion.1.mine_ref, bf16[2,32,512]{2,1,0:T(8,128)(2,1)S(1)} %collective-permute-done.3.near_ref, bf16[2,32,512]{2,1,0:T(8,128)(2,1)S(1)} %collective-permute-done.4.far_ref, ...), custom_call_target="tpu_custom_call" | custom-call | flops 134217728 | bytes 2097152 | tf_op jit(solution)/shard_map/project/pallas_call | solution.py:115
  43.7 0.5 %collective-permute-start.11 = (bf16[32,2048]{1,0:T(8,128)(2,1)S(1)}, bf16[32,2048]{1,0:T(8,128)(2,1)S(1)}, u32[]{:S(2)}, u32[]{:S(2)}) collective-permute-start(bf16[32,2048]{1,0:T(8,128)(2,1)S(1)} %get-tuple-element.14), channel_id=1, source_target_pairs={{0,8},{1,16},{2,10},{3,18},{4,12},{5,20},{6,14},{7,22},{8,0},{9,24... | collective-permute-start | bytes 393224 | tf_op jit(solution)/shard_map/ppermute | solution.py:212
  44.2 3.3 %collective-permute-start.12 = (bf16[32,2048]{1,0:T(8,128)(2,1)S(1)}, bf16[32,2048]{1,0:T(8,128)(2,1)S(1)}, u32[]{:S(2)}, u32[]{:S(2)}) collective-permute-start(bf16[32,2048]{1,0:T(8,128)(2,1)S(1)} %get-tuple-element.15), channel_id=1, source_target_pairs={{1,24},{3,26},{5,28},{7,30},{9,16},{11,18},{13,20},{15,22},{16,9},... | collective-permute-start | bytes 393224 | tf_op jit(solution)/shard_map/ppermute | solution.py:213
  47.6 2.4 %collective-permute-done.11 = bf16[32,2048]{1,0:T(8,128)(2,1)S(1)} collective-permute-done((bf16[32,2048]{1,0:T(8,128)(2,1)S(1)}, bf16[32,2048]{1,0:T(8,128)(2,1)S(1)}, u32[]{:S(2)}, u32[]{:S(2)}) %collective-permute-start.11) | collective-permute-done | bytes 131104 | tf_op jit(solution)/shard_map/ppermute | solution.py:212
  50.1 2.4 %collective-permute-done.12 = bf16[32,2048]{1,0:T(8,128)(2,1)S(1)} collective-permute-done((bf16[32,2048]{1,0:T(8,128)(2,1)S(1)}, bf16[32,2048]{1,0:T(8,128)(2,1)S(1)}, u32[]{:S(2)}, u32[]{:S(2)}) %collective-permute-start.12) | collective-permute-done | bytes 131104 | tf_op jit(solution)/shard_map/ppermute | solution.py:213
  52.5 0.7 %pad_maximum_fusion = bf16[32,4096]{1,0:T(8,128)(2,1)} fusion(bf16[32,2048]{1,0:T(8,128)(2,1)S(1)} %get-tuple-element.17, bf16[32,2048]{1,0:T(8,128)(2,1)S(1)} %get-tuple-element.16), kind=kLoop, calls=%fused_computation.1 | loop fusion | flops 524288 | bytes 524288 | tf_op jit(solution)/shard_map/concatenate | solution.py:217
  (26 shorter events, 0.5 us)
Async XLA Ops:
  2.1 7.6 %copy-start.2 = (bf16[512,128]{1,0:T(8,128)(2,1)S(1)}, bf16[512,128]{1,0:T(8,128)(2,1)}, u32[]{:S(2)}) copy-start(bf16[512,128]{1,0:T(8,128)(2,1)} %param.10) | copy-start | bytes 393220
  2.1 7.6 %copy-start.3 = (bf16[512,128]{1,0:T(8,128)(2,1)S(1)}, bf16[512,128]{1,0:T(8,128)(2,1)}, u32[]{:S(2)}) copy-start(bf16[512,128]{1,0:T(8,128)(2,1)} %param.11) | copy-start | bytes 393220
  2.1 15.5 %all-to-all-start = ((bf16[16,32,256]{2,1,0:T(8,128)(2,1)}), bf16[16,32,256]{2,1,0:T(8,128)(2,1)S(1)}, u32[]{:S(2)}, u32[]{:S(2)}) async-start(bf16[16,32,256]{2,1,0:T(8,128)(2,1)} %broadcast_in_dim.3), calls=%async_computation | async-start | bytes 524288 | tf_op jit(solution)/shard_map/all_to_all | solution.py:186
  9.6 8.0 %copy-start = (bf16[128,1024]{1,0:T(8,128)(2,1)S(1)}, bf16[128,1024]{1,0:T(8,128)(2,1)}, u32[]{:S(2)}) copy-start(bf16[128,1024]{1,0:T(8,128)(2,1)} %queries_ref.1) | copy-start | bytes 786436
  9.7 8.0 %copy-start.1 = (bf16[128,1024]{1,0:T(8,128)(2,1)S(1)}, bf16[128,1024]{1,0:T(8,128)(2,1)}, u32[]{:S(2)}) copy-start(bf16[128,1024]{1,0:T(8,128)(2,1)} %upstream_ref.1) | copy-start | bytes 786436
  9.8 11.6 %collective-permute-start.1 = (bf16[512,256]{1,0:T(8,128)(2,1)S(1)}, bf16[512,256]{1,0:T(8,128)(2,1)S(1)}, u32[]{:S(2)}, u32[]{:S(2)}) collective-permute-start(bf16[512,256]{1,0:T(8,128)(2,1)S(1)} %constant_dynamic-update-slice_fusion.refs_0_), channel_id=1, source_target_pairs={{0,4},{2,6},{4,0},{6,2},{8,12},{10,14},{12,8},{14,10},{16,20},{18,... | collective-permute-start | bytes 786440 | tf_op jit(solution)/shard_map/ppermute | solution.py:20
  11.2 10.2 %collective-permute-start = (bf16[512,256]{1,0:T(8,128)(2,1)S(1)}, bf16[512,256]{1,0:T(8,128)(2,1)S(1)}, u32[]{:S(2)}, u32[]{:S(2)}) collective-permute-start(bf16[512,256]{1,0:T(8,128)(2,1)S(1)} %constant_dynamic-update-slice_fusion.refs_0_), channel_id=1, source_target_pairs={{0,2},{2,0},{4,6},{6,4},{8,10},{10,8},{12,14},{14,12},{16,18},{18,... | collective-permute-start | bytes 786440 | tf_op jit(solution)/shard_map/ppermute | solution.py:20
  12.4 15.4 %collective-permute-start.6 = (bf16[512,256]{1,0:T(8,128)(2,1)S(1)}, bf16[512,256]{1,0:T(8,128)(2,1)S(1)}, u32[]{:S(2)}, u32[]{:S(2)}) collective-permute-start(bf16[512,256]{1,0:T(8,128)(2,1)S(1)} %constant_dynamic-update-slice_fusion.refs_0_), channel_id=1, source_target_pairs={{0,6},{2,4},{4,2},{6,0},{8,14},{10,12},{12,10},{14,8},{16,22},{18,... | collective-permute-start | bytes 786440 | tf_op jit(solution)/shard_map/ppermute | solution.py:20
  21.4 7.6 %all-to-all-start.1 = ((bf16[4,4,32,256]{3,2,1,0:T(8,128)(2,1)}), bf16[4,4,32,256]{3,2,1,0:T(8,128)(2,1)S(1)}, u32[]{:S(2)}, u32[]{:S(2)}) async-start(bf16[4,4,32,256]{3,2,1,0:T(8,128)(2,1)} %get-tuple-element.11), calls=%async_computation.1 | async-start | bytes 524288 | tf_op jit(solution)/shard_map/all_to_all | solution.py:196
  24.8 11.1 %collective-permute-start.7 = (bf16[512,256]{1,0:T(8,128)(2,1)S(1)}, bf16[512,256]{1,0:T(8,128)(2,1)S(1)}, u32[]{:S(2)}, u32[]{:S(2)}) collective-permute-start(bf16[512,256]{1,0:T(8,128)(2,1)S(1)} %constant_dynamic-update-slice_fusion.refs_0_), channel_id=1, source_target_pairs={{0,1},{1,0},{2,3},{3,2},{4,5},{5,4},{6,7},{7,6},{8,9},{9,8},{10,11... | collective-permute-start | bytes 786440 | tf_op jit(solution)/shard_map/ppermute | solution.py:20
  27.7 8.5 %collective-permute-start.10 = (bf16[512,256]{1,0:T(8,128)(2,1)S(1)}, bf16[512,256]{1,0:T(8,128)(2,1)S(1)}, u32[]{:S(2)}, u32[]{:S(2)}) collective-permute-start(bf16[512,256]{1,0:T(8,128)(2,1)S(1)} %collective-permute-done.6.refs_3_), channel_id=1, source_target_pairs={{0,1},{1,0},{2,3},{3,2},{4,5},{5,4},{6,7},{7,6},{8,9},{9,8},{10,11... | collective-permute-start | bytes 786440 | tf_op jit(solution)/shard_map/ppermute | solution.py:20
  29.0 5.0 %collective-permute-start.2 = (f32[2,32,256]{2,1,0:T(8,128)S(1)}, f32[2,32,256]{2,1,0:T(8,128)S(1)}, u32[]{:S(2)}, u32[]{:S(2)}) collective-permute-start(f32[2,32,256]{2,1,0:T(8,128)S(1)} %get-tuple-element.19), channel_id=1, source_target_pairs={{0,1},{1,0},{2,3},{3,2},{4,5},{5,4},{6,7},{7,6},{8,9},{9,8},{10,11... | collective-permute-start | bytes 196616 | tf_op jit(solution)/shard_map/ppermute | solution.py:20
  33.1 4.6 %collective-permute-start.8 = (bf16[512,256]{1,0:T(8,128)(2,1)S(1)}, bf16[512,256]{1,0:T(8,128)(2,1)S(1)}, u32[]{:S(2)}, u32[]{:S(2)}) collective-permute-start(bf16[512,256]{1,0:T(8,128)(2,1)S(1)} %collective-permute-done.refs_1_), channel_id=1, source_target_pairs={{0,1},{1,0},{2,3},{3,2},{4,5},{5,4},{6,7},{7,6},{8,9},{9,8},{10,11... | collective-permute-start | bytes 786440 | tf_op jit(solution)/shard_map/ppermute | solution.py:20
  33.2 4.5 %collective-permute-start.9 = (bf16[512,256]{1,0:T(8,128)(2,1)S(1)}, bf16[512,256]{1,0:T(8,128)(2,1)S(1)}, u32[]{:S(2)}, u32[]{:S(2)}) collective-permute-start(bf16[512,256]{1,0:T(8,128)(2,1)S(1)} %collective-permute-done.1.refs_2_), channel_id=1, source_target_pairs={{0,1},{1,0},{2,3},{3,2},{4,5},{5,4},{6,7},{7,6},{8,9},{9,8},{10,11... | collective-permute-start | bytes 786440 | tf_op jit(solution)/shard_map/ppermute | solution.py:20
  34.0 5.1 %collective-permute-start.5 = (bf16[2,32,512]{2,1,0:T(8,128)(2,1)S(1)}, bf16[2,32,512]{2,1,0:T(8,128)(2,1)S(1)}, u32[]{:S(2)}, u32[]{:S(2)}) collective-permute-start(bf16[2,32,512]{2,1,0:T(8,128)(2,1)S(1)} %fusion), channel_id=1, source_target_pairs={{0,24},{2,26},{4,28},{6,30},{8,16},{10,18},{12,20},{14,22},{16,8},... | collective-permute-start | bytes 196616 | tf_op jit(solution)/shard_map/ppermute | solution.py:20
  35.9 7.1 %collective-permute-start.4 = (bf16[2,32,512]{2,1,0:T(8,128)(2,1)S(1)}, bf16[2,32,512]{2,1,0:T(8,128)(2,1)S(1)}, u32[]{:S(2)}, u32[]{:S(2)}) collective-permute-start(bf16[2,32,512]{2,1,0:T(8,128)(2,1)S(1)} %fusion), channel_id=1, source_target_pairs={{0,16},{2,18},{4,20},{6,22},{8,24},{10,26},{12,28},{14,30},{16,0},... | collective-permute-start | bytes 196616 | tf_op jit(solution)/shard_map/ppermute | solution.py:20
  36.2 6.7 %collective-permute-start.3 = (bf16[2,32,512]{2,1,0:T(8,128)(2,1)S(1)}, bf16[2,32,512]{2,1,0:T(8,128)(2,1)S(1)}, u32[]{:S(2)}, u32[]{:S(2)}) collective-permute-start(bf16[2,32,512]{2,1,0:T(8,128)(2,1)S(1)} %fusion), channel_id=1, source_target_pairs={{0,8},{2,10},{4,12},{6,14},{8,0},{10,2},{12,4},{14,6},{16,24},{18,... | collective-permute-start | bytes 196616 | tf_op jit(solution)/shard_map/ppermute | solution.py:20
  43.7 6.4 %collective-permute-start.11 = (bf16[32,2048]{1,0:T(8,128)(2,1)S(1)}, bf16[32,2048]{1,0:T(8,128)(2,1)S(1)}, u32[]{:S(2)}, u32[]{:S(2)}) collective-permute-start(bf16[32,2048]{1,0:T(8,128)(2,1)S(1)} %get-tuple-element.14), channel_id=1, source_target_pairs={{0,8},{1,16},{2,10},{3,18},{4,12},{5,20},{6,14},{7,22},{8,0},{9,24... | collective-permute-start | bytes 393224 | tf_op jit(solution)/shard_map/ppermute | solution.py:212
  44.2 8.2 %collective-permute-start.12 = (bf16[32,2048]{1,0:T(8,128)(2,1)S(1)}, bf16[32,2048]{1,0:T(8,128)(2,1)S(1)}, u32[]{:S(2)}, u32[]{:S(2)}) collective-permute-start(bf16[32,2048]{1,0:T(8,128)(2,1)S(1)} %get-tuple-element.15), channel_id=1, source_target_pairs={{1,24},{3,26},{5,28},{7,30},{9,16},{11,18},{13,20},{15,22},{16,9},... | collective-permute-start | bytes 393224 | tf_op jit(solution)/shard_map/ppermute | solution.py:213

commit v3 on v2

v3 whole, which is shorter than its diff:
```python
import functools
import math

import jax
import jax.numpy as jnp
from jax import lax
from jax.experimental import pallas as pl
from jax.experimental.pallas import tpu as pltpu
from jax.sharding import PartitionSpec as P

HEAD = 128
F32 = jnp.float32
BF16 = jnp.bfloat16
IN_VMEM = pl.BlockSpec(memory_space=pltpu.VMEM)
SIDE_BY_SIDE = (((1,), (1,)), ((), ()))
ON_TOP = (((0,), (0,)), ((), ()))


def exchange(block, axis, size, distance):
    return lax.ppermute(block, axis, [(i, i ^ distance) for i in range(size)])


def spread_kernel(keys_ref, values_ref, out_ref):
    for i in range(out_ref.shape[0]):
        out_ref[i, :, :HEAD] = keys_ref[...]
        out_ref[i, :, HEAD:] = values_ref[...]


def spread(keys, values, copies):
    return pl.pallas_call(
        spread_kernel,
        out_shape=pltpu.VMEM((copies, keys.shape[0], 2 * HEAD), BF16),
        in_specs=[IN_VMEM] * 2,
        out_specs=IN_VMEM,
        name="spread",
    )(keys, values)


def attention_kernel(queries_ref, upstream_ref, vision_ref, low_ref, *refs):
    terms_refs, (rows, low, sums) = refs[:-3], refs[-3:]
    row_count, width = queries_ref.shape
    heads = width // HEAD
    scaling = 1.0 / math.sqrt(HEAD)
    keys = vision_ref[:, :HEAD]
    values = vision_ref[:, HEAD:]
    for h in range(heads):
        lanes = slice(h * HEAD, (h + 1) * HEAD)
        at = slice(h * row_count, (h + 1) * row_count)
        rows[0, at, :] = queries_ref[:, lanes]
        rows[1, at, :] = upstream_ref[:, lanes]
    step = 2 if heads % 2 == 0 else 1
    for h in range(0, heads, step):
        at = slice(h * row_count, (h + step) * row_count)
        logits = lax.dot_general(keys, rows[0, at, :], SIDE_BY_SIDE, preferred_element_type=F32)
        grad_probs = lax.dot_general(values, rows[1, at, :], SIDE_BY_SIDE, preferred_element_type=F32)
        top = jnp.max(logits, axis=0, keepdims=True)
        exponent = jnp.exp2((logits - top) * (scaling * math.log2(math.e)))
        inverse = 1.0 / jnp.sum(exponent, axis=0, keepdims=True)
        row_dots = jnp.sum(exponent * grad_probs, axis=0, keepdims=True) * inverse
        low[:, at] = (exponent * inverse).astype(BF16)
        low_ref[:, at] = (exponent * (grad_probs - row_dots) * (inverse * scaling)).astype(BF16)
    line, plane, own, _ = sums.shape
    for i, factor in enumerate((low_ref, low)):
        term = jnp.dot(factor[...], rows[i], preferred_element_type=F32)
        sums[:, :, :, i * HEAD : (i + 1) * HEAD] = term.reshape(line, plane, own, HEAD)
    spot = lax.rem(lax.axis_index("seq"), plane)
    for d, ref in enumerate(terms_refs):
        ref[...] = sums[:, jnp.bitwise_xor(spot, d)].astype(ref.dtype)


def attention_terms(queries, upstream, vision, plane, line):
    rows, width = queries.shape
    tokens = vision.shape[0]
    pairs = rows * width // HEAD
    own = tokens // (plane * line)
    low, *terms = pl.pallas_call(
        attention_kernel,
        out_shape=[jax.ShapeDtypeStruct((tokens, pairs), BF16)]
        + [
            jax.ShapeDtypeStruct((line, own, 2 * HEAD), BF16 if d else F32) for d in range(plane)
        ],
        in_specs=[IN_VMEM] * 3,
        out_specs=[IN_VMEM] * (1 + plane),
        scratch_shapes=[
            pltpu.VMEM((2, pairs, HEAD), BF16),
            pltpu.VMEM((tokens, pairs), BF16),
            pltpu.VMEM((line, plane, own, 2 * HEAD), F32),
        ],
        compiler_params=pltpu.CompilerParams(vmem_limit_bytes=48 * 1024 * 1024),
        cost_estimate=pl.CostEstimate(
            flops=8 * pairs * tokens * HEAD,
            bytes_accessed=4 * rows * width + 4 * tokens * HEAD,
            transcendentals=pairs * tokens,
        ),
        name="attention_terms",
    )(queries, upstream, vision)
    return low, terms


def query_kernel(low_ref, vision_ref, query_ref):
    rows = query_ref.shape[0]
    keys = vision_ref[:, :HEAD]
    for h in range(query_ref.shape[1] // HEAD):
        at = slice(h * rows, (h + 1) * rows)
        product = lax.dot_general(low_ref[:, at], keys, ON_TOP, preferred_element_type=F32)
        query_ref[:, h * HEAD : (h + 1) * HEAD] = product.astype(BF16)


def query_gradient(low, vision, rows):
    tokens, pairs = low.shape
    return pl.pallas_call(
        query_kernel,
        out_shape=jax.ShapeDtypeStruct((rows, pairs // rows * HEAD), BF16),
        in_specs=[IN_VMEM] * 2,
        out_specs=IN_VMEM,
        compiler_params=pltpu.CompilerParams(vmem_limit_bytes=32 * 1024 * 1024),
        cost_estimate=pl.CostEstimate(
            flops=2 * pairs * tokens * HEAD, bytes_accessed=2 * pairs * HEAD, transcendentals=0
        ),
        name="query_gradient",
    )(low, vision)


def project_kernel(sums_ref, near_ref, far_ref, cross_ref, *refs):
    weights, (keep_ref, send_ref, grads) = refs[:-3], refs[-3:]
    plane = len(weights)
    me = lax.axis_index("seq")
    core = lax.axis_index("kv")
    home = core == me // (2 * plane)
    odd = lax.rem(me // plane, 2)
    spot = lax.rem(me, plane)
    total = sums_ref[...] + near_ref[...].astype(F32) + far_ref[...].astype(F32)
    grads[...] = (total + cross_ref[...].astype(F32)).astype(BF16)
    first = 2 * core + jnp.where(home, odd, 1 - odd)
    second = 2 * core + jnp.where(home, 1 - odd, odd)
    blocks = [grads[i] for i in (first, second, 3 - first, 3 - second)]
    ordered = jnp.concatenate(blocks, axis=0)
    rows = grads.shape[1]
    for d in range(plane):
        product = lax.dot_general(ordered, weights[d][...], SIDE_BY_SIDE, preferred_element_type=F32)
        columns = weights[d].shape[0]
        at = pl.ds(pl.multiple_of(jnp.bitwise_xor(spot, d) * columns, columns), columns)
        for i in range(2):
            keep_ref[i, :, at] = product[i * rows : (i + 1) * rows]
            send_ref[i, :, at] = product[(i + 2) * rows : (i + 3) * rows].astype(BF16)


def project(sums, arrived, weights):
    rows = sums.shape[1]
    plane = len(weights)
    columns = plane * weights[0].shape[0]
    return pl.pallas_call(
        project_kernel,
        out_shape=(
            jax.ShapeDtypeStruct((2, rows, columns), F32),
            jax.ShapeDtypeStruct((2, rows, columns), BF16),
        ),
        in_specs=[IN_VMEM] * (4 + plane),
        out_specs=(IN_VMEM, IN_VMEM),
        scratch_shapes=[pltpu.VMEM(sums.shape, BF16)],
        compiler_params=pltpu.CompilerParams(vmem_limit_bytes=32 * 1024 * 1024),
        cost_estimate=pl.CostEstimate(
            flops=16 * rows * columns * HEAD, bytes_accessed=4 * columns * HEAD, transcendentals=0
        ),
        name="project",
    )(sums, *arrived, *weights)


def gather_cube(block, cube):
    blocks = [block]
    while len(blocks) < cube:
        distance = len(blocks)
        moved = exchange(jnp.stack(blocks), "seq", 2 * cube, distance)
        blocks += [moved[i] for i in range(distance)]
    return jnp.stack(blocks)


def many_cores(text_query, vision_key, vision_value, grad_output, key_weight, value_weight):
    chips = lax.axis_size("seq")
    cores = lax.axis_size("kv")
    cube = chips // 2
    half = cores // 2
    me = lax.axis_index("seq")
    core = lax.axis_index("kv")
    own = vision_key.shape[0]
    weights = gather_cube(jnp.concatenate([key_weight, value_weight], axis=1), cube)
    vision = lax.all_to_all(spread(vision_key, vision_value, chips), "seq", 0, 0)
    vision = vision.reshape(chips * own, 2 * HEAD)
    low, terms = attention_terms(text_query, grad_output, vision, cube, 2)
    grad_query = query_gradient(low, vision, text_query.shape[0])
    partial = terms[0]
    for d in range(1, cube):
        partial = partial + exchange(terms[d], "seq", chips, d).astype(F32)
    grads = (partial + exchange(partial, "seq", chips, cube)).astype(BF16)
    product = jnp.einsum("qtc,drc->qdtr", grads, weights, preferred_element_type=F32)
    place = (me % cube) ^ jnp.arange(cube)
    product = jnp.take(product, place, axis=1)
    columns = product.transpose(0, 2, 1, 3).reshape(2, own, half, -1).transpose(0, 2, 1, 3)
    columns = columns.reshape(cores, own, -1)
    total = lax.dynamic_index_in_dim(columns, core, 0, keepdims=False)
    for d in range(1, cores):
        other = lax.dynamic_index_in_dim(columns, core ^ d, 0, keepdims=False)
        total = total + exchange(other.astype(BF16), "kv", cores, d).astype(F32)
    total = total.astype(BF16)
    routes = [
        (u * cores + j, (u ^ cube) * cores + (j + half) % cores)
        for u in range(chips)
        for j in range(cores)
        if j // half != u // cube
    ]
    received = lax.ppermute(total, ("seq", "kv"), routes)
    grad_vision = jnp.where(core // half == me // cube, total, received)
    return (grad_query, grad_vision)


def two_cores(text_query, vision_key, vision_value, grad_output, key_weight, value_weight):
    chips = lax.axis_size("seq")
    me = lax.axis_index("seq")
    core = lax.axis_index("kv")
    line = 4
    plane = chips // line
    own = vision_key.shape[0]

    vision = lax.all_to_all(spread(vision_key, vision_value, chips), "seq", 0, 0)
    vision = vision.reshape(chips * own, 2 * HEAD)
    weight = jnp.concatenate([key_weight, value_weight], axis=1)
    weights = [weight] + [exchange(weight, "seq", chips, d) for d in (1, 2)]
    low, terms = attention_terms(text_query, grad_output, vision, plane, line)
    terms, weights = lax.optimization_barrier((terms, weights))
    grad_query = query_gradient(low, vision, text_query.shape[0])
    weight, grad_query = lax.optimization_barrier((weights[0], grad_query))
    weights += [exchange(weight, "seq", chips, d) for d in range(3, plane)]

    arrived = [exchange(terms[d], "seq", chips, d) for d in range(1, plane)]
    arrived, grad_query = lax.optimization_barrier((arrived, grad_query))
    sums = terms[0]
    for block in arrived:
        sums = sums + block.astype(F32)
    near, far, cross = plane, 2 * plane, 3 * plane
    arrived = [exchange(sums.astype(BF16), "seq", chips, d) for d in (near, far, cross)]
    keep, send = project(sums, arrived, weights)
    total = (keep + exchange(send, "kv", 2, 1).astype(F32)).astype(BF16)
    stay, go = total[0], total[1]

    routes_a, routes_b = [], []
    for u in range(chips):
        home = u // far
        routes_a.append((2 * u + home, 2 * (u ^ near) + home))
        routes_a.append((2 * u + 1 - home, 2 * (u ^ far) + home))
        routes_b.append((2 * u + 1 - home, 2 * (u ^ cross) + home))
    at_home = core == me // far
    first = lax.ppermute(go, ("seq", "kv"), routes_a)
    second = lax.ppermute(stay, ("seq", "kv"), routes_b)
    same = jnp.where(at_home, stay, first)
    other = jnp.where(at_home, first, second)
    upper = (me // near) % 2 == 1
    grad_vision = jnp.concatenate(
        [jnp.where(upper, other, same), jnp.where(upper, same, other)], axis=1
    )
    return (grad_query, grad_vision)


def solution(mesh):
    spec = P("seq", "kv")
    return jax.shard_map(
        two_cores if mesh.shape["kv"] == 2 and mesh.shape["seq"] % 4 == 0 else many_cores,
        mesh=mesh,
        in_specs=(spec,) * 6,
        out_specs=(spec, spec),
        check_vma=False,
    )
```

time: 53.6 us -> 51.5 us (0.961)
  starting transfers between devices: 28.8 us -> 25.6 us
  waiting for transfers between devices: 16.8 us -> 18.3 us
  Pallas kernels: 4.49 us -> 5.37 us
  local copies, waits for them, and re-layouts: 0.83 us -> 0.1 us
  other arithmetic: 1.52 us -> 0.83 us
    all_to_all x2 -> x1, starting transfers between devices: 11 us -> 7.55 us  [two_cores(): lax.all_to_all(spread(vision_key, vision_value, chips), 'seq', 0, 0)]
    ppermute x11 -> x10, waiting for transfers between devices: 5.67 us -> 7.43 us  [exchange(): return lax.ppermute(block, axis, [(i, i ^ distance) for i in range(size)])]
    all_to_all x2 -> x1, waiting for transfers between devices: 6.29 us -> 5.24 us  [two_cores(): lax.all_to_all(spread(vision_key, vision_value, chips), 'seq', 0, 0)]
    pallas_call x2 -> x4, Pallas kernels: 4.49 us -> 5.37 us  [the longest x1 2.23 us: attention_terms(): pl.pallas_call(attention_kernel, out_shape=[jax.ShapeDtypeStruct((tokens,...]
    ppermute x1, starting transfers between devices: 3.34 us -> 2.5 us  [two_cores(): second = lax.ppermute(stay, ('seq', 'kv'), routes_b)]
    broadcast_in_dim x1 -> x0, local copies, waits for them, and re-layouts: 0.73 us -> none  [two_cores(): jnp.broadcast_to(pair, (chips,) + pair.shape)]
    ppermute x11 -> x10, starting transfers between devices: 14 us -> 14.7 us  [exchange(): return lax.ppermute(block, axis, [(i, i ^ distance) for i in range(size)])]
    concatenate x2 -> x0, other arithmetic: 0.73 us -> none  [the longest x1 0.72 us: two_cores(): pair = jnp.concatenate([vision_key, vision_value], axis=1)]
  transfers between devices with their start and end apart: 15 -> 13, of which waited for: 7 -> 8; matrix products, arithmetic and copies ran while one was open for 0% -> 0% of each run, Pallas kernels for 7% -> 7%
where the time goes in v3:
time: 51.5 us; the launch traced here: 51 us
  starting transfers between devices  25.6 us (50%)
  waiting for transfers between devices  18.3 us (36%)
  Pallas kernels  5.37 us (10%)
  other arithmetic  0.83 us (2%)
  between operations  0.79 us (2%)
    ppermute x10, starting transfers between devices, exchange(): return lax.ppermute(block, axis, [(i, i ^ distance) for i in range(size)])  14.7 us
    all_to_all x1, starting transfers between devices, two_cores(): lax.all_to_all(spread(vision_key, vision_value, chips), 'seq', 0, 0)  7.55 us
    ppermute x10, waiting for transfers between devices, exchange(): return lax.ppermute(block, axis, [(i, i ^ distance) for i in range(size)])  7.43 us
    all_to_all x1, waiting for transfers between devices, two_cores(): lax.all_to_all(spread(vision_key, vision_value, chips), 'seq', 0, 0)  5.24 us
    ppermute x1, waiting for transfers between devices, two_cores(): second = lax.ppermute(stay, ('seq', 'kv'), routes_b)  2.96 us
    ppermute x1, waiting for transfers between devices, two_cores(): first = lax.ppermute(go, ('seq', 'kv'), routes_a)  2.67 us
    ppermute x1, starting transfers between devices, two_cores(): second = lax.ppermute(stay, ('seq', 'kv'), routes_b)  2.5 us
    pallas_call x1, Pallas kernels, attention_terms(): pl.pallas_call(attention_kernel, out_shape=[jax.ShapeDtypeStruct((tokens,...  2.23 us
  transfers between devices with their start and end apart: 13, of which 8 were waited for; matrix products, arithmetic and copies ran while one was open for 0% of the time, Pallas kernels for 7%

profile of v3, /device:TPU:1, one launch (start us, length us, event | category | flops | bytes accessed | tf_op | source)
XLA Modules:
  0.0 51.0 jit_solution(3202301027335289462)
XLA Ops:
  0.6 1.5 %spread.1 = bf16[16,32,256]{2,1,0:T(8,128)(2,1)} custom-call(bf16[32,128]{1,0:T(8,128)(2,1)} %keys_ref.1, bf16[32,128]{1,0:T(8,128)(2,1)} %values_ref.1), custom_call_target="tpu_custom_call" | custom-call | tf_op jit(solution)/shard_map/spread/pallas_call | solution.py:30
  2.1 7.5 %all-to-all-start = ((bf16[16,32,256]{2,1,0:T(8,128)(2,1)}), bf16[16,32,256]{2,1,0:T(8,128)(2,1)S(1)}, u32[]{:S(2)}, u32[]{:S(2)}) async-start(bf16[16,32,256]{2,1,0:T(8,128)(2,1)} %spread.1), calls=%async_computation | async-start | bytes 524288 | tf_op jit(solution)/shard_map/all_to_all | solution.py:224
  9.8 1.4 %collective-permute-start = (bf16[512,256]{1,0:T(8,128)(2,1)S(1)}, bf16[512,256]{1,0:T(8,128)(2,1)S(1)}, u32[]{:S(2)}, u32[]{:S(2)}) collective-permute-start(bf16[512,256]{1,0:T(8,128)(2,1)S(1)} %constant_dynamic-update-slice_fusion.refs_0_), channel_id=1, source_target_pairs={{0,2},{2,0},{4,6},{6,4},{8,10},{10,8},{12,14},{14,12},{16,18},{18,... | collective-permute-start | bytes 786440 | tf_op jit(solution)/shard_map/ppermute | solution.py:20
  11.2 1.2 %collective-permute-start.1 = (bf16[512,256]{1,0:T(8,128)(2,1)S(1)}, bf16[512,256]{1,0:T(8,128)(2,1)S(1)}, u32[]{:S(2)}, u32[]{:S(2)}) collective-permute-start(bf16[512,256]{1,0:T(8,128)(2,1)S(1)} %constant_dynamic-update-slice_fusion.refs_0_), channel_id=1, source_target_pairs={{0,4},{2,6},{4,0},{6,2},{8,12},{10,14},{12,8},{14,10},{16,20},{18,... | collective-permute-start | bytes 786440 | tf_op jit(solution)/shard_map/ppermute | solution.py:20
  12.4 5.2 %all-to-all-done = bf16[16,32,256]{2,1,0:T(8,128)(2,1)S(1)} async-done(((bf16[16,32,256]{2,1,0:T(8,128)(2,1)}), bf16[16,32,256]{2,1,0:T(8,128)(2,1)S(1)}, u32[]{:S(2)}, u32[]{:S(2)}) %all-to-all-start) | async-done | bytes 262176 | tf_op jit(solution)/shard_map/all_to_all | solution.py:224
  17.6 2.2 %attention_terms.1 = (bf16[512,1024]{1,0:T(8,128)(2,1)S(1)}, f32[4,32,256]{2,1,0:T(8,128)S(1)}, bf16[4,32,256]{2,1,0:T(8,128)(2,1)S(1)}, bf16[4,32,256]{2,1,0:T(8,128)(2,1)S(1)}, bf16[4,32,256]{2,1,0:T(8,128)(2,1)S(1)}) custom-call(bf16[128,1024]{1,0:T(8,128)(2,1)S(1)} %copy-done, bf16[128,1024]{1,0:T(8,128)(2,1)S(1)} %copy-done.1, bf16[512,256]{1,0:T(8,128)(2,1)S(1)} %bitcast.9), custom_call_target="tpu_custom_call" | custom-call | flops 536870912 | bytes 786432 | tf_op jit(solution)/shard_map/attention_terms/pallas_call | solution.py:76
  19.9 0.7 %collective-permute-done.1.refs_2_ = bf16[512,256]{1,0:T(8,128)(2,1)S(1)} collective-permute-done((bf16[512,256]{1,0:T(8,128)(2,1)S(1)}, bf16[512,256]{1,0:T(8,128)(2,1)S(1)}, u32[]{:S(2)}, u32[]{:S(2)}) %collective-permute-start.1) | collective-permute-done | bytes 262176 | tf_op jit(solution)/shard_map/ppermute | solution.py:20
  20.6 0.8 %collective-permute-start.2 = (bf16[4,32,256]{2,1,0:T(8,128)(2,1)S(1)}, bf16[4,32,256]{2,1,0:T(8,128)(2,1)S(1)}, u32[]{:S(2)}, u32[]{:S(2)}) collective-permute-start(bf16[4,32,256]{2,1,0:T(8,128)(2,1)S(1)} %get-tuple-element.26), channel_id=1, source_target_pairs={{0,2},{2,0},{4,6},{6,4},{8,10},{10,8},{12,14},{14,12},{16,18},{18,... | collective-permute-start | bytes 196616 | tf_op jit(solution)/shard_map/ppermute | solution.py:20
  21.4 0.9 %collective-permute-start.3 = (bf16[4,32,256]{2,1,0:T(8,128)(2,1)S(1)}, bf16[4,32,256]{2,1,0:T(8,128)(2,1)S(1)}, u32[]{:S(2)}, u32[]{:S(2)}) collective-permute-start(bf16[4,32,256]{2,1,0:T(8,128)(2,1)S(1)} %get-tuple-element.27), channel_id=1, source_target_pairs={{0,4},{2,6},{4,0},{6,2},{8,12},{10,14},{12,8},{14,10},{16,20},{18,... | collective-permute-start | bytes 196616 | tf_op jit(solution)/shard_map/ppermute | solution.py:20
  22.3 0.9 %collective-permute-start.4 = (bf16[4,32,256]{2,1,0:T(8,128)(2,1)S(1)}, bf16[4,32,256]{2,1,0:T(8,128)(2,1)S(1)}, u32[]{:S(2)}, u32[]{:S(2)}) collective-permute-start(bf16[4,32,256]{2,1,0:T(8,128)(2,1)S(1)} %get-tuple-element.28), channel_id=1, source_target_pairs={{0,6},{2,4},{4,2},{6,0},{8,14},{10,12},{12,10},{14,8},{16,22},{18,... | collective-permute-start | bytes 196616 | tf_op jit(solution)/shard_map/ppermute | solution.py:20
  23.2 1.2 %query_gradient.1 = bf16[128,1024]{1,0:T(8,128)(2,1)} custom-call(bf16[512,1024]{1,0:T(8,128)(2,1)S(1)} %get-tuple-element.30.low_ref, bf16[512,256]{1,0:T(8,128)(2,1)S(1)} %bitcast.10), custom_call_target="tpu_custom_call" | custom-call | flops 134217728 | bytes 262144 | tf_op jit(solution)/shard_map/query_gradient/pallas_call | solution.py:111
  24.5 1.4 %collective-permute-start.8 = (bf16[512,256]{1,0:T(8,128)(2,1)S(1)}, bf16[512,256]{1,0:T(8,128)(2,1)S(1)}, u32[]{:S(2)}, u32[]{:S(2)}) collective-permute-start(bf16[512,256]{1,0:T(8,128)(2,1)S(1)} %constant_dynamic-update-slice_fusion.refs_0_), channel_id=1, source_target_pairs={{0,6},{2,4},{4,2},{6,0},{8,14},{10,12},{12,10},{14,8},{16,22},{18,... | collective-permute-start | bytes 786440 | tf_op jit(solution)/shard_map/ppermute | solution.py:20
  25.9 0.7 %collective-permute-done.4 = bf16[4,32,256]{2,1,0:T(8,128)(2,1)S(1)} collective-permute-done((bf16[4,32,256]{2,1,0:T(8,128)(2,1)S(1)}, bf16[4,32,256]{2,1,0:T(8,128)(2,1)S(1)}, u32[]{:S(2)}, u32[]{:S(2)}) %collective-permute-start.4) | collective-permute-done | bytes 65568 | tf_op jit(solution)/shard_map/ppermute | solution.py:20
  26.6 1.1 %collective-permute-start.5 = (bf16[4,32,256]{2,1,0:T(8,128)(2,1)S(1)}, bf16[4,32,256]{2,1,0:T(8,128)(2,1)S(1)}, u32[]{:S(2)}, u32[]{:S(2)}) collective-permute-start(bf16[4,32,256]{2,1,0:T(8,128)(2,1)S(1)} %get-tuple-element.42), channel_id=1, source_target_pairs={{0,8},{2,10},{4,12},{6,14},{8,0},{10,2},{12,4},{14,6},{16,24},{18,... | collective-permute-start | bytes 196616 | tf_op jit(solution)/shard_map/ppermute | solution.py:20
  27.7 2.3 %collective-permute-start.6 = (bf16[4,32,256]{2,1,0:T(8,128)(2,1)S(1)}, bf16[4,32,256]{2,1,0:T(8,128)(2,1)S(1)}, u32[]{:S(2)}, u32[]{:S(2)}) collective-permute-start(bf16[4,32,256]{2,1,0:T(8,128)(2,1)S(1)} %get-tuple-element.42), channel_id=1, source_target_pairs={{0,16},{2,18},{4,20},{6,22},{8,24},{10,26},{12,28},{14,30},{16,0},... | collective-permute-start | bytes 196616 | tf_op jit(solution)/shard_map/ppermute | solution.py:20
  30.2 1.8 %collective-permute-done.6.far_ref = bf16[4,32,256]{2,1,0:T(8,128)(2,1)S(1)} collective-permute-done((bf16[4,32,256]{2,1,0:T(8,128)(2,1)S(1)}, bf16[4,32,256]{2,1,0:T(8,128)(2,1)S(1)}, u32[]{:S(2)}, u32[]{:S(2)}) %collective-permute-start.6) | collective-permute-done | bytes 65568 | tf_op jit(solution)/shard_map/ppermute | solution.py:20
  32.0 3.1 %collective-permute-done.7.cross_ref = bf16[4,32,256]{2,1,0:T(8,128)(2,1)S(1)} collective-permute-done((bf16[4,32,256]{2,1,0:T(8,128)(2,1)S(1)}, bf16[4,32,256]{2,1,0:T(8,128)(2,1)S(1)}, u32[]{:S(2)}, u32[]{:S(2)}) %collective-permute-start.7) | collective-permute-done | bytes 65568 | tf_op jit(solution)/shard_map/ppermute | solution.py:20
  35.6 4.4 %collective-permute-start.9 = (bf16[2,32,2048]{2,1,0:T(8,128)(2,1)S(1)}, bf16[2,32,2048]{2,1,0:T(8,128)(2,1)S(1)}, u32[]{:S(2)}, u32[]{:S(2)}) collective-permute-start(bf16[2,32,2048]{2,1,0:T(8,128)(2,1)S(1)} %get-tuple-element.41), channel_id=1, source_target_pairs={{0,1},{1,0},{2,3},{3,2},{4,5},{5,4},{6,7},{7,6},{8,9},{9,8},{10,11... | collective-permute-start | bytes 786440 | tf_op jit(solution)/shard_map/ppermute | solution.py:20
  39.9 1.2 %collective-permute-done.9 = bf16[2,32,2048]{2,1,0:T(8,128)(2,1)S(1)} collective-permute-done((bf16[2,32,2048]{2,1,0:T(8,128)(2,1)S(1)}, bf16[2,32,2048]{2,1,0:T(8,128)(2,1)S(1)}, u32[]{:S(2)}, u32[]{:S(2)}) %collective-permute-start.9) | collective-permute-done | bytes 262176 | tf_op jit(solution)/shard_map/ppermute | solution.py:20
  41.2 0.9 %collective-permute-start.10 = (bf16[32,2048]{1,0:T(8,128)(2,1)S(1)}, bf16[32,2048]{1,0:T(8,128)(2,1)S(1)}, u32[]{:S(2)}, u32[]{:S(2)}) collective-permute-start(bf16[32,2048]{1,0:T(8,128)(2,1)S(1)} %get-tuple-element.47), channel_id=1, source_target_pairs={{0,8},{1,16},{2,10},{3,18},{4,12},{5,20},{6,14},{7,22},{8,0},{9,24... | collective-permute-start | bytes 393224 | tf_op jit(solution)/shard_map/ppermute | solution.py:252
  42.1 2.5 %collective-permute-start.11 = (bf16[32,2048]{1,0:T(8,128)(2,1)S(1)}, bf16[32,2048]{1,0:T(8,128)(2,1)S(1)}, u32[]{:S(2)}, u32[]{:S(2)}) collective-permute-start(bf16[32,2048]{1,0:T(8,128)(2,1)S(1)} %get-tuple-element.46), channel_id=1, source_target_pairs={{1,24},{3,26},{5,28},{7,30},{9,16},{11,18},{13,20},{15,22},{16,9},... | collective-permute-start | bytes 393224 | tf_op jit(solution)/shard_map/ppermute | solution.py:253
  44.7 2.7 %collective-permute-done.10 = bf16[32,2048]{1,0:T(8,128)(2,1)S(1)} collective-permute-done((bf16[32,2048]{1,0:T(8,128)(2,1)S(1)}, bf16[32,2048]{1,0:T(8,128)(2,1)S(1)}, u32[]{:S(2)}, u32[]{:S(2)}) %collective-permute-start.10) | collective-permute-done | bytes 131104 | tf_op jit(solution)/shard_map/ppermute | solution.py:252
  47.3 3.0 %collective-permute-done.11 = bf16[32,2048]{1,0:T(8,128)(2,1)S(1)} collective-permute-done((bf16[32,2048]{1,0:T(8,128)(2,1)S(1)}, bf16[32,2048]{1,0:T(8,128)(2,1)S(1)}, u32[]{:S(2)}, u32[]{:S(2)}) %collective-permute-start.11) | collective-permute-done | bytes 131104 | tf_op jit(solution)/shard_map/ppermute | solution.py:253
  50.3 0.7 %pad_maximum_fusion = bf16[32,4096]{1,0:T(8,128)(2,1)} fusion(bf16[32,2048]{1,0:T(8,128)(2,1)S(1)} %get-tuple-element.45, bf16[32,2048]{1,0:T(8,128)(2,1)S(1)} %get-tuple-element.44), kind=kLoop, calls=%fused_computation.1 | loop fusion | flops 524288 | bytes 524288 | tf_op jit(solution)/shard_map/concatenate | solution.py:257
  (21 shorter events, 1.0 us)
Async XLA Ops:
  2.1 7.6 %copy-start.2 = (bf16[512,128]{1,0:T(8,128)(2,1)S(1)}, bf16[512,128]{1,0:T(8,128)(2,1)}, u32[]{:S(2)}) copy-start(bf16[512,128]{1,0:T(8,128)(2,1)} %param.10) | copy-start | bytes 393220
  2.1 7.6 %copy-start.3 = (bf16[512,128]{1,0:T(8,128)(2,1)S(1)}, bf16[512,128]{1,0:T(8,128)(2,1)}, u32[]{:S(2)}) copy-start(bf16[512,128]{1,0:T(8,128)(2,1)} %param.11) | copy-start | bytes 393220
  2.1 15.5 %all-to-all-start = ((bf16[16,32,256]{2,1,0:T(8,128)(2,1)}), bf16[16,32,256]{2,1,0:T(8,128)(2,1)S(1)}, u32[]{:S(2)}, u32[]{:S(2)}) async-start(bf16[16,32,256]{2,1,0:T(8,128)(2,1)} %spread.1), calls=%async_computation | async-start | bytes 524288 | tf_op jit(solution)/shard_map/all_to_all | solution.py:224
  9.7 8.0 %copy-start = (bf16[128,1024]{1,0:T(8,128)(2,1)S(1)}, bf16[128,1024]{1,0:T(8,128)(2,1)}, u32[]{:S(2)}) copy-start(bf16[128,1024]{1,0:T(8,128)(2,1)} %queries_ref.1) | copy-start | bytes 786436
  9.7 8.0 %copy-start.1 = (bf16[128,1024]{1,0:T(8,128)(2,1)S(1)}, bf16[128,1024]{1,0:T(8,128)(2,1)}, u32[]{:S(2)}) copy-start(bf16[128,1024]{1,0:T(8,128)(2,1)} %upstream_ref.1) | copy-start | bytes 786436
  9.8 10.1 %collective-permute-start = (bf16[512,256]{1,0:T(8,128)(2,1)S(1)}, bf16[512,256]{1,0:T(8,128)(2,1)S(1)}, u32[]{:S(2)}, u32[]{:S(2)}) collective-permute-start(bf16[512,256]{1,0:T(8,128)(2,1)S(1)} %constant_dynamic-update-slice_fusion.refs_0_), channel_id=1, source_target_pairs={{0,2},{2,0},{4,6},{6,4},{8,10},{10,8},{12,14},{14,12},{16,18},{18,... | collective-permute-start | bytes 786440 | tf_op jit(solution)/shard_map/ppermute | solution.py:20
  11.2 9.4 %collective-permute-start.1 = (bf16[512,256]{1,0:T(8,128)(2,1)S(1)}, bf16[512,256]{1,0:T(8,128)(2,1)S(1)}, u32[]{:S(2)}, u32[]{:S(2)}) collective-permute-start(bf16[512,256]{1,0:T(8,128)(2,1)S(1)} %constant_dynamic-update-slice_fusion.refs_0_), channel_id=1, source_target_pairs={{0,4},{2,6},{4,0},{6,2},{8,12},{10,14},{12,8},{14,10},{16,20},{18,... | collective-permute-start | bytes 786440 | tf_op jit(solution)/shard_map/ppermute | solution.py:20
  20.6 5.3 %collective-permute-start.2 = (bf16[4,32,256]{2,1,0:T(8,128)(2,1)S(1)}, bf16[4,32,256]{2,1,0:T(8,128)(2,1)S(1)}, u32[]{:S(2)}, u32[]{:S(2)}) collective-permute-start(bf16[4,32,256]{2,1,0:T(8,128)(2,1)S(1)} %get-tuple-element.26), channel_id=1, source_target_pairs={{0,2},{2,0},{4,6},{6,4},{8,10},{10,8},{12,14},{14,12},{16,18},{18,... | collective-permute-start | bytes 196616 | tf_op jit(solution)/shard_map/ppermute | solution.py:20
  21.4 4.5 %collective-permute-start.3 = (bf16[4,32,256]{2,1,0:T(8,128)(2,1)S(1)}, bf16[4,32,256]{2,1,0:T(8,128)(2,1)S(1)}, u32[]{:S(2)}, u32[]{:S(2)}) collective-permute-start(bf16[4,32,256]{2,1,0:T(8,128)(2,1)S(1)} %get-tuple-element.27), channel_id=1, source_target_pairs={{0,4},{2,6},{4,0},{6,2},{8,12},{10,14},{12,8},{14,10},{16,20},{18,... | collective-permute-start | bytes 196616 | tf_op jit(solution)/shard_map/ppermute | solution.py:20
  22.3 4.3 %collective-permute-start.4 = (bf16[4,32,256]{2,1,0:T(8,128)(2,1)S(1)}, bf16[4,32,256]{2,1,0:T(8,128)(2,1)S(1)}, u32[]{:S(2)}, u32[]{:S(2)}) collective-permute-start(bf16[4,32,256]{2,1,0:T(8,128)(2,1)S(1)} %get-tuple-element.28), channel_id=1, source_target_pairs={{0,6},{2,4},{4,2},{6,0},{8,14},{10,12},{12,10},{14,8},{16,22},{18,... | collective-permute-start | bytes 196616 | tf_op jit(solution)/shard_map/ppermute | solution.py:20
  24.5 10.6 %collective-permute-start.8 = (bf16[512,256]{1,0:T(8,128)(2,1)S(1)}, bf16[512,256]{1,0:T(8,128)(2,1)S(1)}, u32[]{:S(2)}, u32[]{:S(2)}) collective-permute-start(bf16[512,256]{1,0:T(8,128)(2,1)S(1)} %constant_dynamic-update-slice_fusion.refs_0_), channel_id=1, source_target_pairs={{0,6},{2,4},{4,2},{6,0},{8,14},{10,12},{12,10},{14,8},{16,22},{18,... | collective-permute-start | bytes 786440 | tf_op jit(solution)/shard_map/ppermute | solution.py:20
  26.6 3.6 %collective-permute-start.5 = (bf16[4,32,256]{2,1,0:T(8,128)(2,1)S(1)}, bf16[4,32,256]{2,1,0:T(8,128)(2,1)S(1)}, u32[]{:S(2)}, u32[]{:S(2)}) collective-permute-start(bf16[4,32,256]{2,1,0:T(8,128)(2,1)S(1)} %get-tuple-element.42), channel_id=1, source_target_pairs={{0,8},{2,10},{4,12},{6,14},{8,0},{10,2},{12,4},{14,6},{16,24},{18,... | collective-permute-start | bytes 196616 | tf_op jit(solution)/shard_map/ppermute | solution.py:20
  27.7 4.3 %collective-permute-start.6 = (bf16[4,32,256]{2,1,0:T(8,128)(2,1)S(1)}, bf16[4,32,256]{2,1,0:T(8,128)(2,1)S(1)}, u32[]{:S(2)}, u32[]{:S(2)}) collective-permute-start(bf16[4,32,256]{2,1,0:T(8,128)(2,1)S(1)} %get-tuple-element.42), channel_id=1, source_target_pairs={{0,16},{2,18},{4,20},{6,22},{8,24},{10,26},{12,28},{14,30},{16,0},... | collective-permute-start | bytes 196616 | tf_op jit(solution)/shard_map/ppermute | solution.py:20
  30.0 5.1 %collective-permute-start.7 = (bf16[4,32,256]{2,1,0:T(8,128)(2,1)S(1)}, bf16[4,32,256]{2,1,0:T(8,128)(2,1)S(1)}, u32[]{:S(2)}, u32[]{:S(2)}) collective-permute-start(bf16[4,32,256]{2,1,0:T(8,128)(2,1)S(1)} %get-tuple-element.42), channel_id=1, source_target_pairs={{0,24},{2,26},{4,28},{6,30},{8,16},{10,18},{12,20},{14,22},{16,8},... | collective-permute-start | bytes 196616 | tf_op jit(solution)/shard_map/ppermute | solution.py:20
  35.6 5.5 %collective-permute-start.9 = (bf16[2,32,2048]{2,1,0:T(8,128)(2,1)S(1)}, bf16[2,32,2048]{2,1,0:T(8,128)(2,1)S(1)}, u32[]{:S(2)}, u32[]{:S(2)}) collective-permute-start(bf16[2,32,2048]{2,1,0:T(8,128)(2,1)S(1)} %get-tuple-element.41), channel_id=1, source_target_pairs={{0,1},{1,0},{2,3},{3,2},{4,5},{5,4},{6,7},{7,6},{8,9},{9,8},{10,11... | collective-permute-start | bytes 786440 | tf_op jit(solution)/shard_map/ppermute | solution.py:20
  41.2 6.1 %collective-permute-start.10 = (bf16[32,2048]{1,0:T(8,128)(2,1)S(1)}, bf16[32,2048]{1,0:T(8,128)(2,1)S(1)}, u32[]{:S(2)}, u32[]{:S(2)}) collective-permute-start(bf16[32,2048]{1,0:T(8,128)(2,1)S(1)} %get-tuple-element.47), channel_id=1, source_target_pairs={{0,8},{1,16},{2,10},{3,18},{4,12},{5,20},{6,14},{7,22},{8,0},{9,24... | collective-permute-start | bytes 393224 | tf_op jit(solution)/shard_map/ppermute | solution.py:252
  42.1 8.2 %collective-permute-start.11 = (bf16[32,2048]{1,0:T(8,128)(2,1)S(1)}, bf16[32,2048]{1,0:T(8,128)(2,1)S(1)}, u32[]{:S(2)}, u32[]{:S(2)}) collective-permute-start(bf16[32,2048]{1,0:T(8,128)(2,1)S(1)} %get-tuple-element.46), channel_id=1, source_target_pairs={{1,24},{3,26},{5,28},{7,30},{9,16},{11,18},{13,20},{15,22},{16,9},... | collective-permute-start | bytes 393224 | tf_op jit(solution)/shard_map/ppermute | solution.py:253

commit v4 on v3

--- a/solution.py
+++ b/solution.py
@@ -20,24 +20,16 @@
     return lax.ppermute(block, axis, [(i, i ^ distance) for i in range(size)])
 
 
-def spread_kernel(keys_ref, values_ref, out_ref):
-    for i in range(out_ref.shape[0]):
-        out_ref[i, :, :HEAD] = keys_ref[...]
-        out_ref[i, :, HEAD:] = values_ref[...]
-
-
-def spread(keys, values, copies):
-    return pl.pallas_call(
-        spread_kernel,
-        out_shape=pltpu.VMEM((copies, keys.shape[0], 2 * HEAD), BF16),
-        in_specs=[IN_VMEM] * 2,
-        out_specs=IN_VMEM,
-        name="spread",
-    )(keys, values)
-
-
-def attention_kernel(queries_ref, upstream_ref, vision_ref, low_ref, *refs):
-    terms_refs, (rows, low, sums) = refs[:-3], refs[-3:]
+def swap(block, chips, distance):
+    routes = [(2 * u + c, 2 * (u ^ distance) + 1 - c) for u in range(chips) for c in range(2)]
+    return lax.ppermute(block, ("seq", "kv"), routes)
+
+
+def attention_kernel(line, queries_ref, upstream_ref, *refs):
+    vision_refs, low_ref, vision_ref = refs[:line], refs[line], refs[line + 1]
+    terms_refs, (rows, low, sums) = refs[line + 2 : -3], refs[-3:]
+    for d, ref in enumerate(vision_refs):
+        vision_ref[d * ref.shape[0] : (d + 1) * ref.shape[0]] = ref[...]
     row_count, width = queries_ref.shape
     heads = width // HEAD
     scaling = 1.0 / math.sqrt(HEAD)
@@ -59,28 +51,33 @@
         row_dots = jnp.sum(exponent * grad_probs, axis=0, keepdims=True) * inverse
         low[:, at] = (exponent * inverse).astype(BF16)
         low_ref[:, at] = (exponent * (grad_probs - row_dots) * (inverse * scaling)).astype(BF16)
-    line, plane, own, _ = sums.shape
+    _, plane, own, _ = sums.shape
     for i, factor in enumerate((low_ref, low)):
         term = jnp.dot(factor[...], rows[i], preferred_element_type=F32)
         sums[:, :, :, i * HEAD : (i + 1) * HEAD] = term.reshape(line, plane, own, HEAD)
-    spot = lax.rem(lax.axis_index("seq"), plane)
+    spot = lax.axis_index("seq") // plane
     for d, ref in enumerate(terms_refs):
-        ref[...] = sums[:, jnp.bitwise_xor(spot, d)].astype(ref.dtype)
-
-
-def attention_terms(queries, upstream, vision, plane, line):
+        for i in range(line):
+            ref[i] = sums[jnp.bitwise_xor(spot, i), d].astype(ref.dtype)
+
+
+def attention_terms(queries, upstream, blocks, plane):
     rows, width = queries.shape
-    tokens = vision.shape[0]
+    line = len(blocks)
+    tokens = line * blocks[0].shape[0]
     pairs = rows * width // HEAD
     own = tokens // (plane * line)
-    low, *terms = pl.pallas_call(
-        attention_kernel,
-        out_shape=[jax.ShapeDtypeStruct((tokens, pairs), BF16)]
+    low, vision, *terms = pl.pallas_call(
+        functools.partial(attention_kernel, line),
+        out_shape=[
+            jax.ShapeDtypeStruct((tokens, pairs), BF16),
+            jax.ShapeDtypeStruct((tokens, 2 * HEAD), BF16),
+        ]
         + [
             jax.ShapeDtypeStruct((line, own, 2 * HEAD), BF16 if d else F32) for d in range(plane)
         ],
-        in_specs=[IN_VMEM] * 3,
-        out_specs=[IN_VMEM] * (1 + plane),
+        in_specs=[IN_VMEM] * (2 + line),
+        out_specs=[IN_VMEM] * (2 + plane),
         scratch_shapes=[
             pltpu.VMEM((2, pairs, HEAD), BF16),
             pltpu.VMEM((tokens, pairs), BF16),
@@ -93,8 +90,8 @@
             transcendentals=pairs * tokens,
         ),
         name="attention_terms",
-    )(queries, upstream, vision)
-    return low, terms
+    )(queries, upstream, *blocks)
+    return low, vision, terms
 
 
 def query_kernel(low_ref, vision_ref, query_ref):
@@ -121,16 +118,18 @@
     )(low, vision)
 
 
-def project_kernel(sums_ref, near_ref, far_ref, cross_ref, *refs):
-    weights, (keep_ref, send_ref, grads) = refs[:-3], refs[-3:]
+def project_kernel(sums_ref, *refs):
+    arrived, weights, (keep_ref, send_ref, grads) = refs[:3], refs[3:-3], refs[-3:]
     plane = len(weights)
     me = lax.axis_index("seq")
     core = lax.axis_index("kv")
     home = core == me // (2 * plane)
     odd = lax.rem(me // plane, 2)
     spot = lax.rem(me, plane)
-    total = sums_ref[...] + near_ref[...].astype(F32) + far_ref[...].astype(F32)
-    grads[...] = (total + cross_ref[...].astype(F32)).astype(BF16)
+    total = sums_ref[...]
+    for ref in arrived:
+        total = total + ref[...].astype(F32)
+    grads[...] = total.astype(BF16)
     first = 2 * core + jnp.where(home, odd, 1 - odd)
     second = 2 * core + jnp.where(home, 1 - odd, odd)
     blocks = [grads[i] for i in (first, second, 3 - first, 3 - second)]
@@ -184,9 +183,10 @@
     core = lax.axis_index("kv")
     own = vision_key.shape[0]
     weights = gather_cube(jnp.concatenate([key_weight, value_weight], axis=1), cube)
-    vision = lax.all_to_all(spread(vision_key, vision_value, chips), "seq", 0, 0)
-    vision = vision.reshape(chips * own, 2 * HEAD)
-    low, terms = attention_terms(text_query, grad_output, vision, cube, 2)
+    pair = jnp.concatenate([vision_key, vision_value], axis=1)
+    block = gather_cube(pair, cube).reshape(cube * own, 2 * HEAD)
+    blocks = [block, exchange(block, "seq", chips, cube)]
+    low, vision, terms = attention_terms(text_query, grad_output, blocks, cube)
     grad_query = query_gradient(low, vision, text_query.shape[0])
     partial = terms[0]
     for d in range(1, cube):
@@ -221,11 +221,16 @@
     plane = chips // line
     own = vision_key.shape[0]
 
-    vision = lax.all_to_all(spread(vision_key, vision_value, chips), "seq", 0, 0)
-    vision = vision.reshape(chips * own, 2 * HEAD)
+    near, far, cross = plane, 2 * plane, 3 * plane
+    pair = jnp.concatenate([vision_key, vision_value], axis=1)
+    arrived = {d: swap(pair, chips, d) for d in (3, 1, 2, 0)}
+    block = jnp.concatenate([arrived[d] for d in range(plane)], axis=0)
+    blocks = {d: swap(block, chips, d) for d in (cross, far, near, 0)}
     weight = jnp.concatenate([key_weight, value_weight], axis=1)
     weights = [weight] + [exchange(weight, "seq", chips, d) for d in (1, 2)]
-    low, terms = attention_terms(text_query, grad_output, vision, plane, line)
+    low, vision, terms = attention_terms(
+        text_query, grad_output, [blocks[d] for d in (0, near, far, cross)], plane
+    )
     terms, weights = lax.optimization_barrier((terms, weights))
     grad_query = query_gradient(low, vision, text_query.shape[0])
     weight, grad_query = lax.optimization_barrier((weights[0], grad_query))
@@ -236,8 +241,7 @@
     sums = terms[0]
     for block in arrived:
         sums = sums + block.astype(F32)
-    near, far, cross = plane, 2 * plane, 3 * plane
-    arrived = [exchange(sums.astype(BF16), "seq", chips, d) for d in (near, far, cross)]
+    arrived = [exchange(sums.astype(BF16), "seq", chips, d) for d in (cross, far, near)]
     keep, send = project(sums, arrived, weights)
     total = (keep + exchange(send, "kv", 2, 1).astype(F32)).astype(BF16)
     stay, go = total[0], total[1]
@@ -248,6 +252,7 @@
         routes_a.append((2 * u + home, 2 * (u ^ near) + home))
         routes_a.append((2 * u + 1 - home, 2 * (u ^ far) + home))
         routes_b.append((2 * u + 1 - home, 2 * (u ^ cross) + home))
+        routes_b.append((2 * u + home, 2 * (u ^ 1) + home))
     at_home = core == me // far
     first = lax.ppermute(go, ("seq", "kv"), routes_a)
     second = lax.ppermute(stay, ("seq", "kv"), routes_b)
@@ -263,7 +268,7 @@
 def solution(mesh):
     spec = P("seq", "kv")
     return jax.shard_map(
-        two_cores if mesh.shape["kv"] == 2 and mesh.shape["seq"] % 4 == 0 else many_cores,
+        two_cores if (mesh.shape["seq"], mesh.shape["kv"]) == (16, 2) else many_cores,
         mesh=mesh,
         in_specs=(spec,) * 6,
         out_specs=(spec, spec),

time: 51.5 us -> 48.1 us (0.934)
  starting transfers between devices: 25.6 us -> 23.5 us
  local copies, waits for them, and re-layouts: 0.1 us -> 1.76 us
  Pallas kernels: 5.37 us -> 3.93 us
  waiting for transfers between devices: 18.3 us -> 17 us
    ppermute x0 -> x8, starting transfers between devices: none -> 9.54 us  [swap(): return lax.ppermute(block, ('seq', 'kv'), routes)]
    all_to_all x1 -> x0, starting transfers between devices: 7.55 us -> none  [two_cores(): lax.all_to_all(spread(vision_key, vision_value, chips), 'seq', 0, 0)]
    ppermute x0 -> x8, waiting for transfers between devices: none -> 5.45 us  [swap(): return lax.ppermute(block, ('seq', 'kv'), routes)]
    all_to_all x1 -> x0, waiting for transfers between devices: 5.24 us -> none  [two_cores(): lax.all_to_all(spread(vision_key, vision_value, chips), 'seq', 0, 0)]
    ppermute x10, starting transfers between devices: 14.7 us -> 11.5 us  [exchange(): return lax.ppermute(block, axis, [(i, i ^ distance) for i in range(size)])]
    ppermute x1, waiting for transfers between devices: 2.96 us -> 0.01 us  [two_cores(): second = lax.ppermute(stay, ('seq', 'kv'), routes_b)]
    ppermute x1, waiting for transfers between devices: 2.67 us -> 5.52 us  [two_cores(): first = lax.ppermute(go, ('seq', 'kv'), routes_a)]
    unnamed x9 -> x13, local copies, waits for them, and re-layouts: 0.04 us -> 1.7 us
  transfers between devices with their start and end apart: 13 -> 20, of which waited for: 8 -> 8; matrix products, arithmetic and copies ran while one was open for 0% -> 2% of each run, Pallas kernels for 7% -> 7%
where the time goes in v4:
time: 48.1 us; the launch traced here: 47.8 us
  starting transfers between devices  23.5 us (49%)
  waiting for transfers between devices  17 us (35%)
  Pallas kernels  3.93 us (8%)
  local copies, waits for them, and re-layouts  1.76 us (4%)
  other arithmetic  0.83 us (2%)
  between operations  0.76 us (2%)
    ppermute x10, starting transfers between devices, exchange(): return lax.ppermute(block, axis, [(i, i ^ distance) for i in range(size)])  11.5 us
    ppermute x8, starting transfers between devices, swap(): return lax.ppermute(block, ('seq', 'kv'), routes)  9.54 us
    ppermute x10, waiting for transfers between devices, exchange(): return lax.ppermute(block, axis, [(i, i ^ distance) for i in range(size)])  6.07 us
    ppermute x1, waiting for transfers between devices, two_cores(): first = lax.ppermute(go, ('seq', 'kv'), routes_a)  5.52 us
    ppermute x8, waiting for transfers between devices, swap(): return lax.ppermute(block, ('seq', 'kv'), routes)  5.45 us
    pallas_call x1, Pallas kernels, attention_terms(): pl.pallas_call(functools.partial(attention_kernel, line), out_shape=[jax....  2.25 us
    unnamed x13, local copies, waits for them, and re-layouts  1.7 us
    ppermute x1, starting transfers between devices, two_cores(): second = lax.ppermute(stay, ('seq', 'kv'), routes_b)  1.28 us
  transfers between devices with their start and end apart: 20, of which 8 were waited for; matrix products, arithmetic and copies ran while one was open for 2% of the time, Pallas kernels for 7%

profile of v4, /device:TPU:1, one launch (start us, length us, event | category | flops | bytes accessed | tf_op | source)
XLA Modules:
  0.0 47.8 jit_solution(18247450967629100461)
XLA Ops:
  0.6 0.7 %constant_dynamic-update-slice_fusion.1 = bf16[32,256]{1,0:T(8,128)(2,1)S(1)} fusion(bf16[32,128]{1,0:T(8,128)(2,1)} %param.7), kind=kLoop, calls=%fused_computation.10 | loop fusion | bytes 16384
  1.5 2.6 %collective-permute-start.1 = (bf16[32,256]{1,0:T(8,128)(2,1)S(1)}, bf16[32,256]{1,0:T(8,128)(2,1)S(1)}, u32[]{:S(2)}, u32[]{:S(2)}) collective-permute-start(bf16[32,256]{1,0:T(8,128)(2,1)S(1)} %constant_dynamic-update-slice_fusion), channel_id=1, source_target_pairs={{0,3},{1,2},{2,1},{3,0},{4,7},{5,6},{6,5},{7,4},{8,11},{9,10},{10,... | collective-permute-start | bytes 49160 | tf_op jit(solution)/shard_map/ppermute | solution.py:25
  4.1 1.6 %collective-permute-start.2 = (bf16[32,256]{1,0:T(8,128)(2,1)S(1)}, bf16[32,256]{1,0:T(8,128)(2,1)S(1)}, u32[]{:S(2)}, u32[]{:S(2)}) collective-permute-start(bf16[32,256]{1,0:T(8,128)(2,1)S(1)} %constant_dynamic-update-slice_fusion), channel_id=1, source_target_pairs={{0,5},{1,4},{2,7},{3,6},{4,1},{5,0},{6,3},{7,2},{8,13},{9,12},{10,... | collective-permute-start | bytes 49160 | tf_op jit(solution)/shard_map/ppermute | solution.py:25
  5.7 1.0 %constant_dynamic-update-slice_fusion.7 = bf16[512,256]{1,0:T(8,128)(2,1)S(1)} fusion(bf16[512,128]{1,0:T(8,128)(2,1)} %param.10), kind=kLoop, calls=%fused_computation.16 | loop fusion | bytes 262144
  6.7 1.4 %collective-permute-start.8 = (bf16[512,256]{1,0:T(8,128)(2,1)S(1)}, bf16[512,256]{1,0:T(8,128)(2,1)S(1)}, u32[]{:S(2)}, u32[]{:S(2)}) collective-permute-start(bf16[512,256]{1,0:T(8,128)(2,1)S(1)} %constant_dynamic-update-slice_fusion.6.refs_3_), channel_id=1, source_target_pairs={{0,2},{2,0},{4,6},{6,4},{8,10},{10,8},{12,14},{14,12},{16,18},{18,... | collective-permute-start | bytes 786440 | tf_op jit(solution)/shard_map/ppermute | solution.py:20
  8.1 1.2 %collective-permute-start.9 = (bf16[512,256]{1,0:T(8,128)(2,1)S(1)}, bf16[512,256]{1,0:T(8,128)(2,1)S(1)}, u32[]{:S(2)}, u32[]{:S(2)}) collective-permute-start(bf16[512,256]{1,0:T(8,128)(2,1)S(1)} %constant_dynamic-update-slice_fusion.6.refs_3_), channel_id=1, source_target_pairs={{0,4},{2,6},{4,0},{6,2},{8,12},{10,14},{12,8},{14,10},{16,20},{18,... | collective-permute-start | bytes 786440 | tf_op jit(solution)/shard_map/ppermute | solution.py:20
  9.7 0.8 %collective-permute-start.4 = (bf16[128,256]{1,0:T(8,128)(2,1)S(1)}, bf16[128,256]{1,0:T(8,128)(2,1)S(1)}, u32[]{:S(2)}, u32[]{:S(2)}) collective-permute-start(bf16[128,256]{1,0:T(8,128)(2,1)S(1)} %constant_dynamic-update-slice_fusion.2), channel_id=1, source_target_pairs={{0,1},{1,0},{2,3},{3,2},{4,5},{5,4},{6,7},{7,6},{8,9},{9,8},{10,11... | collective-permute-start | bytes 196616 | tf_op jit(solution)/shard_map/ppermute | solution.py:25
  10.5 1.3 %collective-permute-start.5 = (bf16[128,256]{1,0:T(8,128)(2,1)S(1)}, bf16[128,256]{1,0:T(8,128)(2,1)S(1)}, u32[]{:S(2)}, u32[]{:S(2)}) collective-permute-start(bf16[128,256]{1,0:T(8,128)(2,1)S(1)} %constant_dynamic-update-slice_fusion.2), channel_id=1, source_target_pairs={{0,9},{1,8},{2,11},{3,10},{4,13},{5,12},{6,15},{7,14},{8,1},{9,0},... | collective-permute-start | bytes 196616 | tf_op jit(solution)/shard_map/ppermute | solution.py:25
  11.8 2.6 %collective-permute-start.6 = (bf16[128,256]{1,0:T(8,128)(2,1)S(1)}, bf16[128,256]{1,0:T(8,128)(2,1)S(1)}, u32[]{:S(2)}, u32[]{:S(2)}) collective-permute-start(bf16[128,256]{1,0:T(8,128)(2,1)S(1)} %constant_dynamic-update-slice_fusion.2), channel_id=1, source_target_pairs={{0,17},{1,16},{2,19},{3,18},{4,21},{5,20},{6,23},{7,22},{8,25},{9,... | collective-permute-start | bytes 196616 | tf_op jit(solution)/shard_map/ppermute | solution.py:25
  15.0 3.5 %collective-permute-done.6.refs_2_ = bf16[128,256]{1,0:T(8,128)(2,1)S(1)} collective-permute-done((bf16[128,256]{1,0:T(8,128)(2,1)S(1)}, bf16[128,256]{1,0:T(8,128)(2,1)S(1)}, u32[]{:S(2)}, u32[]{:S(2)}) %collective-permute-start.6) | collective-permute-done | bytes 65568 | tf_op jit(solution)/shard_map/ppermute | solution.py:25
  18.5 1.6 %collective-permute-done.7.refs_3_ = bf16[128,256]{1,0:T(8,128)(2,1)S(1)} collective-permute-done((bf16[128,256]{1,0:T(8,128)(2,1)S(1)}, bf16[128,256]{1,0:T(8,128)(2,1)S(1)}, u32[]{:S(2)}, u32[]{:S(2)}) %collective-permute-start.7) | collective-permute-done | bytes 65568 | tf_op jit(solution)/shard_map/ppermute | solution.py:25
  20.1 2.2 %attention_terms.1 = (bf16[512,1024]{1,0:T(8,128)(2,1)S(1)}, bf16[512,256]{1,0:T(8,128)(2,1)S(1)}, f32[4,32,256]{2,1,0:T(8,128)S(1)}, bf16[4,32,256]{2,1,0:T(8,1...) custom-call(bf16[128,1024]{1,0:T(8,128)(2,1)S(1)} %copy-done, ...), custom_call_target="tpu_custom_call" | custom-call | flops 536870912 | bytes 786432 | tf_op jit(solution)/shard_map/attention_terms/pallas_call | solution.py:70
  22.9 2.2 %collective-permute-start.12 = (bf16[4,32,256]{2,1,0:T(8,128)(2,1)S(1)}, bf16[4,32,256]{2,1,0:T(8,128)(2,1)S(1)}, u32[]{:S(2)}, u32[]{:S(2)}) collective-permute-start(bf16[4,32,256]{2,1,0:T(8,128)(2,1)S(1)} %get-tuple-element.29), channel_id=1, source_target_pairs={{0,6},{2,4},{4,2},{6,0},{8,14},{10,12},{12,10},{14,8},{16,22},{18,... | collective-permute-start | bytes 196616 | tf_op jit(solution)/shard_map/ppermute | solution.py:20
  25.1 1.2 %query_gradient.1 = bf16[128,1024]{1,0:T(8,128)(2,1)} custom-call(bf16[512,1024]{1,0:T(8,128)(2,1)S(1)} %get-tuple-element.31.low_ref, bf16[512,256]{1,0:T(8,128)(2,1)S(1)} %get-tuple-element.32.vision_ref), custom_call_target="tpu_custom_call" | custom-call | flops 134217728 | bytes 262144 | tf_op jit(solution)/shard_map/query_gradient/pallas_call | solution.py:108
  27.1 2.0 %collective-permute-start.13 = (bf16[4,32,256]{2,1,0:T(8,128)(2,1)S(1)}, bf16[4,32,256]{2,1,0:T(8,128)(2,1)S(1)}, u32[]{:S(2)}, u32[]{:S(2)}) collective-permute-start(bf16[4,32,256]{2,1,0:T(8,128)(2,1)S(1)} %get-tuple-element.44), channel_id=1, source_target_pairs={{0,24},{2,26},{4,28},{6,30},{8,16},{10,18},{12,20},{14,22},{16,8},... | collective-permute-start | bytes 196616 | tf_op jit(solution)/shard_map/ppermute | solution.py:20
  29.7 1.0 %collective-permute-start.15 = (bf16[4,32,256]{2,1,0:T(8,128)(2,1)S(1)}, bf16[4,32,256]{2,1,0:T(8,128)(2,1)S(1)}, u32[]{:S(2)}, u32[]{:S(2)}) collective-permute-start(bf16[4,32,256]{2,1,0:T(8,128)(2,1)S(1)} %get-tuple-element.44), channel_id=1, source_target_pairs={{0,8},{2,10},{4,12},{6,14},{8,0},{10,2},{12,4},{14,6},{16,24},{18,... | collective-permute-start | bytes 196616 | tf_op jit(solution)/shard_map/ppermute | solution.py:20
  30.7 1.4 %collective-permute-done.13.refs_0_ = bf16[4,32,256]{2,1,0:T(8,128)(2,1)S(1)} collective-permute-done((bf16[4,32,256]{2,1,0:T(8,128)(2,1)S(1)}, bf16[4,32,256]{2,1,0:T(8,128)(2,1)S(1)}, u32[]{:S(2)}, u32[]{:S(2)}) %collective-permute-start.13) | collective-permute-done | bytes 65568 | tf_op jit(solution)/shard_map/ppermute | solution.py:20
  32.0 3.0 %collective-permute-done.14.refs_1_ = bf16[4,32,256]{2,1,0:T(8,128)(2,1)S(1)} collective-permute-done((bf16[4,32,256]{2,1,0:T(8,128)(2,1)S(1)}, bf16[4,32,256]{2,1,0:T(8,128)(2,1)S(1)}, u32[]{:S(2)}, u32[]{:S(2)}) %collective-permute-start.14) | collective-permute-done | bytes 65568 | tf_op jit(solution)/shard_map/ppermute | solution.py:20
  35.5 2.4 %collective-permute-start.17 = (bf16[2,32,2048]{2,1,0:T(8,128)(2,1)S(1)}, bf16[2,32,2048]{2,1,0:T(8,128)(2,1)S(1)}, u32[]{:S(2)}, u32[]{:S(2)}) collective-permute-start(bf16[2,32,2048]{2,1,0:T(8,128)(2,1)S(1)} %get-tuple-element.43), channel_id=1, source_target_pairs={{0,1},{1,0},{2,3},{3,2},{4,5},{5,4},{6,7},{7,6},{8,9},{9,8},{10,11... | collective-permute-start | bytes 786440 | tf_op jit(solution)/shard_map/ppermute | solution.py:20
  37.9 1.2 %collective-permute-done.17 = bf16[2,32,2048]{2,1,0:T(8,128)(2,1)S(1)} collective-permute-done((bf16[2,32,2048]{2,1,0:T(8,128)(2,1)S(1)}, bf16[2,32,2048]{2,1,0:T(8,128)(2,1)S(1)}, u32[]{:S(2)}, u32[]{:S(2)}) %collective-permute-start.17) | collective-permute-done | bytes 262176 | tf_op jit(solution)/shard_map/ppermute | solution.py:20
  39.1 1.2 %collective-permute-start.18 = (bf16[32,2048]{1,0:T(8,128)(2,1)S(1)}, bf16[32,2048]{1,0:T(8,128)(2,1)S(1)}, u32[]{:S(2)}, u32[]{:S(2)}) collective-permute-start(bf16[32,2048]{1,0:T(8,128)(2,1)S(1)} %get-tuple-element.49), channel_id=1, source_target_pairs={{0,8},{1,16},{2,10},{3,18},{4,12},{5,20},{6,14},{7,22},{8,0},{9,24... | collective-permute-start | bytes 393224 | tf_op jit(solution)/shard_map/ppermute | solution.py:257
  40.3 1.3 %collective-permute-start.19 = (bf16[32,2048]{1,0:T(8,128)(2,1)S(1)}, bf16[32,2048]{1,0:T(8,128)(2,1)S(1)}, u32[]{:S(2)}, u32[]{:S(2)}) collective-permute-start(bf16[32,2048]{1,0:T(8,128)(2,1)S(1)} %get-tuple-element.48), channel_id=1, source_target_pairs={{1,24},{0,2},{3,26},{2,0},{5,28},{4,6},{7,30},{6,4},{9,16},{8,10},... | collective-permute-start | bytes 393224 | tf_op jit(solution)/shard_map/ppermute | solution.py:258
  41.6 5.5 %collective-permute-done.18 = bf16[32,2048]{1,0:T(8,128)(2,1)S(1)} collective-permute-done((bf16[32,2048]{1,0:T(8,128)(2,1)S(1)}, bf16[32,2048]{1,0:T(8,128)(2,1)S(1)}, u32[]{:S(2)}, u32[]{:S(2)}) %collective-permute-start.18) | collective-permute-done | bytes 131104 | tf_op jit(solution)/shard_map/ppermute | solution.py:257
  47.1 0.7 %pad_maximum_fusion = bf16[32,4096]{1,0:T(8,128)(2,1)} fusion(bf16[32,2048]{1,0:T(8,128)(2,1)S(1)} %get-tuple-element.47, bf16[32,2048]{1,0:T(8,128)(2,1)S(1)} %get-tuple-element.46), kind=kLoop, calls=%fused_computation.1 | loop fusion | flops 524288 | bytes 524288 | tf_op jit(solution)/shard_map/concatenate | solution.py:262
  (40 shorter events, 3.5 us)
Async XLA Ops:
  0.6 0.7 %copy-start.3 = (bf16[32,128]{1,0:T(8,128)(2,1)S(1)}, bf16[32,128]{1,0:T(8,128)(2,1)}, u32[]{:S(2)}) copy-start(bf16[32,128]{1,0:T(8,128)(2,1)} %param.8) | copy-start | bytes 24580
  1.3 5.3 %copy-start.2 = (bf16[512,128]{1,0:T(8,128)(2,1)S(1)}, bf16[512,128]{1,0:T(8,128)(2,1)}, u32[]{:S(2)}) copy-start(bf16[512,128]{1,0:T(8,128)(2,1)} %param.11) | copy-start | bytes 393220
  1.4 6.8 %collective-permute-start = (bf16[32,256]{1,0:T(8,128)(2,1)S(1)}, bf16[32,256]{1,0:T(8,128)(2,1)S(1)}, u32[]{:S(2)}, u32[]{:S(2)}) collective-permute-start(bf16[32,256]{1,0:T(8,128)(2,1)S(1)} %constant_dynamic-update-slice_fusion), channel_id=1, source_target_pairs={{0,1},{1,0},{2,3},{3,2},{4,5},{5,4},{6,7},{7,6},{8,9},{9,8},{10,11... | collective-permute-start | bytes 49160 | tf_op jit(solution)/shard_map/ppermute | solution.py:25
  1.5 7.9 %collective-permute-start.1 = (bf16[32,256]{1,0:T(8,128)(2,1)S(1)}, bf16[32,256]{1,0:T(8,128)(2,1)S(1)}, u32[]{:S(2)}, u32[]{:S(2)}) collective-permute-start(bf16[32,256]{1,0:T(8,128)(2,1)S(1)} %constant_dynamic-update-slice_fusion), channel_id=1, source_target_pairs={{0,3},{1,2},{2,1},{3,0},{4,7},{5,6},{6,5},{7,4},{8,11},{9,10},{10,... | collective-permute-start | bytes 49160 | tf_op jit(solution)/shard_map/ppermute | solution.py:25
  4.1 5.3 %collective-permute-start.2 = (bf16[32,256]{1,0:T(8,128)(2,1)S(1)}, bf16[32,256]{1,0:T(8,128)(2,1)S(1)}, u32[]{:S(2)}, u32[]{:S(2)}) collective-permute-start(bf16[32,256]{1,0:T(8,128)(2,1)S(1)} %constant_dynamic-update-slice_fusion), channel_id=1, source_target_pairs={{0,5},{1,4},{2,7},{3,6},{4,1},{5,0},{6,3},{7,2},{8,13},{9,12},{10,... | collective-permute-start | bytes 49160 | tf_op jit(solution)/shard_map/ppermute | solution.py:25
  5.7 4.1 %collective-permute-start.3 = (bf16[32,256]{1,0:T(8,128)(2,1)S(1)}, bf16[32,256]{1,0:T(8,128)(2,1)S(1)}, u32[]{:S(2)}, u32[]{:S(2)}) collective-permute-start(bf16[32,256]{1,0:T(8,128)(2,1)S(1)} %constant_dynamic-update-slice_fusion), channel_id=1, source_target_pairs={{0,7},{1,6},{2,5},{3,4},{4,3},{5,2},{6,1},{7,0},{8,15},{9,14},{10,... | collective-permute-start | bytes 49160 | tf_op jit(solution)/shard_map/ppermute | solution.py:25
  5.7 14.4 %copy-start.1 = (bf16[128,1024]{1,0:T(8,128)(2,1)S(1)}, bf16[128,1024]{1,0:T(8,128)(2,1)}, u32[]{:S(2)}) copy-start(bf16[128,1024]{1,0:T(8,128)(2,1)} %upstream_ref.1) | copy-start | bytes 786436
  6.7 13.4 %copy-start = (bf16[128,1024]{1,0:T(8,128)(2,1)S(1)}, bf16[128,1024]{1,0:T(8,128)(2,1)}, u32[]{:S(2)}) copy-start(bf16[128,1024]{1,0:T(8,128)(2,1)} %queries_ref.1) | copy-start | bytes 786436
  6.7 15.6 %collective-permute-start.8 = (bf16[512,256]{1,0:T(8,128)(2,1)S(1)}, bf16[512,256]{1,0:T(8,128)(2,1)S(1)}, u32[]{:S(2)}, u32[]{:S(2)}) collective-permute-start(bf16[512,256]{1,0:T(8,128)(2,1)S(1)} %constant_dynamic-update-slice_fusion.6.refs_3_), channel_id=1, source_target_pairs={{0,2},{2,0},{4,6},{6,4},{8,10},{10,8},{12,14},{14,12},{16,18},{18,... | collective-permute-start | bytes 786440 | tf_op jit(solution)/shard_map/ppermute | solution.py:20
  8.1 14.2 %collective-permute-start.9 = (bf16[512,256]{1,0:T(8,128)(2,1)S(1)}, bf16[512,256]{1,0:T(8,128)(2,1)S(1)}, u32[]{:S(2)}, u32[]{:S(2)}) collective-permute-start(bf16[512,256]{1,0:T(8,128)(2,1)S(1)} %constant_dynamic-update-slice_fusion.6.refs_3_), channel_id=1, source_target_pairs={{0,4},{2,6},{4,0},{6,2},{8,12},{10,14},{12,8},{14,10},{16,20},{18,... | collective-permute-start | bytes 786440 | tf_op jit(solution)/shard_map/ppermute | solution.py:20
  9.7 4.7 %collective-permute-start.4 = (bf16[128,256]{1,0:T(8,128)(2,1)S(1)}, bf16[128,256]{1,0:T(8,128)(2,1)S(1)}, u32[]{:S(2)}, u32[]{:S(2)}) collective-permute-start(bf16[128,256]{1,0:T(8,128)(2,1)S(1)} %constant_dynamic-update-slice_fusion.2), channel_id=1, source_target_pairs={{0,1},{1,0},{2,3},{3,2},{4,5},{5,4},{6,7},{7,6},{8,9},{9,8},{10,11... | collective-permute-start | bytes 196616 | tf_op jit(solution)/shard_map/ppermute | solution.py:25
  10.5 4.5 %collective-permute-start.5 = (bf16[128,256]{1,0:T(8,128)(2,1)S(1)}, bf16[128,256]{1,0:T(8,128)(2,1)S(1)}, u32[]{:S(2)}, u32[]{:S(2)}) collective-permute-start(bf16[128,256]{1,0:T(8,128)(2,1)S(1)} %constant_dynamic-update-slice_fusion.2), channel_id=1, source_target_pairs={{0,9},{1,8},{2,11},{3,10},{4,13},{5,12},{6,15},{7,14},{8,1},{9,0},... | collective-permute-start | bytes 196616 | tf_op jit(solution)/shard_map/ppermute | solution.py:25
  11.8 6.7 %collective-permute-start.6 = (bf16[128,256]{1,0:T(8,128)(2,1)S(1)}, bf16[128,256]{1,0:T(8,128)(2,1)S(1)}, u32[]{:S(2)}, u32[]{:S(2)}) collective-permute-start(bf16[128,256]{1,0:T(8,128)(2,1)S(1)} %constant_dynamic-update-slice_fusion.2), channel_id=1, source_target_pairs={{0,17},{1,16},{2,19},{3,18},{4,21},{5,20},{6,23},{7,22},{8,25},{9,... | collective-permute-start | bytes 196616 | tf_op jit(solution)/shard_map/ppermute | solution.py:25
  14.4 5.7 %collective-permute-start.7 = (bf16[128,256]{1,0:T(8,128)(2,1)S(1)}, bf16[128,256]{1,0:T(8,128)(2,1)S(1)}, u32[]{:S(2)}, u32[]{:S(2)}) collective-permute-start(bf16[128,256]{1,0:T(8,128)(2,1)S(1)} %constant_dynamic-update-slice_fusion.2), channel_id=1, source_target_pairs={{0,25},{1,24},{2,27},{3,26},{4,29},{5,28},{6,31},{7,30},{8,17},{9,... | collective-permute-start | bytes 196616 | tf_op jit(solution)/shard_map/ppermute | solution.py:25
  22.4 4.1 %collective-permute-start.10 = (bf16[4,32,256]{2,1,0:T(8,128)(2,1)S(1)}, bf16[4,32,256]{2,1,0:T(8,128)(2,1)S(1)}, u32[]{:S(2)}, u32[]{:S(2)}) collective-permute-start(bf16[4,32,256]{2,1,0:T(8,128)(2,1)S(1)} %get-tuple-element.27), channel_id=1, source_target_pairs={{0,2},{2,0},{4,6},{6,4},{8,10},{10,8},{12,14},{14,12},{16,18},{18,... | collective-permute-start | bytes 196616 | tf_op jit(solution)/shard_map/ppermute | solution.py:20
  22.7 3.8 %collective-permute-start.11 = (bf16[4,32,256]{2,1,0:T(8,128)(2,1)S(1)}, bf16[4,32,256]{2,1,0:T(8,128)(2,1)S(1)}, u32[]{:S(2)}, u32[]{:S(2)}) collective-permute-start(bf16[4,32,256]{2,1,0:T(8,128)(2,1)S(1)} %get-tuple-element.28), channel_id=1, source_target_pairs={{0,4},{2,6},{4,0},{6,2},{8,12},{10,14},{12,8},{14,10},{16,20},{18,... | collective-permute-start | bytes 196616 | tf_op jit(solution)/shard_map/ppermute | solution.py:20
  22.9 4.1 %collective-permute-start.12 = (bf16[4,32,256]{2,1,0:T(8,128)(2,1)S(1)}, bf16[4,32,256]{2,1,0:T(8,128)(2,1)S(1)}, u32[]{:S(2)}, u32[]{:S(2)}) collective-permute-start(bf16[4,32,256]{2,1,0:T(8,128)(2,1)S(1)} %get-tuple-element.29), channel_id=1, source_target_pairs={{0,6},{2,4},{4,2},{6,0},{8,14},{10,12},{12,10},{14,8},{16,22},{18,... | collective-permute-start | bytes 196616 | tf_op jit(solution)/shard_map/ppermute | solution.py:20
  26.3 8.7 %collective-permute-start.16 = (bf16[512,256]{1,0:T(8,128)(2,1)S(1)}, bf16[512,256]{1,0:T(8,128)(2,1)S(1)}, u32[]{:S(2)}, u32[]{:S(2)}) collective-permute-start(bf16[512,256]{1,0:T(8,128)(2,1)S(1)} %constant_dynamic-update-slice_fusion.6.refs_3_), channel_id=1, source_target_pairs={{0,6},{2,4},{4,2},{6,0},{8,14},{10,12},{12,10},{14,8},{16,22},{18,... | collective-permute-start | bytes 786440 | tf_op jit(solution)/shard_map/ppermute | solution.py:20
  27.1 5.0 %collective-permute-start.13 = (bf16[4,32,256]{2,1,0:T(8,128)(2,1)S(1)}, bf16[4,32,256]{2,1,0:T(8,128)(2,1)S(1)}, u32[]{:S(2)}, u32[]{:S(2)}) collective-permute-start(bf16[4,32,256]{2,1,0:T(8,128)(2,1)S(1)} %get-tuple-element.44), channel_id=1, source_target_pairs={{0,24},{2,26},{4,28},{6,30},{8,16},{10,18},{12,20},{14,22},{16,8},... | collective-permute-start | bytes 196616 | tf_op jit(solution)/shard_map/ppermute | solution.py:20
  29.1 5.9 %collective-permute-start.14 = (bf16[4,32,256]{2,1,0:T(8,128)(2,1)S(1)}, bf16[4,32,256]{2,1,0:T(8,128)(2,1)S(1)}, u32[]{:S(2)}, u32[]{:S(2)}) collective-permute-start(bf16[4,32,256]{2,1,0:T(8,128)(2,1)S(1)} %get-tuple-element.44), channel_id=1, source_target_pairs={{0,16},{2,18},{4,20},{6,22},{8,24},{10,26},{12,28},{14,30},{16,0},... | collective-permute-start | bytes 196616 | tf_op jit(solution)/shard_map/ppermute | solution.py:20
  29.7 5.4 %collective-permute-start.15 = (bf16[4,32,256]{2,1,0:T(8,128)(2,1)S(1)}, bf16[4,32,256]{2,1,0:T(8,128)(2,1)S(1)}, u32[]{:S(2)}, u32[]{:S(2)}) collective-permute-start(bf16[4,32,256]{2,1,0:T(8,128)(2,1)S(1)} %get-tuple-element.44), channel_id=1, source_target_pairs={{0,8},{2,10},{4,12},{6,14},{8,0},{10,2},{12,4},{14,6},{16,24},{18,... | collective-permute-start | bytes 196616 | tf_op jit(solution)/shard_map/ppermute | solution.py:20
  35.5 3.5 %collective-permute-start.17 = (bf16[2,32,2048]{2,1,0:T(8,128)(2,1)S(1)}, bf16[2,32,2048]{2,1,0:T(8,128)(2,1)S(1)}, u32[]{:S(2)}, u32[]{:S(2)}) collective-permute-start(bf16[2,32,2048]{2,1,0:T(8,128)(2,1)S(1)} %get-tuple-element.43), channel_id=1, source_target_pairs={{0,1},{1,0},{2,3},{3,2},{4,5},{5,4},{6,7},{7,6},{8,9},{9,8},{10,11... | collective-permute-start | bytes 786440 | tf_op jit(solution)/shard_map/ppermute | solution.py:20
  39.1 8.0 %collective-permute-start.18 = (bf16[32,2048]{1,0:T(8,128)(2,1)S(1)}, bf16[32,2048]{1,0:T(8,128)(2,1)S(1)}, u32[]{:S(2)}, u32[]{:S(2)}) collective-permute-start(bf16[32,2048]{1,0:T(8,128)(2,1)S(1)} %get-tuple-element.49), channel_id=1, source_target_pairs={{0,8},{1,16},{2,10},{3,18},{4,12},{5,20},{6,14},{7,22},{8,0},{9,24... | collective-permute-start | bytes 393224 | tf_op jit(solution)/shard_map/ppermute | solution.py:257
  40.3 6.8 %collective-permute-start.19 = (bf16[32,2048]{1,0:T(8,128)(2,1)S(1)}, bf16[32,2048]{1,0:T(8,128)(2,1)S(1)}, u32[]{:S(2)}, u32[]{:S(2)}) collective-permute-start(bf16[32,2048]{1,0:T(8,128)(2,1)S(1)} %get-tuple-element.48), channel_id=1, source_target_pairs={{1,24},{0,2},{3,26},{2,0},{5,28},{4,6},{7,30},{6,4},{9,16},{8,10},... | collective-permute-start | bytes 393224 | tf_op jit(solution)/shard_map/ppermute | solution.py:258

commit v5 on v4

--- a/solution.py
+++ b/solution.py
@@ -25,9 +25,9 @@
     return lax.ppermute(block, ("seq", "kv"), routes)
 
 
-def attention_kernel(line, queries_ref, upstream_ref, *refs):
-    vision_refs, low_ref, vision_ref = refs[:line], refs[line], refs[line + 1]
-    terms_refs, (rows, low, sums) = refs[line + 2 : -3], refs[-3:]
+def attention_kernel(outer, queries_ref, upstream_ref, *refs):
+    vision_refs, low_ref, vision_ref = refs[:outer], refs[outer], refs[outer + 1]
+    terms_refs, (rows, low, sums) = refs[outer + 2 : -3], refs[-3:]
     for d, ref in enumerate(vision_refs):
         vision_ref[d * ref.shape[0] : (d + 1) * ref.shape[0]] = ref[...]
     row_count, width = queries_ref.shape
@@ -51,43 +51,43 @@
         row_dots = jnp.sum(exponent * grad_probs, axis=0, keepdims=True) * inverse
         low[:, at] = (exponent * inverse).astype(BF16)
         low_ref[:, at] = (exponent * (grad_probs - row_dots) * (inverse * scaling)).astype(BF16)
-    _, plane, own, _ = sums.shape
+    _, inner, own, _ = sums.shape
     for i, factor in enumerate((low_ref, low)):
         term = jnp.dot(factor[...], rows[i], preferred_element_type=F32)
-        sums[:, :, :, i * HEAD : (i + 1) * HEAD] = term.reshape(line, plane, own, HEAD)
-    spot = lax.axis_index("seq") // plane
+        sums[:, :, :, i * HEAD : (i + 1) * HEAD] = term.reshape(outer, inner, own, HEAD)
+    spot = lax.axis_index("seq") // outer
     for d, ref in enumerate(terms_refs):
-        for i in range(line):
-            ref[i] = sums[jnp.bitwise_xor(spot, i), d].astype(ref.dtype)
-
-
-def attention_terms(queries, upstream, blocks, plane):
+        for i in range(inner):
+            ref[i] = sums[d, jnp.bitwise_xor(spot, i)].astype(ref.dtype)
+
+
+def attention_terms(queries, upstream, blocks, inner):
     rows, width = queries.shape
-    line = len(blocks)
-    tokens = line * blocks[0].shape[0]
+    outer = len(blocks)
+    tokens = outer * blocks[0].shape[0]
     pairs = rows * width // HEAD
-    own = tokens // (plane * line)
+    own = tokens // (inner * outer)
     low, vision, *terms = pl.pallas_call(
-        functools.partial(attention_kernel, line),
+        functools.partial(attention_kernel, outer),
         out_shape=[
             jax.ShapeDtypeStruct((tokens, pairs), BF16),
             jax.ShapeDtypeStruct((tokens, 2 * HEAD), BF16),
         ]
         + [
-            jax.ShapeDtypeStruct((line, own, 2 * HEAD), BF16 if d else F32) for d in range(plane)
+            jax.ShapeDtypeStruct((inner, own, 2 * HEAD), BF16 if d else F32) for d in range(outer)
         ],
-        in_specs=[IN_VMEM] * (2 + line),
-        out_specs=[IN_VMEM] * (2 + plane),
+        in_specs=[IN_VMEM] * (2 + outer),
+        out_specs=[IN_VMEM] * (2 + outer),
         scratch_shapes=[
             pltpu.VMEM((2, pairs, HEAD), BF16),
             pltpu.VMEM((tokens, pairs), BF16),
-            pltpu.VMEM((line, plane, own, 2 * HEAD), F32),
+            pltpu.VMEM((outer, inner, own, 2 * HEAD), F32),
         ],
         compiler_params=pltpu.CompilerParams(vmem_limit_bytes=48 * 1024 * 1024),
         cost_estimate=pl.CostEstimate(
-            flops=8 * pairs * tokens * HEAD,
+            flops=40 * pairs * tokens * HEAD,
             bytes_accessed=4 * rows * width + 4 * tokens * HEAD,
-            transcendentals=pairs * tokens,
+            transcendentals=5 * pairs * tokens,
         ),
         name="attention_terms",
     )(queries, upstream, *blocks)
@@ -184,9 +184,10 @@
     own = vision_key.shape[0]
     weights = gather_cube(jnp.concatenate([key_weight, value_weight], axis=1), cube)
     pair = jnp.concatenate([vision_key, vision_value], axis=1)
-    block = gather_cube(pair, cube).reshape(cube * own, 2 * HEAD)
-    blocks = [block, exchange(block, "seq", chips, cube)]
-    low, vision, terms = attention_terms(text_query, grad_output, blocks, cube)
+    both = jnp.concatenate([pair, exchange(pair, "seq", chips, cube)], axis=0)
+    blocks = gather_cube(both, cube)
+    blocks = [blocks[d] for d in range(cube)]
+    low, vision, terms = attention_terms(text_query, grad_output, blocks, 2)
     grad_query = query_gradient(low, vision, text_query.shape[0])
     partial = terms[0]
     for d in range(1, cube):
@@ -222,26 +223,26 @@
     own = vision_key.shape[0]
 
     near, far, cross = plane, 2 * plane, 3 * plane
+
     pair = jnp.concatenate([vision_key, vision_value], axis=1)
-    arrived = {d: swap(pair, chips, d) for d in (3, 1, 2, 0)}
-    block = jnp.concatenate([arrived[d] for d in range(plane)], axis=0)
-    blocks = {d: swap(block, chips, d) for d in (cross, far, near, 0)}
+    arrived = {d: swap(pair, chips, d) for d in (cross, far, near, 0)}
+    block = jnp.concatenate([arrived[d] for d in (0, near, far, cross)], axis=0)
+    blocks = {d: swap(block, chips, d) for d in (3, 1, 2, 0)}
     weight = jnp.concatenate([key_weight, value_weight], axis=1)
     weights = [weight] + [exchange(weight, "seq", chips, d) for d in (1, 2)]
     low, vision, terms = attention_terms(
-        text_query, grad_output, [blocks[d] for d in (0, near, far, cross)], plane
+        text_query, grad_output, [blocks[d] for d in range(plane)], line
     )
-    terms, weights = lax.optimization_barrier((terms, weights))
     grad_query = query_gradient(low, vision, text_query.shape[0])
-    weight, grad_query = lax.optimization_barrier((weights[0], grad_query))
+    weight, grad_query = lax.optimization_barrier((weight, grad_query))
     weights += [exchange(weight, "seq", chips, d) for d in range(3, plane)]
 
     arrived = [exchange(terms[d], "seq", chips, d) for d in range(1, plane)]
-    arrived, grad_query = lax.optimization_barrier((arrived, grad_query))
+    arrived, grad_query, weights[1:3] = lax.optimization_barrier((arrived, grad_query, weights[1:3]))
     sums = terms[0]
     for block in arrived:
         sums = sums + block.astype(F32)
-    arrived = [exchange(sums.astype(BF16), "seq", chips, d) for d in (cross, far, near)]
+    arrived = [exchange(sums.astype(BF16), "seq", chips, d) for d in (far, cross, near)]
     keep, send = project(sums, arrived, weights)
     total = (keep + exchange(send, "kv", 2, 1).astype(F32)).astype(BF16)
     stay, go = total[0], total[1]

time: 48.1 us -> 47.6 us (0.990)
  starting transfers between devices: 23.5 us -> 20.3 us
  waiting for transfers between devices: 17 us -> 19.7 us
    ppermute x10, starting transfers between devices: 11.5 us -> 8.84 us  [exchange(): return lax.ppermute(block, axis, [(i, i ^ distance) for i in range(size)])]
    ppermute x10, waiting for transfers between devices: 6.07 us -> 8.12 us  [exchange(): return lax.ppermute(block, axis, [(i, i ^ distance) for i in range(size)])]
    ppermute x8, starting transfers between devices: 9.54 us -> 8.79 us  [swap(): return lax.ppermute(block, ('seq', 'kv'), routes)]
    ppermute x8, waiting for transfers between devices: 5.45 us -> 6.13 us  [swap(): return lax.ppermute(block, ('seq', 'kv'), routes)]
  transfers between devices with their start and end apart: 20 -> 20, of which waited for: 8 -> 11; matrix products, arithmetic and copies ran while one was open for 2% -> 2% of each run, Pallas kernels for 7% -> 7%
where the time goes in v5:
time: 47.6 us; the launch traced here: 47.3 us
  starting transfers between devices  20.3 us (43%)
  waiting for transfers between devices  19.7 us (41%)
  Pallas kernels  3.91 us (8%)
  local copies, waits for them, and re-layouts  1.76 us (4%)
  other arithmetic  0.83 us (2%)
  between operations  0.75 us (2%)
    ppermute x10, starting transfers between devices, exchange(): return lax.ppermute(block, axis, [(i, i ^ distance) for i in range(size)])  8.84 us
    ppermute x8, starting transfers between devices, swap(): return lax.ppermute(block, ('seq', 'kv'), routes)  8.79 us
    ppermute x10, waiting for transfers between devices, exchange(): return lax.ppermute(block, axis, [(i, i ^ distance) for i in range(size)])  8.12 us
    ppermute x8, waiting for transfers between devices, swap(): return lax.ppermute(block, ('seq', 'kv'), routes)  6.13 us
    ppermute x1, waiting for transfers between devices, two_cores(): first = lax.ppermute(go, ('seq', 'kv'), routes_a)  5.45 us
    pallas_call x1, Pallas kernels, attention_terms(): pl.pallas_call(functools.partial(attention_kernel, outer), out_shape=[jax...  2.24 us
    unnamed x13, local copies, waits for them, and re-layouts  1.7 us
    ppermute x1, starting transfers between devices, two_cores(): first = lax.ppermute(go, ('seq', 'kv'), routes_a)  1.36 us
  transfers between devices with their start and end apart: 20, of which 11 were waited for; matrix products, arithmetic and copies ran while one was open for 2% of the time, Pallas kernels for 7%

profile of v5, /device:TPU:1, one launch (start us, length us, event | category | flops | bytes accessed | tf_op | source)
XLA Modules:
  0.0 47.3 jit_solution(12504947914484069853)
XLA Ops:
  1.5 2.7 %collective-permute-start.1 = (bf16[32,256]{1,0:T(8,128)(2,1)S(1)}, bf16[32,256]{1,0:T(8,128)(2,1)S(1)}, u32[]{:S(2)}, u32[]{:S(2)}) collective-permute-start(bf16[32,256]{1,0:T(8,128)(2,1)S(1)} %constant_dynamic-update-slice_fusion), channel_id=1, source_target_pairs={{0,9},{1,8},{2,11},{3,10},{4,13},{5,12},{6,15},{7,14},{8,1},{9,0},... | collective-permute-start | bytes 49160 | tf_op jit(solution)/shard_map/ppermute | solution.py:25
  4.2 2.6 %collective-permute-start.2 = (bf16[32,256]{1,0:T(8,128)(2,1)S(1)}, bf16[32,256]{1,0:T(8,128)(2,1)S(1)}, u32[]{:S(2)}, u32[]{:S(2)}) collective-permute-start(bf16[32,256]{1,0:T(8,128)(2,1)S(1)} %constant_dynamic-update-slice_fusion), channel_id=1, source_target_pairs={{0,17},{1,16},{2,19},{3,18},{4,21},{5,20},{6,23},{7,22},{8,25},{9,... | collective-permute-start | bytes 49160 | tf_op jit(solution)/shard_map/ppermute | solution.py:25
  6.8 1.0 %constant_dynamic-update-slice_fusion.7 = bf16[512,256]{1,0:T(8,128)(2,1)S(1)} fusion(bf16[512,128]{1,0:T(8,128)(2,1)} %param.10), kind=kLoop, calls=%fused_computation.16 | loop fusion | bytes 262144
  8.4 3.4 %collective-permute-done.3 = bf16[32,256]{1,0:T(8,128)(2,1)S(1)} collective-permute-done((bf16[32,256]{1,0:T(8,128)(2,1)S(1)}, bf16[32,256]{1,0:T(8,128)(2,1)S(1)}, u32[]{:S(2)}, u32[]{:S(2)}) %collective-permute-start.3) | collective-permute-done | bytes 16416 | tf_op jit(solution)/shard_map/ppermute | solution.py:25
  11.9 1.5 %collective-permute-start.5 = (bf16[128,256]{1,0:T(8,128)(2,1)S(1)}, bf16[128,256]{1,0:T(8,128)(2,1)S(1)}, u32[]{:S(2)}, u32[]{:S(2)}) collective-permute-start(bf16[128,256]{1,0:T(8,128)(2,1)S(1)} %constant_dynamic-update-slice_fusion.2), channel_id=1, source_target_pairs={{0,3},{1,2},{2,1},{3,0},{4,7},{5,6},{6,5},{7,4},{8,11},{9,10},{10,... | collective-permute-start | bytes 196616 | tf_op jit(solution)/shard_map/ppermute | solution.py:25
  13.4 1.2 %collective-permute-start.6 = (bf16[128,256]{1,0:T(8,128)(2,1)S(1)}, bf16[128,256]{1,0:T(8,128)(2,1)S(1)}, u32[]{:S(2)}, u32[]{:S(2)}) collective-permute-start(bf16[128,256]{1,0:T(8,128)(2,1)S(1)} %constant_dynamic-update-slice_fusion.2), channel_id=1, source_target_pairs={{0,5},{1,4},{2,7},{3,6},{4,1},{5,0},{6,3},{7,2},{8,13},{9,12},{10,... | collective-permute-start | bytes 196616 | tf_op jit(solution)/shard_map/ppermute | solution.py:25
  15.2 1.3 %collective-permute-start.11 = (bf16[512,256]{1,0:T(8,128)(2,1)S(1)}, bf16[512,256]{1,0:T(8,128)(2,1)S(1)}, u32[]{:S(2)}, u32[]{:S(2)}) collective-permute-start(bf16[512,256]{1,0:T(8,128)(2,1)S(1)} %constant_dynamic-update-slice_fusion.6.refs_3_), channel_id=1, source_target_pairs={{0,2},{2,0},{4,6},{6,4},{8,10},{10,8},{12,14},{14,12},{16,18},{18,... | collective-permute-start | bytes 786440 | tf_op jit(solution)/shard_map/ppermute | solution.py:20
  16.4 1.2 %collective-permute-start.12 = (bf16[512,256]{1,0:T(8,128)(2,1)S(1)}, bf16[512,256]{1,0:T(8,128)(2,1)S(1)}, u32[]{:S(2)}, u32[]{:S(2)}) collective-permute-start(bf16[512,256]{1,0:T(8,128)(2,1)S(1)} %constant_dynamic-update-slice_fusion.6.refs_3_), channel_id=1, source_target_pairs={{0,4},{2,6},{4,0},{6,2},{8,12},{10,14},{12,8},{14,10},{16,20},{18,... | collective-permute-start | bytes 786440 | tf_op jit(solution)/shard_map/ppermute | solution.py:20
  17.7 2.2 %collective-permute-done.7.refs_3_ = bf16[128,256]{1,0:T(8,128)(2,1)S(1)} collective-permute-done((bf16[128,256]{1,0:T(8,128)(2,1)S(1)}, bf16[128,256]{1,0:T(8,128)(2,1)S(1)}, u32[]{:S(2)}, u32[]{:S(2)}) %collective-permute-start.7) | collective-permute-done | bytes 65568 | tf_op jit(solution)/shard_map/ppermute | solution.py:25
  19.9 2.2 %attention_terms.1 = (bf16[512,1024]{1,0:T(8,128)(2,1)S(1)}, bf16[512,256]{1,0:T(8,128)(2,1)S(1)}, f32[4,32,256]{2,1,0:T(8,128)S(1)}, bf16[4,32,256]{2,1,0:T(8,1...) custom-call(bf16[128,1024]{1,0:T(8,128)(2,1)S(1)} %copy-done, ...), custom_call_target="tpu_custom_call" | custom-call | flops 2684354560 | bytes 786432 | tf_op jit(solution)/shard_map/attention_terms/pallas_call | solution.py:70
  22.2 1.4 %collective-permute-start.8 = (bf16[4,32,256]{2,1,0:T(8,128)(2,1)S(1)}, bf16[4,32,256]{2,1,0:T(8,128)(2,1)S(1)}, u32[]{:S(2)}, u32[]{:S(2)}) collective-permute-start(bf16[4,32,256]{2,1,0:T(8,128)(2,1)S(1)} %get-tuple-element.18), channel_id=1, source_target_pairs={{0,2},{2,0},{4,6},{6,4},{8,10},{10,8},{12,14},{14,12},{16,18},{18,... | collective-permute-start | bytes 196616 | tf_op jit(solution)/shard_map/ppermute | solution.py:20
  23.6 1.2 %collective-permute-start.9 = (bf16[4,32,256]{2,1,0:T(8,128)(2,1)S(1)}, bf16[4,32,256]{2,1,0:T(8,128)(2,1)S(1)}, u32[]{:S(2)}, u32[]{:S(2)}) collective-permute-start(bf16[4,32,256]{2,1,0:T(8,128)(2,1)S(1)} %get-tuple-element.19), channel_id=1, source_target_pairs={{0,4},{2,6},{4,0},{6,2},{8,12},{10,14},{12,8},{14,10},{16,20},{18,... | collective-permute-start | bytes 196616 | tf_op jit(solution)/shard_map/ppermute | solution.py:20
  24.9 1.2 %query_gradient.1 = bf16[128,1024]{1,0:T(8,128)(2,1)} custom-call(bf16[512,1024]{1,0:T(8,128)(2,1)S(1)} %get-tuple-element.21.low_ref, bf16[512,256]{1,0:T(8,128)(2,1)S(1)} %get-tuple-element.22.vision_ref), custom_call_target="tpu_custom_call" | custom-call | flops 134217728 | bytes 262144 | tf_op jit(solution)/shard_map/query_gradient/pallas_call | solution.py:108
  27.0 1.0 %collective-permute-done.9 = bf16[4,32,256]{2,1,0:T(8,128)(2,1)S(1)} collective-permute-done((bf16[4,32,256]{2,1,0:T(8,128)(2,1)S(1)}, bf16[4,32,256]{2,1,0:T(8,128)(2,1)S(1)}, u32[]{:S(2)}, u32[]{:S(2)}) %collective-permute-start.9) | collective-permute-done | bytes 65568 | tf_op jit(solution)/shard_map/ppermute | solution.py:20
  28.2 0.7 %collective-permute-start.14 = (bf16[4,32,256]{2,1,0:T(8,128)(2,1)S(1)}, bf16[4,32,256]{2,1,0:T(8,128)(2,1)S(1)}, u32[]{:S(2)}, u32[]{:S(2)}) collective-permute-start(bf16[4,32,256]{2,1,0:T(8,128)(2,1)S(1)} %get-tuple-element.34), channel_id=1, source_target_pairs={{0,24},{2,26},{4,28},{6,30},{8,16},{10,18},{12,20},{14,22},{16,8},... | collective-permute-start | bytes 196616 | tf_op jit(solution)/shard_map/ppermute | solution.py:20
  28.9 1.9 %collective-permute-start.15 = (bf16[4,32,256]{2,1,0:T(8,128)(2,1)S(1)}, bf16[4,32,256]{2,1,0:T(8,128)(2,1)S(1)}, u32[]{:S(2)}, u32[]{:S(2)}) collective-permute-start(bf16[4,32,256]{2,1,0:T(8,128)(2,1)S(1)} %get-tuple-element.34), channel_id=1, source_target_pairs={{0,8},{2,10},{4,12},{6,14},{8,0},{10,2},{12,4},{14,6},{16,24},{18,... | collective-permute-start | bytes 196616 | tf_op jit(solution)/shard_map/ppermute | solution.py:20
  30.8 1.8 %collective-permute-done.13.refs_0_ = bf16[4,32,256]{2,1,0:T(8,128)(2,1)S(1)} collective-permute-done((bf16[4,32,256]{2,1,0:T(8,128)(2,1)S(1)}, bf16[4,32,256]{2,1,0:T(8,128)(2,1)S(1)}, u32[]{:S(2)}, u32[]{:S(2)}) %collective-permute-start.13) | collective-permute-done | bytes 65568 | tf_op jit(solution)/shard_map/ppermute | solution.py:20
  33.4 2.5 %collective-permute-done.15.refs_2_ = bf16[4,32,256]{2,1,0:T(8,128)(2,1)S(1)} collective-permute-done((bf16[4,32,256]{2,1,0:T(8,128)(2,1)S(1)}, bf16[4,32,256]{2,1,0:T(8,128)(2,1)S(1)}, u32[]{:S(2)}, u32[]{:S(2)}) %collective-permute-start.15) | collective-permute-done | bytes 65568 | tf_op jit(solution)/shard_map/ppermute | solution.py:20
  36.4 0.8 %collective-permute-start.17 = (bf16[2,32,2048]{2,1,0:T(8,128)(2,1)S(1)}, bf16[2,32,2048]{2,1,0:T(8,128)(2,1)S(1)}, u32[]{:S(2)}, u32[]{:S(2)}) collective-permute-start(bf16[2,32,2048]{2,1,0:T(8,128)(2,1)S(1)} %get-tuple-element.33), channel_id=1, source_target_pairs={{0,1},{1,0},{2,3},{3,2},{4,5},{5,4},{6,7},{7,6},{8,9},{9,8},{10,11... | collective-permute-start | bytes 786440 | tf_op jit(solution)/shard_map/ppermute | solution.py:20
  37.1 1.2 %collective-permute-done.17 = bf16[2,32,2048]{2,1,0:T(8,128)(2,1)S(1)} collective-permute-done((bf16[2,32,2048]{2,1,0:T(8,128)(2,1)S(1)}, bf16[2,32,2048]{2,1,0:T(8,128)(2,1)S(1)}, u32[]{:S(2)}, u32[]{:S(2)}) %collective-permute-start.17) | collective-permute-done | bytes 262176 | tf_op jit(solution)/shard_map/ppermute | solution.py:20
  38.4 1.4 %collective-permute-start.18 = (bf16[32,2048]{1,0:T(8,128)(2,1)S(1)}, bf16[32,2048]{1,0:T(8,128)(2,1)S(1)}, u32[]{:S(2)}, u32[]{:S(2)}) collective-permute-start(bf16[32,2048]{1,0:T(8,128)(2,1)S(1)} %get-tuple-element.39), channel_id=1, source_target_pairs={{0,8},{1,16},{2,10},{3,18},{4,12},{5,20},{6,14},{7,22},{8,0},{9,24... | collective-permute-start | bytes 393224 | tf_op jit(solution)/shard_map/ppermute | solution.py:258
  39.8 1.4 %collective-permute-start.19 = (bf16[32,2048]{1,0:T(8,128)(2,1)S(1)}, bf16[32,2048]{1,0:T(8,128)(2,1)S(1)}, u32[]{:S(2)}, u32[]{:S(2)}) collective-permute-start(bf16[32,2048]{1,0:T(8,128)(2,1)S(1)} %get-tuple-element.38), channel_id=1, source_target_pairs={{1,24},{0,2},{3,26},{2,0},{5,28},{4,6},{7,30},{6,4},{9,16},{8,10},... | collective-permute-start | bytes 393224 | tf_op jit(solution)/shard_map/ppermute | solution.py:259
  41.1 5.5 %collective-permute-done.18 = bf16[32,2048]{1,0:T(8,128)(2,1)S(1)} collective-permute-done((bf16[32,2048]{1,0:T(8,128)(2,1)S(1)}, bf16[32,2048]{1,0:T(8,128)(2,1)S(1)}, u32[]{:S(2)}, u32[]{:S(2)}) %collective-permute-start.18) | collective-permute-done | bytes 131104 | tf_op jit(solution)/shard_map/ppermute | solution.py:258
  46.6 0.7 %pad_maximum_fusion = bf16[32,4096]{1,0:T(8,128)(2,1)} fusion(bf16[32,2048]{1,0:T(8,128)(2,1)S(1)} %get-tuple-element.37, bf16[32,2048]{1,0:T(8,128)(2,1)S(1)} %get-tuple-element.36), kind=kLoop, calls=%fused_computation.1 | loop fusion | flops 524288 | bytes 524288 | tf_op jit(solution)/shard_map/concatenate | solution.py:263
  (40 shorter events, 4.5 us)
Async XLA Ops:
  0.6 0.7 %copy-start.3 = (bf16[32,128]{1,0:T(8,128)(2,1)S(1)}, bf16[32,128]{1,0:T(8,128)(2,1)}, u32[]{:S(2)}) copy-start(bf16[32,128]{1,0:T(8,128)(2,1)} %param.8) | copy-start | bytes 24580
  1.3 13.8 %copy-start.2 = (bf16[512,128]{1,0:T(8,128)(2,1)S(1)}, bf16[512,128]{1,0:T(8,128)(2,1)}, u32[]{:S(2)}) copy-start(bf16[512,128]{1,0:T(8,128)(2,1)} %param.11) | copy-start | bytes 393220
  1.4 6.5 %collective-permute-start = (bf16[32,256]{1,0:T(8,128)(2,1)S(1)}, bf16[32,256]{1,0:T(8,128)(2,1)S(1)}, u32[]{:S(2)}, u32[]{:S(2)}) collective-permute-start(bf16[32,256]{1,0:T(8,128)(2,1)S(1)} %constant_dynamic-update-slice_fusion), channel_id=1, source_target_pairs={{0,1},{1,0},{2,3},{3,2},{4,5},{5,4},{6,7},{7,6},{8,9},{9,8},{10,11... | collective-permute-start | bytes 49160 | tf_op jit(solution)/shard_map/ppermute | solution.py:25
  1.5 6.4 %collective-permute-start.1 = (bf16[32,256]{1,0:T(8,128)(2,1)S(1)}, bf16[32,256]{1,0:T(8,128)(2,1)S(1)}, u32[]{:S(2)}, u32[]{:S(2)}) collective-permute-start(bf16[32,256]{1,0:T(8,128)(2,1)S(1)} %constant_dynamic-update-slice_fusion), channel_id=1, source_target_pairs={{0,9},{1,8},{2,11},{3,10},{4,13},{5,12},{6,15},{7,14},{8,1},{9,0},... | collective-permute-start | bytes 49160 | tf_op jit(solution)/shard_map/ppermute | solution.py:25
  4.2 4.2 %collective-permute-start.2 = (bf16[32,256]{1,0:T(8,128)(2,1)S(1)}, bf16[32,256]{1,0:T(8,128)(2,1)S(1)}, u32[]{:S(2)}, u32[]{:S(2)}) collective-permute-start(bf16[32,256]{1,0:T(8,128)(2,1)S(1)} %constant_dynamic-update-slice_fusion), channel_id=1, source_target_pairs={{0,17},{1,16},{2,19},{3,18},{4,21},{5,20},{6,23},{7,22},{8,25},{9,... | collective-permute-start | bytes 49160 | tf_op jit(solution)/shard_map/ppermute | solution.py:25
  6.8 5.0 %collective-permute-start.3 = (bf16[32,256]{1,0:T(8,128)(2,1)S(1)}, bf16[32,256]{1,0:T(8,128)(2,1)S(1)}, u32[]{:S(2)}, u32[]{:S(2)}) collective-permute-start(bf16[32,256]{1,0:T(8,128)(2,1)S(1)} %constant_dynamic-update-slice_fusion), channel_id=1, source_target_pairs={{0,25},{1,24},{2,27},{3,26},{4,29},{5,28},{6,31},{7,30},{8,17},{9,... | collective-permute-start | bytes 49160 | tf_op jit(solution)/shard_map/ppermute | solution.py:25
  6.8 13.1 %copy-start.1 = (bf16[128,1024]{1,0:T(8,128)(2,1)S(1)}, bf16[128,1024]{1,0:T(8,128)(2,1)}, u32[]{:S(2)}) copy-start(bf16[128,1024]{1,0:T(8,128)(2,1)} %upstream_ref.1) | copy-start | bytes 786436
  7.8 12.1 %copy-start = (bf16[128,1024]{1,0:T(8,128)(2,1)S(1)}, bf16[128,1024]{1,0:T(8,128)(2,1)}, u32[]{:S(2)}) copy-start(bf16[128,1024]{1,0:T(8,128)(2,1)} %queries_ref.1) | copy-start | bytes 786436
  11.8 4.6 %collective-permute-start.4 = (bf16[128,256]{1,0:T(8,128)(2,1)S(1)}, bf16[128,256]{1,0:T(8,128)(2,1)S(1)}, u32[]{:S(2)}, u32[]{:S(2)}) collective-permute-start(bf16[128,256]{1,0:T(8,128)(2,1)S(1)} %constant_dynamic-update-slice_fusion.2), channel_id=1, source_target_pairs={{0,1},{1,0},{2,3},{3,2},{4,5},{5,4},{6,7},{7,6},{8,9},{9,8},{10,11... | collective-permute-start | bytes 196616 | tf_op jit(solution)/shard_map/ppermute | solution.py:25
  11.9 5.8 %collective-permute-start.5 = (bf16[128,256]{1,0:T(8,128)(2,1)S(1)}, bf16[128,256]{1,0:T(8,128)(2,1)S(1)}, u32[]{:S(2)}, u32[]{:S(2)}) collective-permute-start(bf16[128,256]{1,0:T(8,128)(2,1)S(1)} %constant_dynamic-update-slice_fusion.2), channel_id=1, source_target_pairs={{0,3},{1,2},{2,1},{3,0},{4,7},{5,6},{6,5},{7,4},{8,11},{9,10},{10,... | collective-permute-start | bytes 196616 | tf_op jit(solution)/shard_map/ppermute | solution.py:25
  13.4 4.3 %collective-permute-start.6 = (bf16[128,256]{1,0:T(8,128)(2,1)S(1)}, bf16[128,256]{1,0:T(8,128)(2,1)S(1)}, u32[]{:S(2)}, u32[]{:S(2)}) collective-permute-start(bf16[128,256]{1,0:T(8,128)(2,1)S(1)} %constant_dynamic-update-slice_fusion.2), channel_id=1, source_target_pairs={{0,5},{1,4},{2,7},{3,6},{4,1},{5,0},{6,3},{7,2},{8,13},{9,12},{10,... | collective-permute-start | bytes 196616 | tf_op jit(solution)/shard_map/ppermute | solution.py:25
  14.6 5.3 %collective-permute-start.7 = (bf16[128,256]{1,0:T(8,128)(2,1)S(1)}, bf16[128,256]{1,0:T(8,128)(2,1)S(1)}, u32[]{:S(2)}, u32[]{:S(2)}) collective-permute-start(bf16[128,256]{1,0:T(8,128)(2,1)S(1)} %constant_dynamic-update-slice_fusion.2), channel_id=1, source_target_pairs={{0,7},{1,6},{2,5},{3,4},{4,3},{5,2},{6,1},{7,0},{8,15},{9,14},{10,... | collective-permute-start | bytes 196616 | tf_op jit(solution)/shard_map/ppermute | solution.py:25
  15.2 12.9 %collective-permute-start.11 = (bf16[512,256]{1,0:T(8,128)(2,1)S(1)}, bf16[512,256]{1,0:T(8,128)(2,1)S(1)}, u32[]{:S(2)}, u32[]{:S(2)}) collective-permute-start(bf16[512,256]{1,0:T(8,128)(2,1)S(1)} %constant_dynamic-update-slice_fusion.6.refs_3_), channel_id=1, source_target_pairs={{0,2},{2,0},{4,6},{6,4},{8,10},{10,8},{12,14},{14,12},{16,18},{18,... | collective-permute-start | bytes 786440 | tf_op jit(solution)/shard_map/ppermute | solution.py:20
  16.4 11.7 %collective-permute-start.12 = (bf16[512,256]{1,0:T(8,128)(2,1)S(1)}, bf16[512,256]{1,0:T(8,128)(2,1)S(1)}, u32[]{:S(2)}, u32[]{:S(2)}) collective-permute-start(bf16[512,256]{1,0:T(8,128)(2,1)S(1)} %constant_dynamic-update-slice_fusion.6.refs_3_), channel_id=1, source_target_pairs={{0,4},{2,6},{4,0},{6,2},{8,12},{10,14},{12,8},{14,10},{16,20},{18,... | collective-permute-start | bytes 786440 | tf_op jit(solution)/shard_map/ppermute | solution.py:20
  22.1 4.1 %collective-permute-start.10 = (bf16[4,32,256]{2,1,0:T(8,128)(2,1)S(1)}, bf16[4,32,256]{2,1,0:T(8,128)(2,1)S(1)}, u32[]{:S(2)}, u32[]{:S(2)}) collective-permute-start(bf16[4,32,256]{2,1,0:T(8,128)(2,1)S(1)} %get-tuple-element.20), channel_id=1, source_target_pairs={{0,6},{2,4},{4,2},{6,0},{8,14},{10,12},{12,10},{14,8},{16,22},{18,... | collective-permute-start | bytes 196616 | tf_op jit(solution)/shard_map/ppermute | solution.py:20
  22.2 4.8 %collective-permute-start.8 = (bf16[4,32,256]{2,1,0:T(8,128)(2,1)S(1)}, bf16[4,32,256]{2,1,0:T(8,128)(2,1)S(1)}, u32[]{:S(2)}, u32[]{:S(2)}) collective-permute-start(bf16[4,32,256]{2,1,0:T(8,128)(2,1)S(1)} %get-tuple-element.18), channel_id=1, source_target_pairs={{0,2},{2,0},{4,6},{6,4},{8,10},{10,8},{12,14},{14,12},{16,18},{18,... | collective-permute-start | bytes 196616 | tf_op jit(solution)/shard_map/ppermute | solution.py:20
  23.6 4.5 %collective-permute-start.9 = (bf16[4,32,256]{2,1,0:T(8,128)(2,1)S(1)}, bf16[4,32,256]{2,1,0:T(8,128)(2,1)S(1)}, u32[]{:S(2)}, u32[]{:S(2)}) collective-permute-start(bf16[4,32,256]{2,1,0:T(8,128)(2,1)S(1)} %get-tuple-element.19), channel_id=1, source_target_pairs={{0,4},{2,6},{4,0},{6,2},{8,12},{10,14},{12,8},{14,10},{16,20},{18,... | collective-permute-start | bytes 196616 | tf_op jit(solution)/shard_map/ppermute | solution.py:20
  26.2 9.7 %collective-permute-start.16 = (bf16[512,256]{1,0:T(8,128)(2,1)S(1)}, bf16[512,256]{1,0:T(8,128)(2,1)S(1)}, u32[]{:S(2)}, u32[]{:S(2)}) collective-permute-start(bf16[512,256]{1,0:T(8,128)(2,1)S(1)} %constant_dynamic-update-slice_fusion.6.refs_3_), channel_id=1, source_target_pairs={{0,6},{2,4},{4,2},{6,0},{8,14},{10,12},{12,10},{14,8},{16,22},{18,... | collective-permute-start | bytes 786440 | tf_op jit(solution)/shard_map/ppermute | solution.py:20
  28.1 4.6 %collective-permute-start.13 = (bf16[4,32,256]{2,1,0:T(8,128)(2,1)S(1)}, bf16[4,32,256]{2,1,0:T(8,128)(2,1)S(1)}, u32[]{:S(2)}, u32[]{:S(2)}) collective-permute-start(bf16[4,32,256]{2,1,0:T(8,128)(2,1)S(1)} %get-tuple-element.34), channel_id=1, source_target_pairs={{0,16},{2,18},{4,20},{6,22},{8,24},{10,26},{12,28},{14,30},{16,0},... | collective-permute-start | bytes 196616 | tf_op jit(solution)/shard_map/ppermute | solution.py:20
  28.2 5.1 %collective-permute-start.14 = (bf16[4,32,256]{2,1,0:T(8,128)(2,1)S(1)}, bf16[4,32,256]{2,1,0:T(8,128)(2,1)S(1)}, u32[]{:S(2)}, u32[]{:S(2)}) collective-permute-start(bf16[4,32,256]{2,1,0:T(8,128)(2,1)S(1)} %get-tuple-element.34), channel_id=1, source_target_pairs={{0,24},{2,26},{4,28},{6,30},{8,16},{10,18},{12,20},{14,22},{16,8},... | collective-permute-start | bytes 196616 | tf_op jit(solution)/shard_map/ppermute | solution.py:20
  28.9 7.0 %collective-permute-start.15 = (bf16[4,32,256]{2,1,0:T(8,128)(2,1)S(1)}, bf16[4,32,256]{2,1,0:T(8,128)(2,1)S(1)}, u32[]{:S(2)}, u32[]{:S(2)}) collective-permute-start(bf16[4,32,256]{2,1,0:T(8,128)(2,1)S(1)} %get-tuple-element.34), channel_id=1, source_target_pairs={{0,8},{2,10},{4,12},{6,14},{8,0},{10,2},{12,4},{14,6},{16,24},{18,... | collective-permute-start | bytes 196616 | tf_op jit(solution)/shard_map/ppermute | solution.py:20
  36.4 1.9 %collective-permute-start.17 = (bf16[2,32,2048]{2,1,0:T(8,128)(2,1)S(1)}, bf16[2,32,2048]{2,1,0:T(8,128)(2,1)S(1)}, u32[]{:S(2)}, u32[]{:S(2)}) collective-permute-start(bf16[2,32,2048]{2,1,0:T(8,128)(2,1)S(1)} %get-tuple-element.33), channel_id=1, source_target_pairs={{0,1},{1,0},{2,3},{3,2},{4,5},{5,4},{6,7},{7,6},{8,9},{9,8},{10,11... | collective-permute-start | bytes 786440 | tf_op jit(solution)/shard_map/ppermute | solution.py:20
  38.4 8.2 %collective-permute-start.18 = (bf16[32,2048]{1,0:T(8,128)(2,1)S(1)}, bf16[32,2048]{1,0:T(8,128)(2,1)S(1)}, u32[]{:S(2)}, u32[]{:S(2)}) collective-permute-start(bf16[32,2048]{1,0:T(8,128)(2,1)S(1)} %get-tuple-element.39), channel_id=1, source_target_pairs={{0,8},{1,16},{2,10},{3,18},{4,12},{5,20},{6,14},{7,22},{8,0},{9,24... | collective-permute-start | bytes 393224 | tf_op jit(solution)/shard_map/ppermute | solution.py:258
  39.8 6.8 %collective-permute-start.19 = (bf16[32,2048]{1,0:T(8,128)(2,1)S(1)}, bf16[32,2048]{1,0:T(8,128)(2,1)S(1)}, u32[]{:S(2)}, u32[]{:S(2)}) collective-permute-start(bf16[32,2048]{1,0:T(8,128)(2,1)S(1)} %get-tuple-element.38), channel_id=1, source_target_pairs={{1,24},{0,2},{3,26},{2,0},{5,28},{4,6},{7,30},{6,4},{9,16},{8,10},... | collective-permute-start | bytes 393224 | tf_op jit(solution)/shard_map/ppermute | solution.py:259

commit v6 on v5

--- a/solution.py
+++ b/solution.py
@@ -58,7 +58,7 @@
     spot = lax.axis_index("seq") // outer
     for d, ref in enumerate(terms_refs):
         for i in range(inner):
-            ref[i] = sums[d, jnp.bitwise_xor(spot, i)].astype(ref.dtype)
+            ref[i] = sums[outer - 1 - d, jnp.bitwise_xor(spot, i)].astype(ref.dtype)
 
 
 def attention_terms(queries, upstream, blocks, inner):
@@ -186,7 +186,7 @@
     pair = jnp.concatenate([vision_key, vision_value], axis=1)
     both = jnp.concatenate([pair, exchange(pair, "seq", chips, cube)], axis=0)
     blocks = gather_cube(both, cube)
-    blocks = [blocks[d] for d in range(cube)]
+    blocks = [blocks[d] for d in reversed(range(cube))]
     low, vision, terms = attention_terms(text_query, grad_output, blocks, 2)
     grad_query = query_gradient(low, vision, text_query.shape[0])
     partial = terms[0]
@@ -231,7 +231,7 @@
     weight = jnp.concatenate([key_weight, value_weight], axis=1)
     weights = [weight] + [exchange(weight, "seq", chips, d) for d in (1, 2)]
     low, vision, terms = attention_terms(
-        text_query, grad_output, [blocks[d] for d in range(plane)], line
+        text_query, grad_output, [blocks[d] for d in reversed(range(plane))], line
     )
     grad_query = query_gradient(low, vision, text_query.shape[0])
     weight, grad_query = lax.optimization_barrier((weight, grad_query))
@@ -255,8 +255,8 @@
         routes_b.append((2 * u + 1 - home, 2 * (u ^ cross) + home))
         routes_b.append((2 * u + home, 2 * (u ^ 1) + home))
     at_home = core == me // far
+    second = lax.ppermute(stay, ("seq", "kv"), routes_b)
     first = lax.ppermute(go, ("seq", "kv"), routes_a)
-    second = lax.ppermute(stay, ("seq", "kv"), routes_b)
     same = jnp.where(at_home, stay, first)
     other = jnp.where(at_home, first, second)
     upper = (me // near) % 2 == 1

time: 47.6 us -> 46.9 us (0.985)
  waiting for transfers between devices: 19.7 us -> 18.5 us
  starting transfers between devices: 20.3 us -> 20.8 us
    ppermute x8, waiting for transfers between devices: 6.13 us -> 4.97 us  [swap(): return lax.ppermute(block, ('seq', 'kv'), routes)]
    ppermute x10, starting transfers between devices: 8.84 us -> 9.33 us  [exchange(): return lax.ppermute(block, axis, [(i, i ^ distance) for i in range(size)])]
where the time goes in v6:
time: 46.9 us; the launch traced here: 46.6 us
  starting transfers between devices  20.8 us (44%)
  waiting for transfers between devices  18.5 us (39%)
  Pallas kernels  3.92 us (8%)
  local copies, waits for them, and re-layouts  1.76 us (4%)
  other arithmetic  0.83 us (2%)
  between operations  0.76 us (2%)
    ppermute x10, starting transfers between devices, exchange(): return lax.ppermute(block, axis, [(i, i ^ distance) for i in range(size)])  9.33 us
    ppermute x8, starting transfers between devices, swap(): return lax.ppermute(block, ('seq', 'kv'), routes)  8.79 us
    ppermute x10, waiting for transfers between devices, exchange(): return lax.ppermute(block, axis, [(i, i ^ distance) for i in range(size)])  8.1 us
    ppermute x1, waiting for transfers between devices, two_cores(): first = lax.ppermute(go, ('seq', 'kv'), routes_a)  5.46 us
    ppermute x8, waiting for transfers between devices, swap(): return lax.ppermute(block, ('seq', 'kv'), routes)  4.97 us
    pallas_call x1, Pallas kernels, attention_terms(): pl.pallas_call(functools.partial(attention_kernel, outer), out_shape=[jax...  2.25 us
    ppermute x1, starting transfers between devices, two_cores(): second = lax.ppermute(stay, ('seq', 'kv'), routes_b)  1.78 us
    unnamed x13, local copies, waits for them, and re-layouts  1.7 us
  transfers between devices with their start and end apart: 20, of which 11 were waited for; matrix products, arithmetic and copies ran while one was open for 2% of the time, Pallas kernels for 7%

profile of v6, /device:TPU:1, one launch (start us, length us, event | category | flops | bytes accessed | tf_op | source)
XLA Modules:
  0.0 46.6 jit_solution(11118331722483697034)
XLA Ops:
  0.6 0.7 %constant_dynamic-update-slice_fusion.1 = bf16[32,256]{1,0:T(8,128)(2,1)S(1)} fusion(bf16[32,128]{1,0:T(8,128)(2,1)} %param.7), kind=kLoop, calls=%fused_computation.10 | loop fusion | bytes 16384
  1.5 2.7 %collective-permute-start.1 = (bf16[32,256]{1,0:T(8,128)(2,1)S(1)}, bf16[32,256]{1,0:T(8,128)(2,1)S(1)}, u32[]{:S(2)}, u32[]{:S(2)}) collective-permute-start(bf16[32,256]{1,0:T(8,128)(2,1)S(1)} %constant_dynamic-update-slice_fusion), channel_id=1, source_target_pairs={{0,9},{1,8},{2,11},{3,10},{4,13},{5,12},{6,15},{7,14},{8,1},{9,0},... | collective-permute-start | bytes 49160 | tf_op jit(solution)/shard_map/ppermute | solution.py:25
  4.2 2.6 %collective-permute-start.2 = (bf16[32,256]{1,0:T(8,128)(2,1)S(1)}, bf16[32,256]{1,0:T(8,128)(2,1)S(1)}, u32[]{:S(2)}, u32[]{:S(2)}) collective-permute-start(bf16[32,256]{1,0:T(8,128)(2,1)S(1)} %constant_dynamic-update-slice_fusion), channel_id=1, source_target_pairs={{0,17},{1,16},{2,19},{3,18},{4,21},{5,20},{6,23},{7,22},{8,25},{9,... | collective-permute-start | bytes 49160 | tf_op jit(solution)/shard_map/ppermute | solution.py:25
  6.8 1.0 %constant_dynamic-update-slice_fusion.7 = bf16[512,256]{1,0:T(8,128)(2,1)S(1)} fusion(bf16[512,128]{1,0:T(8,128)(2,1)} %param.10), kind=kLoop, calls=%fused_computation.16 | loop fusion | bytes 262144
  8.4 3.4 %collective-permute-done.3 = bf16[32,256]{1,0:T(8,128)(2,1)S(1)} collective-permute-done((bf16[32,256]{1,0:T(8,128)(2,1)S(1)}, bf16[32,256]{1,0:T(8,128)(2,1)S(1)}, u32[]{:S(2)}, u32[]{:S(2)}) %collective-permute-start.3) | collective-permute-done | bytes 16416 | tf_op jit(solution)/shard_map/ppermute | solution.py:25
  11.8 2.1 %collective-permute-start.4 = (bf16[128,256]{1,0:T(8,128)(2,1)S(1)}, bf16[128,256]{1,0:T(8,128)(2,1)S(1)}, u32[]{:S(2)}, u32[]{:S(2)}) collective-permute-start(bf16[128,256]{1,0:T(8,128)(2,1)S(1)} %constant_dynamic-update-slice_fusion.2), channel_id=1, source_target_pairs={{0,7},{1,6},{2,5},{3,4},{4,3},{5,2},{6,1},{7,0},{8,15},{9,14},{10,... | collective-permute-start | bytes 196616 | tf_op jit(solution)/shard_map/ppermute | solution.py:25
  15.2 1.3 %collective-permute-start.11 = (bf16[512,256]{1,0:T(8,128)(2,1)S(1)}, bf16[512,256]{1,0:T(8,128)(2,1)S(1)}, u32[]{:S(2)}, u32[]{:S(2)}) collective-permute-start(bf16[512,256]{1,0:T(8,128)(2,1)S(1)} %constant_dynamic-update-slice_fusion.6.refs_3_), channel_id=1, source_target_pairs={{0,2},{2,0},{4,6},{6,4},{8,10},{10,8},{12,14},{14,12},{16,18},{18,... | collective-permute-start | bytes 786440 | tf_op jit(solution)/shard_map/ppermute | solution.py:20
  16.5 1.3 %collective-permute-start.12 = (bf16[512,256]{1,0:T(8,128)(2,1)S(1)}, bf16[512,256]{1,0:T(8,128)(2,1)S(1)}, u32[]{:S(2)}, u32[]{:S(2)}) collective-permute-start(bf16[512,256]{1,0:T(8,128)(2,1)S(1)} %constant_dynamic-update-slice_fusion.6.refs_3_), channel_id=1, source_target_pairs={{0,4},{2,6},{4,0},{6,2},{8,12},{10,14},{12,8},{14,10},{16,20},{18,... | collective-permute-start | bytes 786440 | tf_op jit(solution)/shard_map/ppermute | solution.py:20
  18.8 2.2 %attention_terms.1 = (bf16[512,1024]{1,0:T(8,128)(2,1)S(1)}, bf16[512,256]{1,0:T(8,128)(2,1)S(1)}, f32[4,32,256]{2,1,0:T(8,128)S(1)}, bf16[4,32,256]{2,1,0:T(8,1...) custom-call(bf16[128,1024]{1,0:T(8,128)(2,1)S(1)} %copy-done, ...), custom_call_target="tpu_custom_call" | custom-call | flops 2684354560 | bytes 786432 | tf_op jit(solution)/shard_map/attention_terms/pallas_call | solution.py:70
  21.1 1.0 %collective-permute-start.10 = (bf16[4,32,256]{2,1,0:T(8,128)(2,1)S(1)}, bf16[4,32,256]{2,1,0:T(8,128)(2,1)S(1)}, u32[]{:S(2)}, u32[]{:S(2)}) collective-permute-start(bf16[4,32,256]{2,1,0:T(8,128)(2,1)S(1)} %get-tuple-element.20), channel_id=1, source_target_pairs={{0,6},{2,4},{4,2},{6,0},{8,14},{10,12},{12,10},{14,8},{16,22},{18,... | collective-permute-start | bytes 196616 | tf_op jit(solution)/shard_map/ppermute | solution.py:20
  22.1 1.5 %collective-permute-start.8 = (bf16[4,32,256]{2,1,0:T(8,128)(2,1)S(1)}, bf16[4,32,256]{2,1,0:T(8,128)(2,1)S(1)}, u32[]{:S(2)}, u32[]{:S(2)}) collective-permute-start(bf16[4,32,256]{2,1,0:T(8,128)(2,1)S(1)} %get-tuple-element.18), channel_id=1, source_target_pairs={{0,2},{2,0},{4,6},{6,4},{8,10},{10,8},{12,14},{14,12},{16,18},{18,... | collective-permute-start | bytes 196616 | tf_op jit(solution)/shard_map/ppermute | solution.py:20
  23.8 1.2 %query_gradient.1 = bf16[128,1024]{1,0:T(8,128)(2,1)} custom-call(bf16[512,1024]{1,0:T(8,128)(2,1)S(1)} %get-tuple-element.21.low_ref, bf16[512,256]{1,0:T(8,128)(2,1)S(1)} %get-tuple-element.22.vision_ref), custom_call_target="tpu_custom_call" | custom-call | flops 134217728 | bytes 262144 | tf_op jit(solution)/shard_map/query_gradient/pallas_call | solution.py:108
  25.0 1.2 %collective-permute-done.10 = bf16[4,32,256]{2,1,0:T(8,128)(2,1)S(1)} collective-permute-done((bf16[4,32,256]{2,1,0:T(8,128)(2,1)S(1)}, bf16[4,32,256]{2,1,0:T(8,128)(2,1)S(1)}, u32[]{:S(2)}, u32[]{:S(2)}) %collective-permute-start.10) | collective-permute-done | bytes 65568 | tf_op jit(solution)/shard_map/ppermute | solution.py:20
  26.7 0.7 %collective-permute-done.8 = bf16[4,32,256]{2,1,0:T(8,128)(2,1)S(1)} collective-permute-done((bf16[4,32,256]{2,1,0:T(8,128)(2,1)S(1)}, bf16[4,32,256]{2,1,0:T(8,128)(2,1)S(1)}, u32[]{:S(2)}, u32[]{:S(2)}) %collective-permute-start.8) | collective-permute-done | bytes 65568 | tf_op jit(solution)/shard_map/ppermute | solution.py:20
  28.0 2.2 %collective-permute-start.15 = (bf16[4,32,256]{2,1,0:T(8,128)(2,1)S(1)}, bf16[4,32,256]{2,1,0:T(8,128)(2,1)S(1)}, u32[]{:S(2)}, u32[]{:S(2)}) collective-permute-start(bf16[4,32,256]{2,1,0:T(8,128)(2,1)S(1)} %get-tuple-element.34), channel_id=1, source_target_pairs={{0,8},{2,10},{4,12},{6,14},{8,0},{10,2},{12,4},{14,6},{16,24},{18,... | collective-permute-start | bytes 196616 | tf_op jit(solution)/shard_map/ppermute | solution.py:20
  30.2 1.8 %collective-permute-done.13.refs_0_ = bf16[4,32,256]{2,1,0:T(8,128)(2,1)S(1)} collective-permute-done((bf16[4,32,256]{2,1,0:T(8,128)(2,1)S(1)}, bf16[4,32,256]{2,1,0:T(8,128)(2,1)S(1)}, u32[]{:S(2)}, u32[]{:S(2)}) %collective-permute-start.13) | collective-permute-done | bytes 65568 | tf_op jit(solution)/shard_map/ppermute | solution.py:20
  32.0 0.7 %collective-permute-done.14.refs_1_ = bf16[4,32,256]{2,1,0:T(8,128)(2,1)S(1)} collective-permute-done((bf16[4,32,256]{2,1,0:T(8,128)(2,1)S(1)}, bf16[4,32,256]{2,1,0:T(8,128)(2,1)S(1)}, u32[]{:S(2)}, u32[]{:S(2)}) %collective-permute-start.14) | collective-permute-done | bytes 65568 | tf_op jit(solution)/shard_map/ppermute | solution.py:20
  32.7 2.4 %collective-permute-done.15.refs_2_ = bf16[4,32,256]{2,1,0:T(8,128)(2,1)S(1)} collective-permute-done((bf16[4,32,256]{2,1,0:T(8,128)(2,1)S(1)}, bf16[4,32,256]{2,1,0:T(8,128)(2,1)S(1)}, u32[]{:S(2)}, u32[]{:S(2)}) %collective-permute-start.15) | collective-permute-done | bytes 65568 | tf_op jit(solution)/shard_map/ppermute | solution.py:20
  35.7 0.8 %collective-permute-start.17 = (bf16[2,32,2048]{2,1,0:T(8,128)(2,1)S(1)}, bf16[2,32,2048]{2,1,0:T(8,128)(2,1)S(1)}, u32[]{:S(2)}, u32[]{:S(2)}) collective-permute-start(bf16[2,32,2048]{2,1,0:T(8,128)(2,1)S(1)} %get-tuple-element.33), channel_id=1, source_target_pairs={{0,1},{1,0},{2,3},{3,2},{4,5},{5,4},{6,7},{7,6},{8,9},{9,8},{10,11... | collective-permute-start | bytes 786440 | tf_op jit(solution)/shard_map/ppermute | solution.py:20
  36.5 1.2 %collective-permute-done.17 = bf16[2,32,2048]{2,1,0:T(8,128)(2,1)S(1)} collective-permute-done((bf16[2,32,2048]{2,1,0:T(8,128)(2,1)S(1)}, bf16[2,32,2048]{2,1,0:T(8,128)(2,1)S(1)}, u32[]{:S(2)}, u32[]{:S(2)}) %collective-permute-start.17) | collective-permute-done | bytes 262176 | tf_op jit(solution)/shard_map/ppermute | solution.py:20
  37.7 0.9 %collective-permute-start.18 = (bf16[32,2048]{1,0:T(8,128)(2,1)S(1)}, bf16[32,2048]{1,0:T(8,128)(2,1)S(1)}, u32[]{:S(2)}, u32[]{:S(2)}) collective-permute-start(bf16[32,2048]{1,0:T(8,128)(2,1)S(1)} %get-tuple-element.39), channel_id=1, source_target_pairs={{0,8},{1,16},{2,10},{3,18},{4,12},{5,20},{6,14},{7,22},{8,0},{9,24... | collective-permute-start | bytes 393224 | tf_op jit(solution)/shard_map/ppermute | solution.py:259
  38.6 1.8 %collective-permute-start.19 = (bf16[32,2048]{1,0:T(8,128)(2,1)S(1)}, bf16[32,2048]{1,0:T(8,128)(2,1)S(1)}, u32[]{:S(2)}, u32[]{:S(2)}) collective-permute-start(bf16[32,2048]{1,0:T(8,128)(2,1)S(1)} %get-tuple-element.38), channel_id=1, source_target_pairs={{1,24},{0,2},{3,26},{2,0},{5,28},{4,6},{7,30},{6,4},{9,16},{8,10},... | collective-permute-start | bytes 393224 | tf_op jit(solution)/shard_map/ppermute | solution.py:258
  40.4 5.5 %collective-permute-done.18 = bf16[32,2048]{1,0:T(8,128)(2,1)S(1)} collective-permute-done((bf16[32,2048]{1,0:T(8,128)(2,1)S(1)}, bf16[32,2048]{1,0:T(8,128)(2,1)S(1)}, u32[]{:S(2)}, u32[]{:S(2)}) %collective-permute-start.18) | collective-permute-done | bytes 131104 | tf_op jit(solution)/shard_map/ppermute | solution.py:259
  45.9 0.7 %pad_maximum_fusion = bf16[32,4096]{1,0:T(8,128)(2,1)} fusion(bf16[32,2048]{1,0:T(8,128)(2,1)S(1)} %get-tuple-element.37, bf16[32,2048]{1,0:T(8,128)(2,1)S(1)} %get-tuple-element.36), kind=kLoop, calls=%fused_computation.1 | loop fusion | flops 524288 | bytes 524288 | tf_op jit(solution)/shard_map/concatenate | solution.py:263
  (40 shorter events, 4.9 us)
Async XLA Ops:
  0.6 0.7 %copy-start.3 = (bf16[32,128]{1,0:T(8,128)(2,1)S(1)}, bf16[32,128]{1,0:T(8,128)(2,1)}, u32[]{:S(2)}) copy-start(bf16[32,128]{1,0:T(8,128)(2,1)} %param.8) | copy-start | bytes 24580
  1.3 13.8 %copy-start.2 = (bf16[512,128]{1,0:T(8,128)(2,1)S(1)}, bf16[512,128]{1,0:T(8,128)(2,1)}, u32[]{:S(2)}) copy-start(bf16[512,128]{1,0:T(8,128)(2,1)} %param.11) | copy-start | bytes 393220
  1.4 6.5 %collective-permute-start = (bf16[32,256]{1,0:T(8,128)(2,1)S(1)}, bf16[32,256]{1,0:T(8,128)(2,1)S(1)}, u32[]{:S(2)}, u32[]{:S(2)}) collective-permute-start(bf16[32,256]{1,0:T(8,128)(2,1)S(1)} %constant_dynamic-update-slice_fusion), channel_id=1, source_target_pairs={{0,1},{1,0},{2,3},{3,2},{4,5},{5,4},{6,7},{7,6},{8,9},{9,8},{10,11... | collective-permute-start | bytes 49160 | tf_op jit(solution)/shard_map/ppermute | solution.py:25
  1.5 6.4 %collective-permute-start.1 = (bf16[32,256]{1,0:T(8,128)(2,1)S(1)}, bf16[32,256]{1,0:T(8,128)(2,1)S(1)}, u32[]{:S(2)}, u32[]{:S(2)}) collective-permute-start(bf16[32,256]{1,0:T(8,128)(2,1)S(1)} %constant_dynamic-update-slice_fusion), channel_id=1, source_target_pairs={{0,9},{1,8},{2,11},{3,10},{4,13},{5,12},{6,15},{7,14},{8,1},{9,0},... | collective-permute-start | bytes 49160 | tf_op jit(solution)/shard_map/ppermute | solution.py:25
  4.2 4.2 %collective-permute-start.2 = (bf16[32,256]{1,0:T(8,128)(2,1)S(1)}, bf16[32,256]{1,0:T(8,128)(2,1)S(1)}, u32[]{:S(2)}, u32[]{:S(2)}) collective-permute-start(bf16[32,256]{1,0:T(8,128)(2,1)S(1)} %constant_dynamic-update-slice_fusion), channel_id=1, source_target_pairs={{0,17},{1,16},{2,19},{3,18},{4,21},{5,20},{6,23},{7,22},{8,25},{9,... | collective-permute-start | bytes 49160 | tf_op jit(solution)/shard_map/ppermute | solution.py:25
  6.8 5.0 %collective-permute-start.3 = (bf16[32,256]{1,0:T(8,128)(2,1)S(1)}, bf16[32,256]{1,0:T(8,128)(2,1)S(1)}, u32[]{:S(2)}, u32[]{:S(2)}) collective-permute-start(bf16[32,256]{1,0:T(8,128)(2,1)S(1)} %constant_dynamic-update-slice_fusion), channel_id=1, source_target_pairs={{0,25},{1,24},{2,27},{3,26},{4,29},{5,28},{6,31},{7,30},{8,17},{9,... | collective-permute-start | bytes 49160 | tf_op jit(solution)/shard_map/ppermute | solution.py:25
  6.8 12.0 %copy-start.1 = (bf16[128,1024]{1,0:T(8,128)(2,1)S(1)}, bf16[128,1024]{1,0:T(8,128)(2,1)}, u32[]{:S(2)}) copy-start(bf16[128,1024]{1,0:T(8,128)(2,1)} %upstream_ref.1) | copy-start | bytes 786436
  7.8 11.0 %copy-start = (bf16[128,1024]{1,0:T(8,128)(2,1)S(1)}, bf16[128,1024]{1,0:T(8,128)(2,1)}, u32[]{:S(2)}) copy-start(bf16[128,1024]{1,0:T(8,128)(2,1)} %queries_ref.1) | copy-start | bytes 786436
  11.8 4.7 %collective-permute-start.4 = (bf16[128,256]{1,0:T(8,128)(2,1)S(1)}, bf16[128,256]{1,0:T(8,128)(2,1)S(1)}, u32[]{:S(2)}, u32[]{:S(2)}) collective-permute-start(bf16[128,256]{1,0:T(8,128)(2,1)S(1)} %constant_dynamic-update-slice_fusion.2), channel_id=1, source_target_pairs={{0,7},{1,6},{2,5},{3,4},{4,3},{5,2},{6,1},{7,0},{8,15},{9,14},{10,... | collective-permute-start | bytes 196616 | tf_op jit(solution)/shard_map/ppermute | solution.py:25
  13.9 4.2 %collective-permute-start.5 = (bf16[128,256]{1,0:T(8,128)(2,1)S(1)}, bf16[128,256]{1,0:T(8,128)(2,1)S(1)}, u32[]{:S(2)}, u32[]{:S(2)}) collective-permute-start(bf16[128,256]{1,0:T(8,128)(2,1)S(1)} %constant_dynamic-update-slice_fusion.2), channel_id=1, source_target_pairs={{0,5},{1,4},{2,7},{3,6},{4,1},{5,0},{6,3},{7,2},{8,13},{9,12},{10,... | collective-permute-start | bytes 196616 | tf_op jit(solution)/shard_map/ppermute | solution.py:25
  14.5 4.3 %collective-permute-start.6 = (bf16[128,256]{1,0:T(8,128)(2,1)S(1)}, bf16[128,256]{1,0:T(8,128)(2,1)S(1)}, u32[]{:S(2)}, u32[]{:S(2)}) collective-permute-start(bf16[128,256]{1,0:T(8,128)(2,1)S(1)} %constant_dynamic-update-slice_fusion.2), channel_id=1, source_target_pairs={{0,3},{1,2},{2,1},{3,0},{4,7},{5,6},{6,5},{7,4},{8,11},{9,10},{10,... | collective-permute-start | bytes 196616 | tf_op jit(solution)/shard_map/ppermute | solution.py:25
  14.7 4.1 %collective-permute-start.7 = (bf16[128,256]{1,0:T(8,128)(2,1)S(1)}, bf16[128,256]{1,0:T(8,128)(2,1)S(1)}, u32[]{:S(2)}, u32[]{:S(2)}) collective-permute-start(bf16[128,256]{1,0:T(8,128)(2,1)S(1)} %constant_dynamic-update-slice_fusion.2), channel_id=1, source_target_pairs={{0,1},{1,0},{2,3},{3,2},{4,5},{5,4},{6,7},{7,6},{8,9},{9,8},{10,11... | collective-permute-start | bytes 196616 | tf_op jit(solution)/shard_map/ppermute | solution.py:25
  15.2 12.3 %collective-permute-start.11 = (bf16[512,256]{1,0:T(8,128)(2,1)S(1)}, bf16[512,256]{1,0:T(8,128)(2,1)S(1)}, u32[]{:S(2)}, u32[]{:S(2)}) collective-permute-start(bf16[512,256]{1,0:T(8,128)(2,1)S(1)} %constant_dynamic-update-slice_fusion.6.refs_3_), channel_id=1, source_target_pairs={{0,2},{2,0},{4,6},{6,4},{8,10},{10,8},{12,14},{14,12},{16,18},{18,... | collective-permute-start | bytes 786440 | tf_op jit(solution)/shard_map/ppermute | solution.py:20
  16.5 11.0 %collective-permute-start.12 = (bf16[512,256]{1,0:T(8,128)(2,1)S(1)}, bf16[512,256]{1,0:T(8,128)(2,1)S(1)}, u32[]{:S(2)}, u32[]{:S(2)}) collective-permute-start(bf16[512,256]{1,0:T(8,128)(2,1)S(1)} %constant_dynamic-update-slice_fusion.6.refs_3_), channel_id=1, source_target_pairs={{0,4},{2,6},{4,0},{6,2},{8,12},{10,14},{12,8},{14,10},{16,20},{18,... | collective-permute-start | bytes 786440 | tf_op jit(solution)/shard_map/ppermute | solution.py:20
  21.1 5.1 %collective-permute-start.10 = (bf16[4,32,256]{2,1,0:T(8,128)(2,1)S(1)}, bf16[4,32,256]{2,1,0:T(8,128)(2,1)S(1)}, u32[]{:S(2)}, u32[]{:S(2)}) collective-permute-start(bf16[4,32,256]{2,1,0:T(8,128)(2,1)S(1)} %get-tuple-element.20), channel_id=1, source_target_pairs={{0,6},{2,4},{4,2},{6,0},{8,14},{10,12},{12,10},{14,8},{16,22},{18,... | collective-permute-start | bytes 196616 | tf_op jit(solution)/shard_map/ppermute | solution.py:20
  22.1 5.4 %collective-permute-start.8 = (bf16[4,32,256]{2,1,0:T(8,128)(2,1)S(1)}, bf16[4,32,256]{2,1,0:T(8,128)(2,1)S(1)}, u32[]{:S(2)}, u32[]{:S(2)}) collective-permute-start(bf16[4,32,256]{2,1,0:T(8,128)(2,1)S(1)} %get-tuple-element.18), channel_id=1, source_target_pairs={{0,2},{2,0},{4,6},{6,4},{8,10},{10,8},{12,14},{14,12},{16,18},{18,... | collective-permute-start | bytes 196616 | tf_op jit(solution)/shard_map/ppermute | solution.py:20
  23.6 3.9 %collective-permute-start.9 = (bf16[4,32,256]{2,1,0:T(8,128)(2,1)S(1)}, bf16[4,32,256]{2,1,0:T(8,128)(2,1)S(1)}, u32[]{:S(2)}, u32[]{:S(2)}) collective-permute-start(bf16[4,32,256]{2,1,0:T(8,128)(2,1)S(1)} %get-tuple-element.19), channel_id=1, source_target_pairs={{0,4},{2,6},{4,0},{6,2},{8,12},{10,14},{12,8},{14,10},{16,20},{18,... | collective-permute-start | bytes 196616 | tf_op jit(solution)/shard_map/ppermute | solution.py:20
  26.2 9.0 %collective-permute-start.16 = (bf16[512,256]{1,0:T(8,128)(2,1)S(1)}, bf16[512,256]{1,0:T(8,128)(2,1)S(1)}, u32[]{:S(2)}, u32[]{:S(2)}) collective-permute-start(bf16[512,256]{1,0:T(8,128)(2,1)S(1)} %constant_dynamic-update-slice_fusion.6.refs_3_), channel_id=1, source_target_pairs={{0,6},{2,4},{4,2},{6,0},{8,14},{10,12},{12,10},{14,8},{16,22},{18,... | collective-permute-start | bytes 786440 | tf_op jit(solution)/shard_map/ppermute | solution.py:20
  27.5 4.5 %collective-permute-start.13 = (bf16[4,32,256]{2,1,0:T(8,128)(2,1)S(1)}, bf16[4,32,256]{2,1,0:T(8,128)(2,1)S(1)}, u32[]{:S(2)}, u32[]{:S(2)}) collective-permute-start(bf16[4,32,256]{2,1,0:T(8,128)(2,1)S(1)} %get-tuple-element.34), channel_id=1, source_target_pairs={{0,16},{2,18},{4,20},{6,22},{8,24},{10,26},{12,28},{14,30},{16,0},... | collective-permute-start | bytes 196616 | tf_op jit(solution)/shard_map/ppermute | solution.py:20
  27.6 5.1 %collective-permute-start.14 = (bf16[4,32,256]{2,1,0:T(8,128)(2,1)S(1)}, bf16[4,32,256]{2,1,0:T(8,128)(2,1)S(1)}, u32[]{:S(2)}, u32[]{:S(2)}) collective-permute-start(bf16[4,32,256]{2,1,0:T(8,128)(2,1)S(1)} %get-tuple-element.34), channel_id=1, source_target_pairs={{0,24},{2,26},{4,28},{6,30},{8,16},{10,18},{12,20},{14,22},{16,8},... | collective-permute-start | bytes 196616 | tf_op jit(solution)/shard_map/ppermute | solution.py:20
  28.0 7.1 %collective-permute-start.15 = (bf16[4,32,256]{2,1,0:T(8,128)(2,1)S(1)}, bf16[4,32,256]{2,1,0:T(8,128)(2,1)S(1)}, u32[]{:S(2)}, u32[]{:S(2)}) collective-permute-start(bf16[4,32,256]{2,1,0:T(8,128)(2,1)S(1)} %get-tuple-element.34), channel_id=1, source_target_pairs={{0,8},{2,10},{4,12},{6,14},{8,0},{10,2},{12,4},{14,6},{16,24},{18,... | collective-permute-start | bytes 196616 | tf_op jit(solution)/shard_map/ppermute | solution.py:20
  35.7 2.0 %collective-permute-start.17 = (bf16[2,32,2048]{2,1,0:T(8,128)(2,1)S(1)}, bf16[2,32,2048]{2,1,0:T(8,128)(2,1)S(1)}, u32[]{:S(2)}, u32[]{:S(2)}) collective-permute-start(bf16[2,32,2048]{2,1,0:T(8,128)(2,1)S(1)} %get-tuple-element.33), channel_id=1, source_target_pairs={{0,1},{1,0},{2,3},{3,2},{4,5},{5,4},{6,7},{7,6},{8,9},{9,8},{10,11... | collective-permute-start | bytes 786440 | tf_op jit(solution)/shard_map/ppermute | solution.py:20
  37.7 8.2 %collective-permute-start.18 = (bf16[32,2048]{1,0:T(8,128)(2,1)S(1)}, bf16[32,2048]{1,0:T(8,128)(2,1)S(1)}, u32[]{:S(2)}, u32[]{:S(2)}) collective-permute-start(bf16[32,2048]{1,0:T(8,128)(2,1)S(1)} %get-tuple-element.39), channel_id=1, source_target_pairs={{0,8},{1,16},{2,10},{3,18},{4,12},{5,20},{6,14},{7,22},{8,0},{9,24... | collective-permute-start | bytes 393224 | tf_op jit(solution)/shard_map/ppermute | solution.py:259
  38.6 7.2 %collective-permute-start.19 = (bf16[32,2048]{1,0:T(8,128)(2,1)S(1)}, bf16[32,2048]{1,0:T(8,128)(2,1)S(1)}, u32[]{:S(2)}, u32[]{:S(2)}) collective-permute-start(bf16[32,2048]{1,0:T(8,128)(2,1)S(1)} %get-tuple-element.38), channel_id=1, source_target_pairs={{1,24},{0,2},{3,26},{2,0},{5,28},{4,6},{7,30},{6,4},{9,16},{8,10},... | collective-permute-start | bytes 393224 | tf_op jit(solution)/shard_map/ppermute | solution.py:258

commit v7 on v6

--- a/solution.py
+++ b/solution.py
@@ -58,7 +58,7 @@
     spot = lax.axis_index("seq") // outer
     for d, ref in enumerate(terms_refs):
         for i in range(inner):
-            ref[i] = sums[outer - 1 - d, jnp.bitwise_xor(spot, i)].astype(ref.dtype)
+            ref[i] = sums[outer - 1 - d, lax.rem(inner - jnp.bitwise_xor(spot, i), inner)].astype(ref.dtype)
 
 
 def attention_terms(queries, upstream, blocks, inner):
@@ -226,7 +226,7 @@
 
     pair = jnp.concatenate([vision_key, vision_value], axis=1)
     arrived = {d: swap(pair, chips, d) for d in (cross, far, near, 0)}
-    block = jnp.concatenate([arrived[d] for d in (0, near, far, cross)], axis=0)
+    block = jnp.concatenate([arrived[d] for d in (0, cross, far, near)], axis=0)
     blocks = {d: swap(block, chips, d) for d in (3, 1, 2, 0)}
     weight = jnp.concatenate([key_weight, value_weight], axis=1)
     weights = [weight] + [exchange(weight, "seq", chips, d) for d in (1, 2)]

time: 46.9 us -> 46.2 us (0.985)
  waiting for transfers between devices: 18.5 us -> 16.1 us
  starting transfers between devices: 20.8 us -> 22.6 us
    ppermute x10, starting transfers between devices: 9.33 us -> 11.1 us  [exchange(): return lax.ppermute(block, axis, [(i, i ^ distance) for i in range(size)])]
    ppermute x8, waiting for transfers between devices: 4.97 us -> 3.58 us  [swap(): return lax.ppermute(block, ('seq', 'kv'), routes)]
    ppermute x10, waiting for transfers between devices: 8.1 us -> 7.05 us  [exchange(): return lax.ppermute(block, axis, [(i, i ^ distance) for i in range(size)])]
    ppermute x1, starting transfers between devices: 0.93 us -> 1.79 us  [two_cores(): first = lax.ppermute(go, ('seq', 'kv'), routes_a)]
    ppermute x1, starting transfers between devices: 1.78 us -> 0.92 us  [two_cores(): second = lax.ppermute(stay, ('seq', 'kv'), routes_b)]
  transfers between devices with their start and end apart: 20 -> 20, of which waited for: 11 -> 11; matrix products, arithmetic and copies ran while one was open for 2% -> 2% of each run, Pallas kernels for 7% -> 8%
where the time goes in v7:
time: 46.2 us; the launch traced here: 46 us
  starting transfers between devices  22.6 us (49%)
  waiting for transfers between devices  16.1 us (35%)
  Pallas kernels  3.93 us (9%)
  local copies, waits for them, and re-layouts  1.76 us (4%)
  other arithmetic  0.83 us (2%)
  between operations  0.75 us (2%)
    ppermute x10, starting transfers between devices, exchange(): return lax.ppermute(block, axis, [(i, i ^ distance) for i in range(size)])  11.1 us
    ppermute x8, starting transfers between devices, swap(): return lax.ppermute(block, ('seq', 'kv'), routes)  8.84 us
    ppermute x10, waiting for transfers between devices, exchange(): return lax.ppermute(block, axis, [(i, i ^ distance) for i in range(size)])  7.05 us
    ppermute x1, waiting for transfers between devices, two_cores(): first = lax.ppermute(go, ('seq', 'kv'), routes_a)  5.45 us
    ppermute x8, waiting for transfers between devices, swap(): return lax.ppermute(block, ('seq', 'kv'), routes)  3.58 us
    pallas_call x1, Pallas kernels, attention_terms(): pl.pallas_call(functools.partial(attention_kernel, outer), out_shape=[jax...  2.26 us
    ppermute x1, starting transfers between devices, two_cores(): first = lax.ppermute(go, ('seq', 'kv'), routes_a)  1.79 us
    unnamed x13, local copies, waits for them, and re-layouts  1.7 us
  transfers between devices with their start and end apart: 20, of which 11 were waited for; matrix products, arithmetic and copies ran while one was open for 2% of the time, Pallas kernels for 8%

profile of v7, /device:TPU:1, one launch (start us, length us, event | category | flops | bytes accessed | tf_op | source)
XLA Modules:
  0.0 46.0 jit_solution(10741655264562134182)
XLA Ops:
  0.6 0.7 %constant_dynamic-update-slice_fusion.1 = bf16[32,256]{1,0:T(8,128)(2,1)S(1)} fusion(bf16[32,128]{1,0:T(8,128)(2,1)} %param.7), kind=kLoop, calls=%fused_computation.10 | loop fusion | bytes 16384
  1.5 4.7 %collective-permute-start.1 = (bf16[32,256]{1,0:T(8,128)(2,1)S(1)}, bf16[32,256]{1,0:T(8,128)(2,1)S(1)}, u32[]{:S(2)}, u32[]{:S(2)}) collective-permute-start(bf16[32,256]{1,0:T(8,128)(2,1)S(1)} %constant_dynamic-update-slice_fusion), channel_id=1, source_target_pairs={{0,25},{1,24},{2,27},{3,26},{4,29},{5,28},{6,31},{7,30},{8,17},{9,... | collective-permute-start | bytes 49160 | tf_op jit(solution)/shard_map/ppermute | solution.py:25
  6.2 0.6 %collective-permute-start.3 = (bf16[32,256]{1,0:T(8,128)(2,1)S(1)}, bf16[32,256]{1,0:T(8,128)(2,1)S(1)}, u32[]{:S(2)}, u32[]{:S(2)}) collective-permute-start(bf16[32,256]{1,0:T(8,128)(2,1)S(1)} %constant_dynamic-update-slice_fusion), channel_id=1, source_target_pairs={{0,9},{1,8},{2,11},{3,10},{4,13},{5,12},{6,15},{7,14},{8,1},{9,0},... | collective-permute-start | bytes 49160 | tf_op jit(solution)/shard_map/ppermute | solution.py:25
  6.8 1.0 %constant_dynamic-update-slice_fusion.7 = bf16[512,256]{1,0:T(8,128)(2,1)S(1)} fusion(bf16[512,128]{1,0:T(8,128)(2,1)} %param.10), kind=kLoop, calls=%fused_computation.16 | loop fusion | bytes 262144
  7.8 2.5 %collective-permute-done.2 = bf16[32,256]{1,0:T(8,128)(2,1)S(1)} collective-permute-done((bf16[32,256]{1,0:T(8,128)(2,1)S(1)}, bf16[32,256]{1,0:T(8,128)(2,1)S(1)}, u32[]{:S(2)}, u32[]{:S(2)}) %collective-permute-start.2) | collective-permute-done | bytes 16416 | tf_op jit(solution)/shard_map/ppermute | solution.py:25
  10.3 2.5 %collective-permute-start.4 = (bf16[128,256]{1,0:T(8,128)(2,1)S(1)}, bf16[128,256]{1,0:T(8,128)(2,1)S(1)}, u32[]{:S(2)}, u32[]{:S(2)}) collective-permute-start(bf16[128,256]{1,0:T(8,128)(2,1)S(1)} %constant_dynamic-update-slice_fusion.2), channel_id=1, source_target_pairs={{0,7},{1,6},{2,5},{3,4},{4,3},{5,2},{6,1},{7,0},{8,15},{9,14},{10,... | collective-permute-start | bytes 196616 | tf_op jit(solution)/shard_map/ppermute | solution.py:25
  13.8 1.3 %collective-permute-start.11 = (bf16[512,256]{1,0:T(8,128)(2,1)S(1)}, bf16[512,256]{1,0:T(8,128)(2,1)S(1)}, u32[]{:S(2)}, u32[]{:S(2)}) collective-permute-start(bf16[512,256]{1,0:T(8,128)(2,1)S(1)} %constant_dynamic-update-slice_fusion.6.refs_3_), channel_id=1, source_target_pairs={{0,2},{2,0},{4,6},{6,4},{8,10},{10,8},{12,14},{14,12},{16,18},{18,... | collective-permute-start | bytes 786440 | tf_op jit(solution)/shard_map/ppermute | solution.py:20
  15.4 1.3 %collective-permute-start.12 = (bf16[512,256]{1,0:T(8,128)(2,1)S(1)}, bf16[512,256]{1,0:T(8,128)(2,1)S(1)}, u32[]{:S(2)}, u32[]{:S(2)}) collective-permute-start(bf16[512,256]{1,0:T(8,128)(2,1)S(1)} %constant_dynamic-update-slice_fusion.6.refs_3_), channel_id=1, source_target_pairs={{0,4},{2,6},{4,0},{6,2},{8,12},{10,14},{12,8},{14,10},{16,20},{18,... | collective-permute-start | bytes 786440 | tf_op jit(solution)/shard_map/ppermute | solution.py:20
  17.5 2.3 %attention_terms.1 = (bf16[512,1024]{1,0:T(8,128)(2,1)S(1)}, bf16[512,256]{1,0:T(8,128)(2,1)S(1)}, f32[4,32,256]{2,1,0:T(8,128)S(1)}, bf16[4,32,256]{2,1,0:T(8,1...) custom-call(bf16[128,1024]{1,0:T(8,128)(2,1)S(1)} %copy-done, ...), custom_call_target="tpu_custom_call" | custom-call | flops 2684354560 | bytes 786432 | tf_op jit(solution)/shard_map/attention_terms/pallas_call | solution.py:70
  19.7 1.1 %collective-permute-start.10 = (bf16[4,32,256]{2,1,0:T(8,128)(2,1)S(1)}, bf16[4,32,256]{2,1,0:T(8,128)(2,1)S(1)}, u32[]{:S(2)}, u32[]{:S(2)}) collective-permute-start(bf16[4,32,256]{2,1,0:T(8,128)(2,1)S(1)} %get-tuple-element.20), channel_id=1, source_target_pairs={{0,6},{2,4},{4,2},{6,0},{8,14},{10,12},{12,10},{14,8},{16,22},{18,... | collective-permute-start | bytes 196616 | tf_op jit(solution)/shard_map/ppermute | solution.py:20
  20.8 1.4 %collective-permute-start.8 = (bf16[4,32,256]{2,1,0:T(8,128)(2,1)S(1)}, bf16[4,32,256]{2,1,0:T(8,128)(2,1)S(1)}, u32[]{:S(2)}, u32[]{:S(2)}) collective-permute-start(bf16[4,32,256]{2,1,0:T(8,128)(2,1)S(1)} %get-tuple-element.18), channel_id=1, source_target_pairs={{0,2},{2,0},{4,6},{6,4},{8,10},{10,8},{12,14},{14,12},{16,18},{18,... | collective-permute-start | bytes 196616 | tf_op jit(solution)/shard_map/ppermute | solution.py:20
  22.5 1.2 %query_gradient.1 = bf16[128,1024]{1,0:T(8,128)(2,1)} custom-call(bf16[512,1024]{1,0:T(8,128)(2,1)S(1)} %get-tuple-element.21.low_ref, bf16[512,256]{1,0:T(8,128)(2,1)S(1)} %get-tuple-element.22.vision_ref), custom_call_target="tpu_custom_call" | custom-call | flops 134217728 | bytes 262144 | tf_op jit(solution)/shard_map/query_gradient/pallas_call | solution.py:108
  23.7 1.6 %collective-permute-done.10 = bf16[4,32,256]{2,1,0:T(8,128)(2,1)S(1)} collective-permute-done((bf16[4,32,256]{2,1,0:T(8,128)(2,1)S(1)}, bf16[4,32,256]{2,1,0:T(8,128)(2,1)S(1)}, u32[]{:S(2)}, u32[]{:S(2)}) %collective-permute-start.10) | collective-permute-done | bytes 65568 | tf_op jit(solution)/shard_map/ppermute | solution.py:20
  25.2 0.7 %collective-permute-start.16 = (bf16[512,256]{1,0:T(8,128)(2,1)S(1)}, bf16[512,256]{1,0:T(8,128)(2,1)S(1)}, u32[]{:S(2)}, u32[]{:S(2)}) collective-permute-start(bf16[512,256]{1,0:T(8,128)(2,1)S(1)} %constant_dynamic-update-slice_fusion.6.refs_3_), channel_id=1, source_target_pairs={{0,6},{2,4},{4,2},{6,0},{8,14},{10,12},{12,10},{14,8},{16,22},{18,... | collective-permute-start | bytes 786440 | tf_op jit(solution)/shard_map/ppermute | solution.py:20
  26.3 1.6 %collective-permute-start.13 = (bf16[4,32,256]{2,1,0:T(8,128)(2,1)S(1)}, bf16[4,32,256]{2,1,0:T(8,128)(2,1)S(1)}, u32[]{:S(2)}, u32[]{:S(2)}) collective-permute-start(bf16[4,32,256]{2,1,0:T(8,128)(2,1)S(1)} %get-tuple-element.34), channel_id=1, source_target_pairs={{0,16},{2,18},{4,20},{6,22},{8,24},{10,26},{12,28},{14,30},{16,0},... | collective-permute-start | bytes 196616 | tf_op jit(solution)/shard_map/ppermute | solution.py:20
  27.9 1.1 %collective-permute-start.15 = (bf16[4,32,256]{2,1,0:T(8,128)(2,1)S(1)}, bf16[4,32,256]{2,1,0:T(8,128)(2,1)S(1)}, u32[]{:S(2)}, u32[]{:S(2)}) collective-permute-start(bf16[4,32,256]{2,1,0:T(8,128)(2,1)S(1)} %get-tuple-element.34), channel_id=1, source_target_pairs={{0,8},{2,10},{4,12},{6,14},{8,0},{10,2},{12,4},{14,6},{16,24},{18,... | collective-permute-start | bytes 196616 | tf_op jit(solution)/shard_map/ppermute | solution.py:20
  29.0 1.7 %collective-permute-done.13.refs_0_ = bf16[4,32,256]{2,1,0:T(8,128)(2,1)S(1)} collective-permute-done((bf16[4,32,256]{2,1,0:T(8,128)(2,1)S(1)}, bf16[4,32,256]{2,1,0:T(8,128)(2,1)S(1)}, u32[]{:S(2)}, u32[]{:S(2)}) %collective-permute-start.13) | collective-permute-done | bytes 65568 | tf_op jit(solution)/shard_map/ppermute | solution.py:20
  30.6 2.3 %collective-permute-done.14.refs_1_ = bf16[4,32,256]{2,1,0:T(8,128)(2,1)S(1)} collective-permute-done((bf16[4,32,256]{2,1,0:T(8,128)(2,1)S(1)}, bf16[4,32,256]{2,1,0:T(8,128)(2,1)S(1)}, u32[]{:S(2)}, u32[]{:S(2)}) %collective-permute-start.14) | collective-permute-done | bytes 65568 | tf_op jit(solution)/shard_map/ppermute | solution.py:20
  33.5 2.3 %collective-permute-start.17 = (bf16[2,32,2048]{2,1,0:T(8,128)(2,1)S(1)}, bf16[2,32,2048]{2,1,0:T(8,128)(2,1)S(1)}, u32[]{:S(2)}, u32[]{:S(2)}) collective-permute-start(bf16[2,32,2048]{2,1,0:T(8,128)(2,1)S(1)} %get-tuple-element.33), channel_id=1, source_target_pairs={{0,1},{1,0},{2,3},{3,2},{4,5},{5,4},{6,7},{7,6},{8,9},{9,8},{10,11... | collective-permute-start | bytes 786440 | tf_op jit(solution)/shard_map/ppermute | solution.py:20
  35.8 1.2 %collective-permute-done.17 = bf16[2,32,2048]{2,1,0:T(8,128)(2,1)S(1)} collective-permute-done((bf16[2,32,2048]{2,1,0:T(8,128)(2,1)S(1)}, bf16[2,32,2048]{2,1,0:T(8,128)(2,1)S(1)}, u32[]{:S(2)}, u32[]{:S(2)}) %collective-permute-start.17) | collective-permute-done | bytes 262176 | tf_op jit(solution)/shard_map/ppermute | solution.py:20
  37.0 1.8 %collective-permute-start.18 = (bf16[32,2048]{1,0:T(8,128)(2,1)S(1)}, bf16[32,2048]{1,0:T(8,128)(2,1)S(1)}, u32[]{:S(2)}, u32[]{:S(2)}) collective-permute-start(bf16[32,2048]{1,0:T(8,128)(2,1)S(1)} %get-tuple-element.39), channel_id=1, source_target_pairs={{0,8},{1,16},{2,10},{3,18},{4,12},{5,20},{6,14},{7,22},{8,0},{9,24... | collective-permute-start | bytes 393224 | tf_op jit(solution)/shard_map/ppermute | solution.py:259
  38.8 0.9 %collective-permute-start.19 = (bf16[32,2048]{1,0:T(8,128)(2,1)S(1)}, bf16[32,2048]{1,0:T(8,128)(2,1)S(1)}, u32[]{:S(2)}, u32[]{:S(2)}) collective-permute-start(bf16[32,2048]{1,0:T(8,128)(2,1)S(1)} %get-tuple-element.38), channel_id=1, source_target_pairs={{1,24},{0,2},{3,26},{2,0},{5,28},{4,6},{7,30},{6,4},{9,16},{8,10},... | collective-permute-start | bytes 393224 | tf_op jit(solution)/shard_map/ppermute | solution.py:258
  39.8 5.5 %collective-permute-done.18 = bf16[32,2048]{1,0:T(8,128)(2,1)S(1)} collective-permute-done((bf16[32,2048]{1,0:T(8,128)(2,1)S(1)}, bf16[32,2048]{1,0:T(8,128)(2,1)S(1)}, u32[]{:S(2)}, u32[]{:S(2)}) %collective-permute-start.18) | collective-permute-done | bytes 131104 | tf_op jit(solution)/shard_map/ppermute | solution.py:259
  45.2 0.7 %pad_maximum_fusion = bf16[32,4096]{1,0:T(8,128)(2,1)} fusion(bf16[32,2048]{1,0:T(8,128)(2,1)S(1)} %get-tuple-element.37, bf16[32,2048]{1,0:T(8,128)(2,1)S(1)} %get-tuple-element.36), kind=kLoop, calls=%fused_computation.1 | loop fusion | flops 524288 | bytes 524288 | tf_op jit(solution)/shard_map/concatenate | solution.py:263
  (40 shorter events, 3.4 us)
Async XLA Ops:
  0.6 0.7 %copy-start.3 = (bf16[32,128]{1,0:T(8,128)(2,1)S(1)}, bf16[32,128]{1,0:T(8,128)(2,1)}, u32[]{:S(2)}) copy-start(bf16[32,128]{1,0:T(8,128)(2,1)} %param.8) | copy-start | bytes 24580
  1.3 12.4 %copy-start.2 = (bf16[512,128]{1,0:T(8,128)(2,1)S(1)}, bf16[512,128]{1,0:T(8,128)(2,1)}, u32[]{:S(2)}) copy-start(bf16[512,128]{1,0:T(8,128)(2,1)} %param.11) | copy-start | bytes 393220
  1.4 6.4 %collective-permute-start = (bf16[32,256]{1,0:T(8,128)(2,1)S(1)}, bf16[32,256]{1,0:T(8,128)(2,1)S(1)}, u32[]{:S(2)}, u32[]{:S(2)}) collective-permute-start(bf16[32,256]{1,0:T(8,128)(2,1)S(1)} %constant_dynamic-update-slice_fusion), channel_id=1, source_target_pairs={{0,1},{1,0},{2,3},{3,2},{4,5},{5,4},{6,7},{7,6},{8,9},{9,8},{10,11... | collective-permute-start | bytes 49160 | tf_op jit(solution)/shard_map/ppermute | solution.py:25
  1.5 6.3 %collective-permute-start.1 = (bf16[32,256]{1,0:T(8,128)(2,1)S(1)}, bf16[32,256]{1,0:T(8,128)(2,1)S(1)}, u32[]{:S(2)}, u32[]{:S(2)}) collective-permute-start(bf16[32,256]{1,0:T(8,128)(2,1)S(1)} %constant_dynamic-update-slice_fusion), channel_id=1, source_target_pairs={{0,25},{1,24},{2,27},{3,26},{4,29},{5,28},{6,31},{7,30},{8,17},{9,... | collective-permute-start | bytes 49160 | tf_op jit(solution)/shard_map/ppermute | solution.py:25
  6.2 4.1 %collective-permute-start.2 = (bf16[32,256]{1,0:T(8,128)(2,1)S(1)}, bf16[32,256]{1,0:T(8,128)(2,1)S(1)}, u32[]{:S(2)}, u32[]{:S(2)}) collective-permute-start(bf16[32,256]{1,0:T(8,128)(2,1)S(1)} %constant_dynamic-update-slice_fusion), channel_id=1, source_target_pairs={{0,17},{1,16},{2,19},{3,18},{4,21},{5,20},{6,23},{7,22},{8,25},{9,... | collective-permute-start | bytes 49160 | tf_op jit(solution)/shard_map/ppermute | solution.py:25
  6.2 4.1 %collective-permute-start.3 = (bf16[32,256]{1,0:T(8,128)(2,1)S(1)}, bf16[32,256]{1,0:T(8,128)(2,1)S(1)}, u32[]{:S(2)}, u32[]{:S(2)}) collective-permute-start(bf16[32,256]{1,0:T(8,128)(2,1)S(1)} %constant_dynamic-update-slice_fusion), channel_id=1, source_target_pairs={{0,9},{1,8},{2,11},{3,10},{4,13},{5,12},{6,15},{7,14},{8,1},{9,0},... | collective-permute-start | bytes 49160 | tf_op jit(solution)/shard_map/ppermute | solution.py:25
  6.8 10.7 %copy-start.1 = (bf16[128,1024]{1,0:T(8,128)(2,1)S(1)}, bf16[128,1024]{1,0:T(8,128)(2,1)}, u32[]{:S(2)}) copy-start(bf16[128,1024]{1,0:T(8,128)(2,1)} %upstream_ref.1) | copy-start | bytes 786436
  7.8 9.7 %copy-start = (bf16[128,1024]{1,0:T(8,128)(2,1)S(1)}, bf16[128,1024]{1,0:T(8,128)(2,1)}, u32[]{:S(2)}) copy-start(bf16[128,1024]{1,0:T(8,128)(2,1)} %queries_ref.1) | copy-start | bytes 786436
  10.3 5.1 %collective-permute-start.4 = (bf16[128,256]{1,0:T(8,128)(2,1)S(1)}, bf16[128,256]{1,0:T(8,128)(2,1)S(1)}, u32[]{:S(2)}, u32[]{:S(2)}) collective-permute-start(bf16[128,256]{1,0:T(8,128)(2,1)S(1)} %constant_dynamic-update-slice_fusion.2), channel_id=1, source_target_pairs={{0,7},{1,6},{2,5},{3,4},{4,3},{5,2},{6,1},{7,0},{8,15},{9,14},{10,... | collective-permute-start | bytes 196616 | tf_op jit(solution)/shard_map/ppermute | solution.py:25
  12.9 4.2 %collective-permute-start.5 = (bf16[128,256]{1,0:T(8,128)(2,1)S(1)}, bf16[128,256]{1,0:T(8,128)(2,1)S(1)}, u32[]{:S(2)}, u32[]{:S(2)}) collective-permute-start(bf16[128,256]{1,0:T(8,128)(2,1)S(1)} %constant_dynamic-update-slice_fusion.2), channel_id=1, source_target_pairs={{0,5},{1,4},{2,7},{3,6},{4,1},{5,0},{6,3},{7,2},{8,13},{9,12},{10,... | collective-permute-start | bytes 196616 | tf_op jit(solution)/shard_map/ppermute | solution.py:25
  13.1 4.4 %collective-permute-start.6 = (bf16[128,256]{1,0:T(8,128)(2,1)S(1)}, bf16[128,256]{1,0:T(8,128)(2,1)S(1)}, u32[]{:S(2)}, u32[]{:S(2)}) collective-permute-start(bf16[128,256]{1,0:T(8,128)(2,1)S(1)} %constant_dynamic-update-slice_fusion.2), channel_id=1, source_target_pairs={{0,3},{1,2},{2,1},{3,0},{4,7},{5,6},{6,5},{7,4},{8,11},{9,10},{10,... | collective-permute-start | bytes 196616 | tf_op jit(solution)/shard_map/ppermute | solution.py:25
  13.6 3.8 %collective-permute-start.7 = (bf16[128,256]{1,0:T(8,128)(2,1)S(1)}, bf16[128,256]{1,0:T(8,128)(2,1)S(1)}, u32[]{:S(2)}, u32[]{:S(2)}) collective-permute-start(bf16[128,256]{1,0:T(8,128)(2,1)S(1)} %constant_dynamic-update-slice_fusion.2), channel_id=1, source_target_pairs={{0,1},{1,0},{2,3},{3,2},{4,5},{5,4},{6,7},{7,6},{8,9},{9,8},{10,11... | collective-permute-start | bytes 196616 | tf_op jit(solution)/shard_map/ppermute | solution.py:25
  13.8 12.5 %collective-permute-start.11 = (bf16[512,256]{1,0:T(8,128)(2,1)S(1)}, bf16[512,256]{1,0:T(8,128)(2,1)S(1)}, u32[]{:S(2)}, u32[]{:S(2)}) collective-permute-start(bf16[512,256]{1,0:T(8,128)(2,1)S(1)} %constant_dynamic-update-slice_fusion.6.refs_3_), channel_id=1, source_target_pairs={{0,2},{2,0},{4,6},{6,4},{8,10},{10,8},{12,14},{14,12},{16,18},{18,... | collective-permute-start | bytes 786440 | tf_op jit(solution)/shard_map/ppermute | solution.py:20
  15.4 10.8 %collective-permute-start.12 = (bf16[512,256]{1,0:T(8,128)(2,1)S(1)}, bf16[512,256]{1,0:T(8,128)(2,1)S(1)}, u32[]{:S(2)}, u32[]{:S(2)}) collective-permute-start(bf16[512,256]{1,0:T(8,128)(2,1)S(1)} %constant_dynamic-update-slice_fusion.6.refs_3_), channel_id=1, source_target_pairs={{0,4},{2,6},{4,0},{6,2},{8,12},{10,14},{12,8},{14,10},{16,20},{18,... | collective-permute-start | bytes 786440 | tf_op jit(solution)/shard_map/ppermute | solution.py:20
  19.7 5.5 %collective-permute-start.10 = (bf16[4,32,256]{2,1,0:T(8,128)(2,1)S(1)}, bf16[4,32,256]{2,1,0:T(8,128)(2,1)S(1)}, u32[]{:S(2)}, u32[]{:S(2)}) collective-permute-start(bf16[4,32,256]{2,1,0:T(8,128)(2,1)S(1)} %get-tuple-element.20), channel_id=1, source_target_pairs={{0,6},{2,4},{4,2},{6,0},{8,14},{10,12},{12,10},{14,8},{16,22},{18,... | collective-permute-start | bytes 196616 | tf_op jit(solution)/shard_map/ppermute | solution.py:20
  20.8 5.1 %collective-permute-start.8 = (bf16[4,32,256]{2,1,0:T(8,128)(2,1)S(1)}, bf16[4,32,256]{2,1,0:T(8,128)(2,1)S(1)}, u32[]{:S(2)}, u32[]{:S(2)}) collective-permute-start(bf16[4,32,256]{2,1,0:T(8,128)(2,1)S(1)} %get-tuple-element.18), channel_id=1, source_target_pairs={{0,2},{2,0},{4,6},{6,4},{8,10},{10,8},{12,14},{14,12},{16,18},{18,... | collective-permute-start | bytes 196616 | tf_op jit(solution)/shard_map/ppermute | solution.py:20
  22.2 4.0 %collective-permute-start.9 = (bf16[4,32,256]{2,1,0:T(8,128)(2,1)S(1)}, bf16[4,32,256]{2,1,0:T(8,128)(2,1)S(1)}, u32[]{:S(2)}, u32[]{:S(2)}) collective-permute-start(bf16[4,32,256]{2,1,0:T(8,128)(2,1)S(1)} %get-tuple-element.19), channel_id=1, source_target_pairs={{0,4},{2,6},{4,0},{6,2},{8,12},{10,14},{12,8},{14,10},{16,20},{18,... | collective-permute-start | bytes 196616 | tf_op jit(solution)/shard_map/ppermute | solution.py:20
  25.2 7.8 %collective-permute-start.16 = (bf16[512,256]{1,0:T(8,128)(2,1)S(1)}, bf16[512,256]{1,0:T(8,128)(2,1)S(1)}, u32[]{:S(2)}, u32[]{:S(2)}) collective-permute-start(bf16[512,256]{1,0:T(8,128)(2,1)S(1)} %constant_dynamic-update-slice_fusion.6.refs_3_), channel_id=1, source_target_pairs={{0,6},{2,4},{4,2},{6,0},{8,14},{10,12},{12,10},{14,8},{16,22},{18,... | collective-permute-start | bytes 786440 | tf_op jit(solution)/shard_map/ppermute | solution.py:20
  26.3 4.4 %collective-permute-start.13 = (bf16[4,32,256]{2,1,0:T(8,128)(2,1)S(1)}, bf16[4,32,256]{2,1,0:T(8,128)(2,1)S(1)}, u32[]{:S(2)}, u32[]{:S(2)}) collective-permute-start(bf16[4,32,256]{2,1,0:T(8,128)(2,1)S(1)} %get-tuple-element.34), channel_id=1, source_target_pairs={{0,16},{2,18},{4,20},{6,22},{8,24},{10,26},{12,28},{14,30},{16,0},... | collective-permute-start | bytes 196616 | tf_op jit(solution)/shard_map/ppermute | solution.py:20
  27.9 5.1 %collective-permute-start.14 = (bf16[4,32,256]{2,1,0:T(8,128)(2,1)S(1)}, bf16[4,32,256]{2,1,0:T(8,128)(2,1)S(1)}, u32[]{:S(2)}, u32[]{:S(2)}) collective-permute-start(bf16[4,32,256]{2,1,0:T(8,128)(2,1)S(1)} %get-tuple-element.34), channel_id=1, source_target_pairs={{0,24},{2,26},{4,28},{6,30},{8,16},{10,18},{12,20},{14,22},{16,8},... | collective-permute-start | bytes 196616 | tf_op jit(solution)/shard_map/ppermute | solution.py:20
  27.9 5.1 %collective-permute-start.15 = (bf16[4,32,256]{2,1,0:T(8,128)(2,1)S(1)}, bf16[4,32,256]{2,1,0:T(8,128)(2,1)S(1)}, u32[]{:S(2)}, u32[]{:S(2)}) collective-permute-start(bf16[4,32,256]{2,1,0:T(8,128)(2,1)S(1)} %get-tuple-element.34), channel_id=1, source_target_pairs={{0,8},{2,10},{4,12},{6,14},{8,0},{10,2},{12,4},{14,6},{16,24},{18,... | collective-permute-start | bytes 196616 | tf_op jit(solution)/shard_map/ppermute | solution.py:20
  33.5 3.5 %collective-permute-start.17 = (bf16[2,32,2048]{2,1,0:T(8,128)(2,1)S(1)}, bf16[2,32,2048]{2,1,0:T(8,128)(2,1)S(1)}, u32[]{:S(2)}, u32[]{:S(2)}) collective-permute-start(bf16[2,32,2048]{2,1,0:T(8,128)(2,1)S(1)} %get-tuple-element.33), channel_id=1, source_target_pairs={{0,1},{1,0},{2,3},{3,2},{4,5},{5,4},{6,7},{7,6},{8,9},{9,8},{10,11... | collective-permute-start | bytes 786440 | tf_op jit(solution)/shard_map/ppermute | solution.py:20
  37.0 8.2 %collective-permute-start.18 = (bf16[32,2048]{1,0:T(8,128)(2,1)S(1)}, bf16[32,2048]{1,0:T(8,128)(2,1)S(1)}, u32[]{:S(2)}, u32[]{:S(2)}) collective-permute-start(bf16[32,2048]{1,0:T(8,128)(2,1)S(1)} %get-tuple-element.39), channel_id=1, source_target_pairs={{0,8},{1,16},{2,10},{3,18},{4,12},{5,20},{6,14},{7,22},{8,0},{9,24... | collective-permute-start | bytes 393224 | tf_op jit(solution)/shard_map/ppermute | solution.py:259
  38.8 6.4 %collective-permute-start.19 = (bf16[32,2048]{1,0:T(8,128)(2,1)S(1)}, bf16[32,2048]{1,0:T(8,128)(2,1)S(1)}, u32[]{:S(2)}, u32[]{:S(2)}) collective-permute-start(bf16[32,2048]{1,0:T(8,128)(2,1)S(1)} %get-tuple-element.38), channel_id=1, source_target_pairs={{1,24},{0,2},{3,26},{2,0},{5,28},{4,6},{7,30},{6,4},{9,16},{8,10},... | collective-permute-start | bytes 393224 | tf_op jit(solution)/shard_map/ppermute | solution.py:258

commit v8 on v7

--- a/solution.py
+++ b/solution.py
@@ -229,7 +229,8 @@
     block = jnp.concatenate([arrived[d] for d in (0, cross, far, near)], axis=0)
     blocks = {d: swap(block, chips, d) for d in (3, 1, 2, 0)}
     weight = jnp.concatenate([key_weight, value_weight], axis=1)
-    weights = [weight] + [exchange(weight, "seq", chips, d) for d in (1, 2)]
+    weights = [exchange(weight, "seq", chips, d) for d in (2, 1)]
+    weights = [weight, weights[1], weights[0]]
     low, vision, terms = attention_terms(
         text_query, grad_output, [blocks[d] for d in reversed(range(plane))], line
     )

time: 46.2 us -> 46.2 us (level)
  no operation moved by 1% of the time
where the time goes in v8:
time: 46.2 us; the launch traced here: 46 us
  starting transfers between devices  22.6 us (49%)
  waiting for transfers between devices  16.1 us (35%)
  Pallas kernels  3.93 us (9%)
  local copies, waits for them, and re-layouts  1.76 us (4%)
  other arithmetic  0.83 us (2%)
  between operations  0.75 us (2%)
    ppermute x10, starting transfers between devices, exchange(): return lax.ppermute(block, axis, [(i, i ^ distance) for i in range(size)])  11.1 us
    ppermute x8, starting transfers between devices, swap(): return lax.ppermute(block, ('seq', 'kv'), routes)  8.84 us
    ppermute x10, waiting for transfers between devices, exchange(): return lax.ppermute(block, axis, [(i, i ^ distance) for i in range(size)])  7.05 us
    ppermute x1, waiting for transfers between devices, two_cores(): first = lax.ppermute(go, ('seq', 'kv'), routes_a)  5.45 us
    ppermute x8, waiting for transfers between devices, swap(): return lax.ppermute(block, ('seq', 'kv'), routes)  3.58 us
    pallas_call x1, Pallas kernels, attention_terms(): pl.pallas_call(functools.partial(attention_kernel, outer), out_shape=[jax...  2.26 us
    ppermute x1, starting transfers between devices, two_cores(): first = lax.ppermute(go, ('seq', 'kv'), routes_a)  1.79 us
    unnamed x13, local copies, waits for them, and re-layouts  1.7 us
  transfers between devices with their start and end apart: 20, of which 11 were waited for; matrix products, arithmetic and copies ran while one was open for 2% of the time, Pallas kernels for 8%

profile of v8, /device:TPU:1, one launch (start us, length us, event | category | flops | bytes accessed | tf_op | source)
XLA Modules:
  0.0 46.0 jit_solution(10741655264562134182)
XLA Ops:
  0.6 0.7 %constant_dynamic-update-slice_fusion.1 = bf16[32,256]{1,0:T(8,128)(2,1)S(1)} fusion(bf16[32,128]{1,0:T(8,128)(2,1)} %param.7), kind=kLoop, calls=%fused_computation.10 | loop fusion | bytes 16384
  1.5 4.7 %collective-permute-start.1 = (bf16[32,256]{1,0:T(8,128)(2,1)S(1)}, bf16[32,256]{1,0:T(8,128)(2,1)S(1)}, u32[]{:S(2)}, u32[]{:S(2)}) collective-permute-start(bf16[32,256]{1,0:T(8,128)(2,1)S(1)} %constant_dynamic-update-slice_fusion), channel_id=1, source_target_pairs={{0,25},{1,24},{2,27},{3,26},{4,29},{5,28},{6,31},{7,30},{8,17},{9,... | collective-permute-start | bytes 49160 | tf_op jit(solution)/shard_map/ppermute | solution.py:25
  6.2 0.6 %collective-permute-start.3 = (bf16[32,256]{1,0:T(8,128)(2,1)S(1)}, bf16[32,256]{1,0:T(8,128)(2,1)S(1)}, u32[]{:S(2)}, u32[]{:S(2)}) collective-permute-start(bf16[32,256]{1,0:T(8,128)(2,1)S(1)} %constant_dynamic-update-slice_fusion), channel_id=1, source_target_pairs={{0,9},{1,8},{2,11},{3,10},{4,13},{5,12},{6,15},{7,14},{8,1},{9,0},... | collective-permute-start | bytes 49160 | tf_op jit(solution)/shard_map/ppermute | solution.py:25
  6.8 1.0 %constant_dynamic-update-slice_fusion.7 = bf16[512,256]{1,0:T(8,128)(2,1)S(1)} fusion(bf16[512,128]{1,0:T(8,128)(2,1)} %param.10), kind=kLoop, calls=%fused_computation.16 | loop fusion | bytes 262144
  7.8 2.5 %collective-permute-done.2 = bf16[32,256]{1,0:T(8,128)(2,1)S(1)} collective-permute-done((bf16[32,256]{1,0:T(8,128)(2,1)S(1)}, bf16[32,256]{1,0:T(8,128)(2,1)S(1)}, u32[]{:S(2)}, u32[]{:S(2)}) %collective-permute-start.2) | collective-permute-done | bytes 16416 | tf_op jit(solution)/shard_map/ppermute | solution.py:25
  10.3 2.5 %collective-permute-start.4 = (bf16[128,256]{1,0:T(8,128)(2,1)S(1)}, bf16[128,256]{1,0:T(8,128)(2,1)S(1)}, u32[]{:S(2)}, u32[]{:S(2)}) collective-permute-start(bf16[128,256]{1,0:T(8,128)(2,1)S(1)} %constant_dynamic-update-slice_fusion.2), channel_id=1, source_target_pairs={{0,7},{1,6},{2,5},{3,4},{4,3},{5,2},{6,1},{7,0},{8,15},{9,14},{10,... | collective-permute-start | bytes 196616 | tf_op jit(solution)/shard_map/ppermute | solution.py:25
  13.8 1.3 %collective-permute-start.11 = (bf16[512,256]{1,0:T(8,128)(2,1)S(1)}, bf16[512,256]{1,0:T(8,128)(2,1)S(1)}, u32[]{:S(2)}, u32[]{:S(2)}) collective-permute-start(bf16[512,256]{1,0:T(8,128)(2,1)S(1)} %constant_dynamic-update-slice_fusion.6.refs_3_), channel_id=1, source_target_pairs={{0,2},{2,0},{4,6},{6,4},{8,10},{10,8},{12,14},{14,12},{16,18},{18,... | collective-permute-start | bytes 786440 | tf_op jit(solution)/shard_map/ppermute | solution.py:20
  15.4 1.3 %collective-permute-start.12 = (bf16[512,256]{1,0:T(8,128)(2,1)S(1)}, bf16[512,256]{1,0:T(8,128)(2,1)S(1)}, u32[]{:S(2)}, u32[]{:S(2)}) collective-permute-start(bf16[512,256]{1,0:T(8,128)(2,1)S(1)} %constant_dynamic-update-slice_fusion.6.refs_3_), channel_id=1, source_target_pairs={{0,4},{2,6},{4,0},{6,2},{8,12},{10,14},{12,8},{14,10},{16,20},{18,... | collective-permute-start | bytes 786440 | tf_op jit(solution)/shard_map/ppermute | solution.py:20
  17.5 2.3 %attention_terms.1 = (bf16[512,1024]{1,0:T(8,128)(2,1)S(1)}, bf16[512,256]{1,0:T(8,128)(2,1)S(1)}, f32[4,32,256]{2,1,0:T(8,128)S(1)}, bf16[4,32,256]{2,1,0:T(8,1...) custom-call(bf16[128,1024]{1,0:T(8,128)(2,1)S(1)} %copy-done, ...), custom_call_target="tpu_custom_call" | custom-call | flops 2684354560 | bytes 786432 | tf_op jit(solution)/shard_map/attention_terms/pallas_call | solution.py:70
  19.7 1.1 %collective-permute-start.10 = (bf16[4,32,256]{2,1,0:T(8,128)(2,1)S(1)}, bf16[4,32,256]{2,1,0:T(8,128)(2,1)S(1)}, u32[]{:S(2)}, u32[]{:S(2)}) collective-permute-start(bf16[4,32,256]{2,1,0:T(8,128)(2,1)S(1)} %get-tuple-element.20), channel_id=1, source_target_pairs={{0,6},{2,4},{4,2},{6,0},{8,14},{10,12},{12,10},{14,8},{16,22},{18,... | collective-permute-start | bytes 196616 | tf_op jit(solution)/shard_map/ppermute | solution.py:20
  20.8 1.4 %collective-permute-start.8 = (bf16[4,32,256]{2,1,0:T(8,128)(2,1)S(1)}, bf16[4,32,256]{2,1,0:T(8,128)(2,1)S(1)}, u32[]{:S(2)}, u32[]{:S(2)}) collective-permute-start(bf16[4,32,256]{2,1,0:T(8,128)(2,1)S(1)} %get-tuple-element.18), channel_id=1, source_target_pairs={{0,2},{2,0},{4,6},{6,4},{8,10},{10,8},{12,14},{14,12},{16,18},{18,... | collective-permute-start | bytes 196616 | tf_op jit(solution)/shard_map/ppermute | solution.py:20
  22.5 1.2 %query_gradient.1 = bf16[128,1024]{1,0:T(8,128)(2,1)} custom-call(bf16[512,1024]{1,0:T(8,128)(2,1)S(1)} %get-tuple-element.21.low_ref, bf16[512,256]{1,0:T(8,128)(2,1)S(1)} %get-tuple-element.22.vision_ref), custom_call_target="tpu_custom_call" | custom-call | flops 134217728 | bytes 262144 | tf_op jit(solution)/shard_map/query_gradient/pallas_call | solution.py:108
  23.7 1.6 %collective-permute-done.10 = bf16[4,32,256]{2,1,0:T(8,128)(2,1)S(1)} collective-permute-done((bf16[4,32,256]{2,1,0:T(8,128)(2,1)S(1)}, bf16[4,32,256]{2,1,0:T(8,128)(2,1)S(1)}, u32[]{:S(2)}, u32[]{:S(2)}) %collective-permute-start.10) | collective-permute-done | bytes 65568 | tf_op jit(solution)/shard_map/ppermute | solution.py:20
  25.2 0.7 %collective-permute-start.16 = (bf16[512,256]{1,0:T(8,128)(2,1)S(1)}, bf16[512,256]{1,0:T(8,128)(2,1)S(1)}, u32[]{:S(2)}, u32[]{:S(2)}) collective-permute-start(bf16[512,256]{1,0:T(8,128)(2,1)S(1)} %constant_dynamic-update-slice_fusion.6.refs_3_), channel_id=1, source_target_pairs={{0,6},{2,4},{4,2},{6,0},{8,14},{10,12},{12,10},{14,8},{16,22},{18,... | collective-permute-start | bytes 786440 | tf_op jit(solution)/shard_map/ppermute | solution.py:20
  26.3 1.6 %collective-permute-start.13 = (bf16[4,32,256]{2,1,0:T(8,128)(2,1)S(1)}, bf16[4,32,256]{2,1,0:T(8,128)(2,1)S(1)}, u32[]{:S(2)}, u32[]{:S(2)}) collective-permute-start(bf16[4,32,256]{2,1,0:T(8,128)(2,1)S(1)} %get-tuple-element.34), channel_id=1, source_target_pairs={{0,16},{2,18},{4,20},{6,22},{8,24},{10,26},{12,28},{14,30},{16,0},... | collective-permute-start | bytes 196616 | tf_op jit(solution)/shard_map/ppermute | solution.py:20
  27.9 1.1 %collective-permute-start.15 = (bf16[4,32,256]{2,1,0:T(8,128)(2,1)S(1)}, bf16[4,32,256]{2,1,0:T(8,128)(2,1)S(1)}, u32[]{:S(2)}, u32[]{:S(2)}) collective-permute-start(bf16[4,32,256]{2,1,0:T(8,128)(2,1)S(1)} %get-tuple-element.34), channel_id=1, source_target_pairs={{0,8},{2,10},{4,12},{6,14},{8,0},{10,2},{12,4},{14,6},{16,24},{18,... | collective-permute-start | bytes 196616 | tf_op jit(solution)/shard_map/ppermute | solution.py:20
  29.0 1.7 %collective-permute-done.13.refs_0_ = bf16[4,32,256]{2,1,0:T(8,128)(2,1)S(1)} collective-permute-done((bf16[4,32,256]{2,1,0:T(8,128)(2,1)S(1)}, bf16[4,32,256]{2,1,0:T(8,128)(2,1)S(1)}, u32[]{:S(2)}, u32[]{:S(2)}) %collective-permute-start.13) | collective-permute-done | bytes 65568 | tf_op jit(solution)/shard_map/ppermute | solution.py:20
  30.6 2.3 %collective-permute-done.14.refs_1_ = bf16[4,32,256]{2,1,0:T(8,128)(2,1)S(1)} collective-permute-done((bf16[4,32,256]{2,1,0:T(8,128)(2,1)S(1)}, bf16[4,32,256]{2,1,0:T(8,128)(2,1)S(1)}, u32[]{:S(2)}, u32[]{:S(2)}) %collective-permute-start.14) | collective-permute-done | bytes 65568 | tf_op jit(solution)/shard_map/ppermute | solution.py:20
  33.5 2.3 %collective-permute-start.17 = (bf16[2,32,2048]{2,1,0:T(8,128)(2,1)S(1)}, bf16[2,32,2048]{2,1,0:T(8,128)(2,1)S(1)}, u32[]{:S(2)}, u32[]{:S(2)}) collective-permute-start(bf16[2,32,2048]{2,1,0:T(8,128)(2,1)S(1)} %get-tuple-element.33), channel_id=1, source_target_pairs={{0,1},{1,0},{2,3},{3,2},{4,5},{5,4},{6,7},{7,6},{8,9},{9,8},{10,11... | collective-permute-start | bytes 786440 | tf_op jit(solution)/shard_map/ppermute | solution.py:20
  35.8 1.2 %collective-permute-done.17 = bf16[2,32,2048]{2,1,0:T(8,128)(2,1)S(1)} collective-permute-done((bf16[2,32,2048]{2,1,0:T(8,128)(2,1)S(1)}, bf16[2,32,2048]{2,1,0:T(8,128)(2,1)S(1)}, u32[]{:S(2)}, u32[]{:S(2)}) %collective-permute-start.17) | collective-permute-done | bytes 262176 | tf_op jit(solution)/shard_map/ppermute | solution.py:20
  37.0 1.8 %collective-permute-start.18 = (bf16[32,2048]{1,0:T(8,128)(2,1)S(1)}, bf16[32,2048]{1,0:T(8,128)(2,1)S(1)}, u32[]{:S(2)}, u32[]{:S(2)}) collective-permute-start(bf16[32,2048]{1,0:T(8,128)(2,1)S(1)} %get-tuple-element.39), channel_id=1, source_target_pairs={{0,8},{1,16},{2,10},{3,18},{4,12},{5,20},{6,14},{7,22},{8,0},{9,24... | collective-permute-start | bytes 393224 | tf_op jit(solution)/shard_map/ppermute | solution.py:260
  38.8 0.9 %collective-permute-start.19 = (bf16[32,2048]{1,0:T(8,128)(2,1)S(1)}, bf16[32,2048]{1,0:T(8,128)(2,1)S(1)}, u32[]{:S(2)}, u32[]{:S(2)}) collective-permute-start(bf16[32,2048]{1,0:T(8,128)(2,1)S(1)} %get-tuple-element.38), channel_id=1, source_target_pairs={{1,24},{0,2},{3,26},{2,0},{5,28},{4,6},{7,30},{6,4},{9,16},{8,10},... | collective-permute-start | bytes 393224 | tf_op jit(solution)/shard_map/ppermute | solution.py:259
  39.8 5.5 %collective-permute-done.18 = bf16[32,2048]{1,0:T(8,128)(2,1)S(1)} collective-permute-done((bf16[32,2048]{1,0:T(8,128)(2,1)S(1)}, bf16[32,2048]{1,0:T(8,128)(2,1)S(1)}, u32[]{:S(2)}, u32[]{:S(2)}) %collective-permute-start.18) | collective-permute-done | bytes 131104 | tf_op jit(solution)/shard_map/ppermute | solution.py:260
  45.2 0.7 %pad_maximum_fusion = bf16[32,4096]{1,0:T(8,128)(2,1)} fusion(bf16[32,2048]{1,0:T(8,128)(2,1)S(1)} %get-tuple-element.37, bf16[32,2048]{1,0:T(8,128)(2,1)S(1)} %get-tuple-element.36), kind=kLoop, calls=%fused_computation.1 | loop fusion | flops 524288 | bytes 524288 | tf_op jit(solution)/shard_map/concatenate | solution.py:264
  (40 shorter events, 3.4 us)
Async XLA Ops:
  0.6 0.7 %copy-start.3 = (bf16[32,128]{1,0:T(8,128)(2,1)S(1)}, bf16[32,128]{1,0:T(8,128)(2,1)}, u32[]{:S(2)}) copy-start(bf16[32,128]{1,0:T(8,128)(2,1)} %param.8) | copy-start | bytes 24580
  1.3 12.4 %copy-start.2 = (bf16[512,128]{1,0:T(8,128)(2,1)S(1)}, bf16[512,128]{1,0:T(8,128)(2,1)}, u32[]{:S(2)}) copy-start(bf16[512,128]{1,0:T(8,128)(2,1)} %param.11) | copy-start | bytes 393220
  1.4 6.4 %collective-permute-start = (bf16[32,256]{1,0:T(8,128)(2,1)S(1)}, bf16[32,256]{1,0:T(8,128)(2,1)S(1)}, u32[]{:S(2)}, u32[]{:S(2)}) collective-permute-start(bf16[32,256]{1,0:T(8,128)(2,1)S(1)} %constant_dynamic-update-slice_fusion), channel_id=1, source_target_pairs={{0,1},{1,0},{2,3},{3,2},{4,5},{5,4},{6,7},{7,6},{8,9},{9,8},{10,11... | collective-permute-start | bytes 49160 | tf_op jit(solution)/shard_map/ppermute | solution.py:25
  1.5 6.3 %collective-permute-start.1 = (bf16[32,256]{1,0:T(8,128)(2,1)S(1)}, bf16[32,256]{1,0:T(8,128)(2,1)S(1)}, u32[]{:S(2)}, u32[]{:S(2)}) collective-permute-start(bf16[32,256]{1,0:T(8,128)(2,1)S(1)} %constant_dynamic-update-slice_fusion), channel_id=1, source_target_pairs={{0,25},{1,24},{2,27},{3,26},{4,29},{5,28},{6,31},{7,30},{8,17},{9,... | collective-permute-start | bytes 49160 | tf_op jit(solution)/shard_map/ppermute | solution.py:25
  6.2 4.1 %collective-permute-start.2 = (bf16[32,256]{1,0:T(8,128)(2,1)S(1)}, bf16[32,256]{1,0:T(8,128)(2,1)S(1)}, u32[]{:S(2)}, u32[]{:S(2)}) collective-permute-start(bf16[32,256]{1,0:T(8,128)(2,1)S(1)} %constant_dynamic-update-slice_fusion), channel_id=1, source_target_pairs={{0,17},{1,16},{2,19},{3,18},{4,21},{5,20},{6,23},{7,22},{8,25},{9,... | collective-permute-start | bytes 49160 | tf_op jit(solution)/shard_map/ppermute | solution.py:25
  6.2 4.1 %collective-permute-start.3 = (bf16[32,256]{1,0:T(8,128)(2,1)S(1)}, bf16[32,256]{1,0:T(8,128)(2,1)S(1)}, u32[]{:S(2)}, u32[]{:S(2)}) collective-permute-start(bf16[32,256]{1,0:T(8,128)(2,1)S(1)} %constant_dynamic-update-slice_fusion), channel_id=1, source_target_pairs={{0,9},{1,8},{2,11},{3,10},{4,13},{5,12},{6,15},{7,14},{8,1},{9,0},... | collective-permute-start | bytes 49160 | tf_op jit(solution)/shard_map/ppermute | solution.py:25
  6.8 10.7 %copy-start.1 = (bf16[128,1024]{1,0:T(8,128)(2,1)S(1)}, bf16[128,1024]{1,0:T(8,128)(2,1)}, u32[]{:S(2)}) copy-start(bf16[128,1024]{1,0:T(8,128)(2,1)} %upstream_ref.1) | copy-start | bytes 786436
  7.8 9.7 %copy-start = (bf16[128,1024]{1,0:T(8,128)(2,1)S(1)}, bf16[128,1024]{1,0:T(8,128)(2,1)}, u32[]{:S(2)}) copy-start(bf16[128,1024]{1,0:T(8,128)(2,1)} %queries_ref.1) | copy-start | bytes 786436
  10.3 5.1 %collective-permute-start.4 = (bf16[128,256]{1,0:T(8,128)(2,1)S(1)}, bf16[128,256]{1,0:T(8,128)(2,1)S(1)}, u32[]{:S(2)}, u32[]{:S(2)}) collective-permute-start(bf16[128,256]{1,0:T(8,128)(2,1)S(1)} %constant_dynamic-update-slice_fusion.2), channel_id=1, source_target_pairs={{0,7},{1,6},{2,5},{3,4},{4,3},{5,2},{6,1},{7,0},{8,15},{9,14},{10,... | collective-permute-start | bytes 196616 | tf_op jit(solution)/shard_map/ppermute | solution.py:25
  12.9 4.2 %collective-permute-start.5 = (bf16[128,256]{1,0:T(8,128)(2,1)S(1)}, bf16[128,256]{1,0:T(8,128)(2,1)S(1)}, u32[]{:S(2)}, u32[]{:S(2)}) collective-permute-start(bf16[128,256]{1,0:T(8,128)(2,1)S(1)} %constant_dynamic-update-slice_fusion.2), channel_id=1, source_target_pairs={{0,5},{1,4},{2,7},{3,6},{4,1},{5,0},{6,3},{7,2},{8,13},{9,12},{10,... | collective-permute-start | bytes 196616 | tf_op jit(solution)/shard_map/ppermute | solution.py:25
  13.1 4.4 %collective-permute-start.6 = (bf16[128,256]{1,0:T(8,128)(2,1)S(1)}, bf16[128,256]{1,0:T(8,128)(2,1)S(1)}, u32[]{:S(2)}, u32[]{:S(2)}) collective-permute-start(bf16[128,256]{1,0:T(8,128)(2,1)S(1)} %constant_dynamic-update-slice_fusion.2), channel_id=1, source_target_pairs={{0,3},{1,2},{2,1},{3,0},{4,7},{5,6},{6,5},{7,4},{8,11},{9,10},{10,... | collective-permute-start | bytes 196616 | tf_op jit(solution)/shard_map/ppermute | solution.py:25
  13.6 3.8 %collective-permute-start.7 = (bf16[128,256]{1,0:T(8,128)(2,1)S(1)}, bf16[128,256]{1,0:T(8,128)(2,1)S(1)}, u32[]{:S(2)}, u32[]{:S(2)}) collective-permute-start(bf16[128,256]{1,0:T(8,128)(2,1)S(1)} %constant_dynamic-update-slice_fusion.2), channel_id=1, source_target_pairs={{0,1},{1,0},{2,3},{3,2},{4,5},{5,4},{6,7},{7,6},{8,9},{9,8},{10,11... | collective-permute-start | bytes 196616 | tf_op jit(solution)/shard_map/ppermute | solution.py:25
  13.8 12.5 %collective-permute-start.11 = (bf16[512,256]{1,0:T(8,128)(2,1)S(1)}, bf16[512,256]{1,0:T(8,128)(2,1)S(1)}, u32[]{:S(2)}, u32[]{:S(2)}) collective-permute-start(bf16[512,256]{1,0:T(8,128)(2,1)S(1)} %constant_dynamic-update-slice_fusion.6.refs_3_), channel_id=1, source_target_pairs={{0,2},{2,0},{4,6},{6,4},{8,10},{10,8},{12,14},{14,12},{16,18},{18,... | collective-permute-start | bytes 786440 | tf_op jit(solution)/shard_map/ppermute | solution.py:20
  15.4 10.8 %collective-permute-start.12 = (bf16[512,256]{1,0:T(8,128)(2,1)S(1)}, bf16[512,256]{1,0:T(8,128)(2,1)S(1)}, u32[]{:S(2)}, u32[]{:S(2)}) collective-permute-start(bf16[512,256]{1,0:T(8,128)(2,1)S(1)} %constant_dynamic-update-slice_fusion.6.refs_3_), channel_id=1, source_target_pairs={{0,4},{2,6},{4,0},{6,2},{8,12},{10,14},{12,8},{14,10},{16,20},{18,... | collective-permute-start | bytes 786440 | tf_op jit(solution)/shard_map/ppermute | solution.py:20
  19.7 5.5 %collective-permute-start.10 = (bf16[4,32,256]{2,1,0:T(8,128)(2,1)S(1)}, bf16[4,32,256]{2,1,0:T(8,128)(2,1)S(1)}, u32[]{:S(2)}, u32[]{:S(2)}) collective-permute-start(bf16[4,32,256]{2,1,0:T(8,128)(2,1)S(1)} %get-tuple-element.20), channel_id=1, source_target_pairs={{0,6},{2,4},{4,2},{6,0},{8,14},{10,12},{12,10},{14,8},{16,22},{18,... | collective-permute-start | bytes 196616 | tf_op jit(solution)/shard_map/ppermute | solution.py:20
  20.8 5.1 %collective-permute-start.8 = (bf16[4,32,256]{2,1,0:T(8,128)(2,1)S(1)}, bf16[4,32,256]{2,1,0:T(8,128)(2,1)S(1)}, u32[]{:S(2)}, u32[]{:S(2)}) collective-permute-start(bf16[4,32,256]{2,1,0:T(8,128)(2,1)S(1)} %get-tuple-element.18), channel_id=1, source_target_pairs={{0,2},{2,0},{4,6},{6,4},{8,10},{10,8},{12,14},{14,12},{16,18},{18,... | collective-permute-start | bytes 196616 | tf_op jit(solution)/shard_map/ppermute | solution.py:20
  22.2 4.0 %collective-permute-start.9 = (bf16[4,32,256]{2,1,0:T(8,128)(2,1)S(1)}, bf16[4,32,256]{2,1,0:T(8,128)(2,1)S(1)}, u32[]{:S(2)}, u32[]{:S(2)}) collective-permute-start(bf16[4,32,256]{2,1,0:T(8,128)(2,1)S(1)} %get-tuple-element.19), channel_id=1, source_target_pairs={{0,4},{2,6},{4,0},{6,2},{8,12},{10,14},{12,8},{14,10},{16,20},{18,... | collective-permute-start | bytes 196616 | tf_op jit(solution)/shard_map/ppermute | solution.py:20
  25.2 7.8 %collective-permute-start.16 = (bf16[512,256]{1,0:T(8,128)(2,1)S(1)}, bf16[512,256]{1,0:T(8,128)(2,1)S(1)}, u32[]{:S(2)}, u32[]{:S(2)}) collective-permute-start(bf16[512,256]{1,0:T(8,128)(2,1)S(1)} %constant_dynamic-update-slice_fusion.6.refs_3_), channel_id=1, source_target_pairs={{0,6},{2,4},{4,2},{6,0},{8,14},{10,12},{12,10},{14,8},{16,22},{18,... | collective-permute-start | bytes 786440 | tf_op jit(solution)/shard_map/ppermute | solution.py:20
  26.3 4.4 %collective-permute-start.13 = (bf16[4,32,256]{2,1,0:T(8,128)(2,1)S(1)}, bf16[4,32,256]{2,1,0:T(8,128)(2,1)S(1)}, u32[]{:S(2)}, u32[]{:S(2)}) collective-permute-start(bf16[4,32,256]{2,1,0:T(8,128)(2,1)S(1)} %get-tuple-element.34), channel_id=1, source_target_pairs={{0,16},{2,18},{4,20},{6,22},{8,24},{10,26},{12,28},{14,30},{16,0},... | collective-permute-start | bytes 196616 | tf_op jit(solution)/shard_map/ppermute | solution.py:20
  27.9 5.1 %collective-permute-start.14 = (bf16[4,32,256]{2,1,0:T(8,128)(2,1)S(1)}, bf16[4,32,256]{2,1,0:T(8,128)(2,1)S(1)}, u32[]{:S(2)}, u32[]{:S(2)}) collective-permute-start(bf16[4,32,256]{2,1,0:T(8,128)(2,1)S(1)} %get-tuple-element.34), channel_id=1, source_target_pairs={{0,24},{2,26},{4,28},{6,30},{8,16},{10,18},{12,20},{14,22},{16,8},... | collective-permute-start | bytes 196616 | tf_op jit(solution)/shard_map/ppermute | solution.py:20
  27.9 5.1 %collective-permute-start.15 = (bf16[4,32,256]{2,1,0:T(8,128)(2,1)S(1)}, bf16[4,32,256]{2,1,0:T(8,128)(2,1)S(1)}, u32[]{:S(2)}, u32[]{:S(2)}) collective-permute-start(bf16[4,32,256]{2,1,0:T(8,128)(2,1)S(1)} %get-tuple-element.34), channel_id=1, source_target_pairs={{0,8},{2,10},{4,12},{6,14},{8,0},{10,2},{12,4},{14,6},{16,24},{18,... | collective-permute-start | bytes 196616 | tf_op jit(solution)/shard_map/ppermute | solution.py:20
  33.5 3.5 %collective-permute-start.17 = (bf16[2,32,2048]{2,1,0:T(8,128)(2,1)S(1)}, bf16[2,32,2048]{2,1,0:T(8,128)(2,1)S(1)}, u32[]{:S(2)}, u32[]{:S(2)}) collective-permute-start(bf16[2,32,2048]{2,1,0:T(8,128)(2,1)S(1)} %get-tuple-element.33), channel_id=1, source_target_pairs={{0,1},{1,0},{2,3},{3,2},{4,5},{5,4},{6,7},{7,6},{8,9},{9,8},{10,11... | collective-permute-start | bytes 786440 | tf_op jit(solution)/shard_map/ppermute | solution.py:20
  37.0 8.2 %collective-permute-start.18 = (bf16[32,2048]{1,0:T(8,128)(2,1)S(1)}, bf16[32,2048]{1,0:T(8,128)(2,1)S(1)}, u32[]{:S(2)}, u32[]{:S(2)}) collective-permute-start(bf16[32,2048]{1,0:T(8,128)(2,1)S(1)} %get-tuple-element.39), channel_id=1, source_target_pairs={{0,8},{1,16},{2,10},{3,18},{4,12},{5,20},{6,14},{7,22},{8,0},{9,24... | collective-permute-start | bytes 393224 | tf_op jit(solution)/shard_map/ppermute | solution.py:260
  38.8 6.4 %collective-permute-start.19 = (bf16[32,2048]{1,0:T(8,128)(2,1)S(1)}, bf16[32,2048]{1,0:T(8,128)(2,1)S(1)}, u32[]{:S(2)}, u32[]{:S(2)}) collective-permute-start(bf16[32,2048]{1,0:T(8,128)(2,1)S(1)} %get-tuple-element.38), channel_id=1, source_target_pairs={{1,24},{0,2},{3,26},{2,0},{5,28},{4,6},{7,30},{6,4},{9,16},{8,10},... | collective-permute-start | bytes 393224 | tf_op jit(solution)/shard_map/ppermute | solution.py:259
